TPU v7x, 32 devices: a whole 2x2x4 slice. The times are simulated.
32 devices in a mesh: dp: 4 (over x, core), fsdp: 8 (over z, y).
Axes of the slice: x: 2, y: 2, z: 4, core: 2. Of those that a mesh axis runs over, the one named last changes fastest.
Arguments:
- inputs: bfloat16 [2, 4, 512, 2048], P(None, 'dp', 'fsdp'), may hold values from -6 to 6
- cotangent: bfloat16 [2, 4, 512, 2048], P(None, 'dp', 'fsdp'), may hold values from -6 to 6
- norm_gain: bfloat16 [2048], P(('dp', 'fsdp')), may hold values from 0.5 to 1.5
- mixer_gain: bfloat16 [2048], P(('dp', 'fsdp')), may hold values from 0.5 to 1.5
- ffn_gain: bfloat16 [2048], P(('dp', 'fsdp')), may hold values from 0.5 to 1.5
- slack: bfloat16 [2048], P(('dp', 'fsdp')), may hold values from 2.99e-05 to 0.0601
- w_query: bfloat16 [2048, 2048], P(('dp', 'fsdp')), may hold values from -0.125 to 0.125
- w_forget: bfloat16 [2048, 2048], P(('dp', 'fsdp')), may hold values from -0.125 to 0.125
- w_input: bfloat16 [2048, 2048], P(('dp', 'fsdp')), may hold values from -0.125 to 0.125
- w_gate_out: bfloat16 [2048, 2048], P(('dp', 'fsdp')), may hold values from -0.125 to 0.125
- w_out: bfloat16 [2048, 2048], P(('dp', 'fsdp')), may hold values from -0.125 to 0.125
- w_gate: bfloat16 [2048, 5632], P(('dp', 'fsdp')), may hold values from -0.125 to 0.125
- w_up: bfloat16 [2048, 5632], P(('dp', 'fsdp')), may hold values from -0.125 to 0.125
- w_down: bfloat16 [5632, 2048], P(('dp', 'fsdp')), may hold values from -0.15625 to 0.15625
Outputs:
- output: float32 [2, 4, 512, 2048], P(None, 'dp', 'fsdp')
- input_grad: float32 [2, 4, 512, 2048], P(None, 'dp', 'fsdp')
- grad_norm_gain: float32 [2048], P(('dp', 'fsdp'))
- grad_mixer_gain: float32 [2048], P(('dp', 'fsdp'))
- grad_ffn_gain: float32 [2048], P(('dp', 'fsdp'))
- grad_slack: float32 [2048], P(('dp', 'fsdp'))
- grad_query: float32 [2048, 2048], P(('dp', 'fsdp'))
- grad_forget: float32 [2048, 2048], P(('dp', 'fsdp'))
- grad_input: float32 [2048, 2048], P(('dp', 'fsdp'))
- grad_gate_out: float32 [2048, 2048], P(('dp', 'fsdp'))
- grad_out: float32 [2048, 2048], P(('dp', 'fsdp'))
- grad_gate: float32 [2048, 5632], P(('dp', 'fsdp'))
- grad_up: float32 [2048, 5632], P(('dp', 'fsdp'))
- grad_down: float32 [5632, 2048], P(('dp', 'fsdp'))
All inputs are finite; a program needn't handle non-finite values.
Results may differ from a plain program's by a relative error of at most 0.014.
Values may be sent and summed in bfloat16 or wider, within the bound.
No kernel may reach another device: no remote copies, remote signals or barrier semaphores. Data moves between devices by JAX's collectives and lax.ppermute only.
A program may use at most 512 MiB of HBM per device.

v0:
```python
import jax
import jax.numpy as jnp
from jax import lax
from jax.sharding import PartitionSpec as P

HEADS = 16
HEAD = 128
SPAN = 16


def carried_in(part, axis, combine, identity):
    place = lax.axis_index(axis)
    gathered = jax.tree.map(lambda a: lax.all_gather(a, axis), part)
    state = jax.tree.map(lambda a, e: jnp.zeros_like(a) + jnp.asarray(e, a.dtype), part, identity)

    def one(step, state):
        return combine(
            state, jax.tree.map(lambda a: lax.dynamic_index_in_dim(a, step, 0, False), gathered)
        )

    return lax.fori_loop(0, place, one, state)


def entering(value, axis, combine, identity):
    count, index = (lax.axis_size(axis), lax.axis_index(axis))
    everything = jax.tree.map(
        lambda part, kind: lax.all_gather(part.astype(kind), axis),
        value,
        jax.tree.map(lambda a: jnp.bfloat16 if a.dtype == jnp.float32 else a.dtype, value),
    )
    start = jax.tree.map(
        lambda part, zero: jnp.broadcast_to(jnp.asarray(zero, part.dtype), part.shape),
        value,
        identity,
    )

    def step(k, before):
        at = count - 1 - k
        reached = at > index
        new = combine(
            before, jax.tree.map(lambda part, own: part[at].astype(own.dtype), everything, value)
        )
        return jax.tree.map(lambda a, b: jnp.where(reached, a, b), new, before)

    return lax.fori_loop(0, count, step, start)


def precise_einsum(form, *operands):
    return jnp.einsum(form, *operands, precision=lax.Precision.HIGHEST)


def matmul(left_side, right_side):
    return jnp.dot(left_side, right_side, preferred_element_type=jnp.float32)


def outer_sum(left_side, right_side):
    return lax.dot_general(
        left_side, right_side, (((0,), (0,)), ((), ())), preferred_element_type=jnp.float32
    )


def back_product(left_side, right_side):
    return lax.dot_general(
        left_side, right_side, (((1,), (1,)), ((), ())), preferred_element_type=jnp.float32
    )


def rms_scale(values, gain):
    return values * lax.rsqrt(jnp.mean(values * values, axis=-1, keepdims=True) + 1e-06) * gain


def forget_terms(forget_proj, slack):
    incoming_keys = slack * (1.0 - jax.nn.sigmoid(forget_proj))
    return (incoming_keys, jnp.log1p(-incoming_keys))


def gated_group_norm(mixed_out, gate_out, mixer_gain):
    gated = mixed_out * jax.nn.silu(gate_out)
    grouped = gated.reshape(gated.shape[:-1] + (HEADS, HEAD))
    centred = grouped - jnp.mean(grouped, axis=-1, keepdims=True)
    scaled = centred * lax.rsqrt(jnp.mean(centred * centred, axis=-1, keepdims=True) + 1e-05)
    return scaled.reshape(gated.shape) * mixer_gain


def block_step(carried, pieces):
    recurrent_state, offset_log = carried
    query_rows, log_decay, incoming_keys, incoming_values = pieces
    cumulative_log = jnp.cumsum(log_decay, axis=0)
    positions = jnp.arange(query_rows.shape[0])
    causal = (positions[:, None] >= positions[None, :])[:, :, None, None]
    log_gap = cumulative_log[:, None] - cumulative_log[None, :]
    weight = jnp.where(causal, jnp.exp(jnp.where(causal, log_gap, 0.0)), 0.0)
    scores = precise_einsum("thk,shk,tshk->tsh", query_rows, incoming_keys, weight)
    inner_part = precise_einsum("tsh,shv->thv", scores, incoming_values)
    cross_block_part = precise_einsum(
        "jod,ode->joe", query_rows * jnp.exp(cumulative_log), recurrent_state
    )
    closing_log_decay = cumulative_log[-1]
    fresh_state = precise_einsum(
        "mcl,mcg->clg",
        incoming_keys * jnp.exp(closing_log_decay[None] - cumulative_log),
        incoming_values,
    )
    recurrent_state = jnp.exp(closing_log_decay)[..., None] * recurrent_state + fresh_state
    return (
        (recurrent_state, offset_log + closing_log_decay),
        (inner_part + cross_block_part, offset_log[None] + cumulative_log),
    )


def run_blocks(query_rows, log_decay, incoming_keys, incoming_values, recurrent_state):
    blocks = query_rows.shape[0] // SPAN

    def to_blocks(array):
        return array.reshape((blocks, SPAN) + array.shape[1:])

    start_log = jnp.zeros(log_decay.shape[1:], jnp.float32)
    (recurrent_state, _), (outputs, running) = lax.scan(
        block_step,
        (recurrent_state, start_log),
        (
            to_blocks(query_rows),
            to_blocks(log_decay),
            to_blocks(incoming_keys),
            to_blocks(incoming_values),
        ),
    )
    return (outputs.reshape(query_rows.shape), recurrent_state, running.reshape(log_decay.shape))


def full_run(query_rows, log_decay, incoming_keys, incoming_values, recurrent_state):
    outputs, memory_out, _ = run_blocks(
        query_rows, log_decay, incoming_keys, incoming_values, recurrent_state
    )
    return (outputs, memory_out)


def batched_run(query_rows, log_decay, incoming_keys, incoming_values, recurrent_state):
    return jax.vmap(full_run)(
        query_rows, log_decay, incoming_keys, incoming_values, recurrent_state
    )


def chain(earlier, later_part):
    return (earlier[0] * later_part[0], later_part[0][..., None] * earlier[1] + later_part[1])


def on_device(
    inputs,
    cotangent,
    norm_gain,
    mixer_gain,
    ffn_gain,
    slack,
    w_query,
    w_forget,
    w_input,
    w_gate_out,
    w_out,
    w_gate,
    w_up,
    w_down,
):
    micro_count = inputs.shape[0]
    tok_rows = inputs.shape[2]
    width = inputs.shape[3]
    all_rows = micro_count * tok_rows
    head_shape = (micro_count, tok_rows, HEADS, HEAD)
    identity = (
        jnp.ones((micro_count, HEADS, HEAD), jnp.float32),
        jnp.zeros((micro_count, HEADS, HEAD, HEAD), jnp.float32),
    )
    mixer_full = (
        lax.all_gather(norm_gain, ("dp", "fsdp"), axis=0, tiled=True),
        lax.all_gather(mixer_gain, ("dp", "fsdp"), axis=0, tiled=True),
        lax.all_gather(ffn_gain, ("dp", "fsdp"), axis=0, tiled=True),
        lax.all_gather(slack, ("dp", "fsdp"), axis=0, tiled=True),
        lax.all_gather(w_query, ("dp", "fsdp"), axis=0, tiled=True),
        lax.all_gather(w_forget, ("dp", "fsdp"), axis=0, tiled=True),
        lax.all_gather(w_input, ("dp", "fsdp"), axis=0, tiled=True),
        lax.all_gather(w_gate_out, ("dp", "fsdp"), axis=0, tiled=True),
        lax.all_gather(w_out, ("dp", "fsdp"), axis=0, tiled=True),
    )
    gain_first, gain_mixer, gain_ffn, slack_full = [
        gain.astype(jnp.float32) for gain in mixer_full[:4]
    ]
    full_query, full_forget, full_input, full_gate_out, full_out = mixer_full[4:]
    tokens = inputs[:, 0].astype(jnp.float32).reshape(all_rows, width)
    normed = rms_scale(tokens, gain_first).astype(jnp.bfloat16)
    query_rows = matmul(normed, full_query)
    forget_proj = matmul(normed, full_forget)
    incoming_values = matmul(normed, full_input)
    gate_out = matmul(normed, full_gate_out)
    incoming_keys, log_decay = forget_terms(forget_proj, slack_full)
    query_heads = query_rows.reshape(head_shape)
    decay_heads = log_decay.reshape(head_shape)
    key_heads = incoming_keys.reshape(head_shape)
    value_heads = incoming_values.reshape(head_shape)
    local_out, local_state, running = jax.vmap(run_blocks)(
        query_heads, decay_heads, key_heads, value_heads, identity[1]
    )
    decay_all = jnp.exp(running[:, -1])
    _, state_in = carried_in((decay_all, local_state), "fsdp", chain, identity)
    reach_weight = query_heads * jnp.exp(running)
    mixed_out = (local_out + precise_einsum("mthk,mhkv->mthv", reach_weight, state_in)).reshape(
        all_rows, width
    )
    unit_normed = gated_group_norm(mixed_out, gate_out, gain_mixer).astype(jnp.bfloat16)
    hidden = tokens + matmul(unit_normed, full_out)
    hidden_normed = rms_scale(hidden, gain_ffn).astype(jnp.bfloat16)
    mlp_full = (
        lax.all_gather(w_gate, ("dp", "fsdp"), axis=0, tiled=True),
        lax.all_gather(w_up, ("dp", "fsdp"), axis=0, tiled=True),
        lax.all_gather(w_down, ("dp", "fsdp"), axis=0, tiled=True),
    )
    gate_proj = matmul(hidden_normed, mlp_full[0])
    up_proj = matmul(hidden_normed, mlp_full[1])
    inner_part = (jax.nn.silu(gate_proj) * up_proj).astype(jnp.bfloat16)
    output = hidden + matmul(inner_part, mlp_full[2])
    d_output = cotangent[:, 0].astype(jnp.float32).reshape(all_rows, width)
    d_down = d_output.astype(jnp.bfloat16)
    d_inner = back_product(d_down, mlp_full[2])
    sigmoid_gate = jax.nn.sigmoid(gate_proj)
    d_gate = (d_inner * up_proj * sigmoid_gate * (1.0 + gate_proj * (1.0 - sigmoid_gate))).astype(
        jnp.bfloat16
    )
    d_up = (d_inner * gate_proj * sigmoid_gate).astype(jnp.bfloat16)
    d_hn = back_product(d_gate, mlp_full[0]) + back_product(d_up, mlp_full[1])
    term_gate = outer_sum(hidden_normed, d_gate)
    term_up = outer_sum(hidden_normed, d_up)
    term_down = outer_sum(inner_part, d_down)
    grad_gate, grad_up, grad_down = (
        lax.psum_scatter(term_gate, ("dp", "fsdp"), scatter_dimension=0, tiled=True),
        lax.psum_scatter(term_up, ("dp", "fsdp"), scatter_dimension=0, tiled=True),
        lax.psum_scatter(term_down, ("dp", "fsdp"), scatter_dimension=0, tiled=True),
    )
    _, pullback = jax.vjp(rms_scale, hidden, gain_ffn)
    d_hidden_norm, term_ffn_gain = pullback(d_hn)
    d_hidden = d_output + d_hidden_norm
    d_branch = d_hidden.astype(jnp.bfloat16)
    full_query, full_forget, full_input, full_gate_out, full_out = (
        lax.all_gather(w_query, ("dp", "fsdp"), axis=0, tiled=True),
        lax.all_gather(w_forget, ("dp", "fsdp"), axis=0, tiled=True),
        lax.all_gather(w_input, ("dp", "fsdp"), axis=0, tiled=True),
        lax.all_gather(w_gate_out, ("dp", "fsdp"), axis=0, tiled=True),
        lax.all_gather(w_out, ("dp", "fsdp"), axis=0, tiled=True),
    )
    term_out = outer_sum(unit_normed, d_branch)
    d_unit = back_product(d_branch, full_out)
    _, pullback = jax.vjp(gated_group_norm, mixed_out, gate_out, gain_mixer)
    d_mixed, d_gate_raw, term_mixer_gain = pullback(d_unit)
    d_gate_out = d_gate_raw.astype(jnp.bfloat16)
    d_mixed_heads = d_mixed.reshape(head_shape)
    leak_term = precise_einsum("mthk,mthv->mhkv", reach_weight, d_mixed_heads)
    _, state_grad = entering((decay_all, leak_term), "fsdp", chain, identity)
    _, pullback = jax.vjp(batched_run, query_heads, decay_heads, key_heads, value_heads, state_in)
    d_queries, d_log, d_keys, d_values, _ = pullback((d_mixed_heads, state_grad))
    _, pullback = jax.vjp(forget_terms, forget_proj, slack_full)
    d_forget, term_slack = pullback(
        (d_keys.reshape(all_rows, width), d_log.reshape(all_rows, width))
    )
    d_query_low = d_queries.reshape(all_rows, width).astype(jnp.bfloat16)
    d_forget_low = d_forget.astype(jnp.bfloat16)
    d_value_low = d_values.reshape(all_rows, width).astype(jnp.bfloat16)
    term_query = outer_sum(normed, d_query_low)
    term_forget = outer_sum(normed, d_forget_low)
    term_input = outer_sum(normed, d_value_low)
    term_gate_out = outer_sum(normed, d_gate_out)
    d_normed = (
        back_product(d_query_low, full_query)
        + back_product(d_forget_low, full_forget)
        + back_product(d_value_low, full_input)
        + back_product(d_gate_out, full_gate_out)
    )
    _, pullback = jax.vjp(rms_scale, tokens, gain_first)
    d_token_norm, term_norm_gain = pullback(d_normed)
    input_grad = d_hidden + d_token_norm
    mixer_sum = (
        lax.psum_scatter(term_norm_gain, ("dp", "fsdp"), scatter_dimension=0, tiled=True),
        lax.psum_scatter(term_mixer_gain, ("dp", "fsdp"), scatter_dimension=0, tiled=True),
        lax.psum_scatter(term_ffn_gain, ("dp", "fsdp"), scatter_dimension=0, tiled=True),
        lax.psum_scatter(term_slack, ("dp", "fsdp"), scatter_dimension=0, tiled=True),
        lax.psum_scatter(term_query, ("dp", "fsdp"), scatter_dimension=0, tiled=True),
        lax.psum_scatter(term_forget, ("dp", "fsdp"), scatter_dimension=0, tiled=True),
        lax.psum_scatter(term_input, ("dp", "fsdp"), scatter_dimension=0, tiled=True),
        lax.psum_scatter(term_gate_out, ("dp", "fsdp"), scatter_dimension=0, tiled=True),
        lax.psum_scatter(term_out, ("dp", "fsdp"), scatter_dimension=0, tiled=True),
    )
    output = output.reshape(micro_count, 1, tok_rows, width)
    input_grad = input_grad.reshape(micro_count, 1, tok_rows, width)
    return (
        output,
        input_grad,
        mixer_sum[0],
        mixer_sum[1],
        mixer_sum[2],
        mixer_sum[3],
        mixer_sum[4],
        mixer_sum[5],
        mixer_sum[6],
        mixer_sum[7],
        mixer_sum[8],
        grad_gate,
        grad_up,
        grad_down,
    )


def solution(mesh):
    in_specs = (
        P(None, "dp", "fsdp", None),
        P(None, "dp", "fsdp", None),
        P(("dp", "fsdp")),
        P(("dp", "fsdp")),
        P(("dp", "fsdp")),
        P(("dp", "fsdp")),
        P(("dp", "fsdp"), None),
        P(("dp", "fsdp"), None),
        P(("dp", "fsdp"), None),
        P(("dp", "fsdp"), None),
        P(("dp", "fsdp"), None),
        P(("dp", "fsdp"), None),
        P(("dp", "fsdp"), None),
        P(("dp", "fsdp"), None),
    )
    out_specs = (
        P(None, "dp", "fsdp", None),
        P(None, "dp", "fsdp", None),
        P(("dp", "fsdp")),
        P(("dp", "fsdp")),
        P(("dp", "fsdp")),
        P(("dp", "fsdp")),
        P(("dp", "fsdp"), None),
        P(("dp", "fsdp"), None),
        P(("dp", "fsdp"), None),
        P(("dp", "fsdp"), None),
        P(("dp", "fsdp"), None),
        P(("dp", "fsdp"), None),
        P(("dp", "fsdp"), None),
        P(("dp", "fsdp"), None),
    )
    return jax.shard_map(
        on_device, mesh=mesh, in_specs=in_specs, out_specs=out_specs, check_vma=False
    )
```

profile of v0, /device:TPU:2, one launch (start us, length us, event | category | flops | bytes accessed | tf_op | source)
XLA Modules:
  0.0 5995.0 jit_solution(6615835946494121550)
XLA Ops:
  13.4 41.8 all-reduce.10
  59.8 30.0 all-gather.15.cloned.1.call-done
  98.2 70.7 %all-gather.19.cloned.1.call-done = bf16[2048,2048]{1,0:T(8,128)(2,1)} async-done(((bf16[64,2048]{1,0:T(8,128)(2,1)}), bf16[2048,2048]{1,0:T(8,128)(2,1)}) %all-gather.19.cloned.1.call-update) | async-done | bytes 8388624 | tf_op jit(solution)/shard_map/all_gather | solution.py:178
  175.9 72.0 %all-gather.17.cloned.1.call-done = bf16[2048,2048]{1,0:T(8,128)(2,1)} async-done(((bf16[64,2048]{1,0:T(8,128)(2,1)}), bf16[2048,2048]{1,0:T(8,128)(2,1)}) %all-gather.17.cloned.1.call-update) | async-done | bytes 8388624 | tf_op jit(solution)/shard_map/all_gather | solution.py:180
  269.9 75.3 %while.109 = (s32[]{:T(128)}, f32[2,16,128,128]{3,2,1,0:T(8,128)S(1)}, f32[2,16,128]{2,1,0:T(8,128)S(1)}, f32[4,2,16,16,128]{4,2,3,1,0:T(8,128)}, f32[4,2,16,16,...) while((s32[]{:T(128)}, ...), condition=%wide.region_3.4_spmd.clone, body=%wide.region_1.3_spmd.clone.sunk | while | flops 223609088 | bytes 21987996 | solution.py:118
  352.6 31.6 all-gather
  391.2 182.8 %all-gather.31.cloned.1.call-done = f32[16,16,128,128]{3,2,1,0:T(8,128)} async-done(((f32[2,16,128,128]{3,2,1,0:T(8,128)}), f32[16,16,128,128]{3,2,1,0:T(8,128)}) %all-gather.31.cloned.1.call-update) | async-done | bytes 16777232 | tf_op jit(solution)/shard_map/all_gather | solution.py:13
  588.1 64.3 %all-gather.23.cloned.1.call-done = bf16[2048,2048]{1,0:T(8,128)(2,1)} async-done(((bf16[64,2048]{1,0:T(8,128)(2,1)}), bf16[2048,2048]{1,0:T(8,128)(2,1)}) %all-gather.23.cloned.1.call-update) | async-done | bytes 8388624 | tf_op jit(solution)/shard_map/all_gather | solution.py:182
  658.5 139.9 %all-gather.25.cloned.1.call-done = bf16[2048,5632]{1,0:T(8,128)(2,1)} async-done(((bf16[64,5632]{1,0:T(8,128)(2,1)}), bf16[2048,5632]{1,0:T(8,128)(2,1)}) %all-gather.25.cloned.1.call-update) | async-done | bytes 23068688 | tf_op jit(solution)/shard_map/all_gather | solution.py:212
  810.8 133.3 %all-gather.27.cloned.1.call-done = bf16[2048,5632]{1,0:T(8,128)(2,1)} async-done(((bf16[64,5632]{1,0:T(8,128)(2,1)}), bf16[2048,5632]{1,0:T(8,128)(2,1)}) %all-gather.27.cloned.1.call-update) | async-done | bytes 23068688 | tf_op jit(solution)/shard_map/all_gather | solution.py:213
  957.0 132.8 %all-gather.29.cloned.1.call-done = bf16[5632,2048]{1,0:T(8,128)(2,1)} async-done(((bf16[176,2048]{1,0:T(8,128)(2,1)}), bf16[5632,2048]{1,0:T(8,128)(2,1)}) %all-gather.29.cloned.1.call-update) | async-done | bytes 23068688 | tf_op jit(solution)/shard_map/all_gather | solution.py:214
  1164.0 31.1 all-gather.3
  1212.4 115.4 %while.107 = (s32[]{:T(128)}, f32[2,16,128,128]{3,2,1,0:T(8,128)}, f32[4,2,16,16,16,128]{5,4,3,2,1,0:T(8,128)}, f32[4,2,16,16,128,16]{4,5,3,2,1,0:T(8,128)}, f32...) while((s32[]{:T(128)}, f32[2,16,128,128]{3,2,1,0:T(8,128)}, ...), condition=%wide.region_16.17_spmd.clone.clone, body=%wide.region_14.16_spmd.clone.clone.sunk | while | flops 113500160 | bytes 36719068 | solution.py:118
  1345.3 187.7 %while.108 = (s32[]{:T(128)}, f32[2,16,128,128]{3,2,1,0:T(8,128)S(1)}, bf16[4,2,16,16,128]{4,2,3,1,0:T(8,128)(2,1)}, f32[4,2,16,16,128]{4,3,2,1,0:T(8,128)}, f32...) while((s32[]{:T(128)}, ...), condition=%wide.region_23.24_spmd.clone.clone, body=%wide.region_17.23_spmd.clone.clone.sunk | while | flops 444399616 | bytes 64262320 | solution.py:118
  1566.9 18.4 fusion.157
  1606.2 18.2 fusion.159
  1660.4 45.5 all-reduce.9
  1709.4 287.1 %reduce-scatter.17.cloned.1.call-done = f32[64,2048]{1,0:T(8,128)} async-done(((f32[2048,2048]{1,0:T(8,128)}), f32[64,2048]{1,0:T(8,128)}) %reduce-scatter.17.cloned.1.call-update) | async-done | bytes 524304 | tf_op jit(solution)/shard_map/reduce_scatter | solution.py:287
  1996.6 360.2 %reduce-scatter.9.cloned.1.call-done = f32[64,2048]{1,0:T(8,128)} async-done(((f32[2048,2048]{1,0:T(8,128)}), f32[64,2048]{1,0:T(8,128)}) %reduce-scatter.9.cloned.1.call-update) | async-done | bytes 524304 | tf_op jit(solution)/shard_map/reduce_scatter | solution.py:283
  2356.8 360.1 %reduce-scatter.11.cloned.1.call-done = f32[64,2048]{1,0:T(8,128)} async-done(((f32[2048,2048]{1,0:T(8,128)}), f32[64,2048]{1,0:T(8,128)}) %reduce-scatter.11.cloned.1.call-update) | async-done | bytes 524304 | tf_op jit(solution)/shard_map/reduce_scatter | solution.py:284
  2716.9 360.1 %reduce-scatter.13.cloned.1.call-done = f32[64,2048]{1,0:T(8,128)} async-done(((f32[2048,2048]{1,0:T(8,128)}), f32[64,2048]{1,0:T(8,128)}) %reduce-scatter.13.cloned.1.call-update) | async-done | bytes 524304 | tf_op jit(solution)/shard_map/reduce_scatter | solution.py:285
  3077.0 970.8 %reduce-scatter.19.cloned.1.call-done = f32[64,5632]{1,0:T(8,128)} async-done(((f32[2048,5632]{1,0:T(8,128)}), f32[64,5632]{1,0:T(8,128)}) %reduce-scatter.19.cloned.1.call-update) | async-done | bytes 1441808 | tf_op jit(solution)/shard_map/reduce_scatter | solution.py:233
  4047.8 970.1 %reduce-scatter.21.cloned.1.call-done = f32[64,5632]{1,0:T(8,128)} async-done(((f32[2048,5632]{1,0:T(8,128)}), f32[64,5632]{1,0:T(8,128)}) %reduce-scatter.21.cloned.1.call-update) | async-done | bytes 1441808 | tf_op jit(solution)/shard_map/reduce_scatter | solution.py:234
  5017.8 970.1 %reduce-scatter.23.cloned.1.call-done = f32[176,2048]{1,0:T(8,128)} async-done(((f32[5632,2048]{1,0:T(8,128)}), f32[176,2048]{1,0:T(8,128)}) %reduce-scatter.23.cloned.1.call-update) | async-done | bytes 1441808 | tf_op jit(solution)/shard_map/reduce_scatter | solution.py:235
  (530 shorter events, 701.9 us)
Async XLA Ops:
  7.2 82.7 %all-gather.15.cloned.1.call-start = ((), (), s32[]{:S(2)}) async-start(), calls=%async_computation.8 | async-start | bytes 8650752 | tf_op jit(solution)/shard_map/all_gather | solution.py:179
  7.9 161.0 %all-gather.19.cloned.1.call-start = ((), (), s32[]{:S(2)}) async-start(), calls=%async_computation.10 | async-start | bytes 8650752 | tf_op jit(solution)/shard_map/all_gather | solution.py:178
  8.7 239.2 %all-gather.17.cloned.1.call-start = ((), (), s32[]{:S(2)}) async-start(), calls=%async_computation.9 | async-start | bytes 8650752 | tf_op jit(solution)/shard_map/all_gather | solution.py:180
  9.4 377.1 %all-gather.21.cloned.1.call-start = ((), (), s32[]{:S(2)}) async-start(), calls=%async_computation.11 | async-start | bytes 8650752 | tf_op jit(solution)/shard_map/all_gather | solution.py:181
  10.0 564.0 %all-gather.31.cloned.1.call-start = ((), (), s32[]{:S(2)}) async-start(), calls=%async_computation.24 | async-start | bytes 18874368 | tf_op jit(solution)/shard_map/all_gather | solution.py:13
  58.4 110.5 %copy-start.8 = (bf16[128,2048]{1,0:T(8,128)(2,1)}, bf16[128,2048]{1,0:T(8,128)(2,1)S(1)}, u32[]{:S(2)}) copy-start(bf16[128,2048]{1,0:T(8,128)(2,1)S(1)} %fusion.118) | copy-start | bytes 1572868
  59.8 200.4 %copy-start.32 = (bf16[2,1,64,2048]{3,2,1,0:T(8,128)(2,1)}, bf16[2,1,64,2048]{3,2,1,0:T(8,128)(2,1)S(1)}, u32[]{:S(2)}) copy-start(bf16[2,1,64,2048]{3,2,1,0:T(8,128)(2,1)S(1)} %fusion.122) | copy-start | bytes 1572868
  346.6 305.8 %all-gather.23.cloned.1.call-start = ((), (), s32[]{:S(2)}) async-start(), calls=%async_computation.12 | async-start | bytes 8650752 | tf_op jit(solution)/shard_map/all_gather | solution.py:182
  347.2 451.2 %all-gather.25.cloned.1.call-start = ((), (), s32[]{:S(2)}) async-start(), calls=%async_computation.13 | async-start | bytes 23789568 | tf_op jit(solution)/shard_map/all_gather | solution.py:212
  347.9 596.2 %all-gather.27.cloned.1.call-start = ((), (), s32[]{:S(2)}) async-start(), calls=%async_computation.14 | async-start | bytes 23789568 | tf_op jit(solution)/shard_map/all_gather | solution.py:213
  348.7 741.2 %all-gather.29.cloned.1.call-start = ((), (), s32[]{:S(2)}) async-start(), calls=%async_computation.15 | async-start | bytes 23789568 | tf_op jit(solution)/shard_map/all_gather | solution.py:214
  349.4 978.4 %all-gather.33.cloned.1.call-start = ((), (), s32[]{:S(2)}) async-start(), calls=%async_computation.25 | async-start | bytes 9437184 | tf_op jit(solution)/shard_map/all_gather | solution.py:27
  391.2 193.7 %copy-start.6 = (f32[128,2048]{1,0:T(8,128)}, f32[128,2048]{1,0:T(8,128)S(1)}, u32[]{:S(2)}) copy-start(f32[128,2048]{1,0:T(8,128)S(1)} %fusion.151) | copy-start | bytes 3145732
  657.4 474.9 %copy-start.4 = (f32[128,2048]{1,0:T(8,128)}, f32[128,2048]{1,0:T(8,128)S(1)}, u32[]{:S(2)}) copy-start(f32[128,2048]{1,0:T(8,128)S(1)} %get-tuple-element.1614) | copy-start | bytes 3145732
  1153.1 556.3 %reduce-scatter.15.cloned.1.call-start = ((), (), s32[]{:S(2)}) async-start(), calls=%async_computation.19 | async-start | bytes 17301504 | tf_op jit(solution)/shard_map/reduce_scatter | solution.py:286
  1162.2 834.4 %reduce-scatter.17.cloned.1.call-start = ((), (), s32[]{:S(2)}) async-start(), calls=%async_computation.20 | async-start | bytes 17301504 | tf_op jit(solution)/shard_map/reduce_scatter | solution.py:287
  1207.6 1149.2 %reduce-scatter.9.cloned.1.call-start = ((), (), s32[]{:S(2)}) async-start(), calls=%async_computation.16 | async-start | bytes 17301504 | tf_op jit(solution)/shard_map/reduce_scatter | solution.py:283
  1543.5 1173.4 %reduce-scatter.11.cloned.1.call-start = ((), (), s32[]{:S(2)}) async-start(), calls=%async_computation.17 | async-start | bytes 17301504 | tf_op jit(solution)/shard_map/reduce_scatter | solution.py:284
  1555.9 1521.1 %reduce-scatter.13.cloned.1.call-start = ((), (), s32[]{:S(2)}) async-start(), calls=%async_computation.18 | async-start | bytes 17301504 | tf_op jit(solution)/shard_map/reduce_scatter | solution.py:285
  1565.4 2482.4 %reduce-scatter.19.cloned.1.call-start = ((), (), s32[]{:S(2)}) async-start(), calls=%async_computation.21 | async-start | bytes 47579136 | tf_op jit(solution)/shard_map/reduce_scatter | solution.py:233
  1585.3 3432.6 %reduce-scatter.21.cloned.1.call-start = ((), (), s32[]{:S(2)}) async-start(), calls=%async_computation.22 | async-start | bytes 47579136 | tf_op jit(solution)/shard_map/reduce_scatter | solution.py:234
  1604.8 4383.2 %reduce-scatter.23.cloned.1.call-start = ((), (), s32[]{:S(2)}) async-start(), calls=%async_computation.23 | async-start | bytes 47579136 | tf_op jit(solution)/shard_map/reduce_scatter | solution.py:235
  1657.2 50.9 copy-start.56
  1657.2 50.9 copy-start.20
  (68 other events, 483.0 us)
Sparse Core Ops, SparseCore 0:
  11.0 78.8 all-gather.14
  92.8 75.9 all-gather.18
  171.9 75.9 all-gather.16
  250.7 75.9 all-gather.20
  346.7 227.2 all-gather.30
  576.8 75.5 all-gather.22
  655.3 143.0 all-gather.24
  801.3 142.7 all-gather.26
  947.0 142.7 all-gather.28
  1153.2 124.0 all-gather.32
  1280.2 354.7 reduce-scatter.14
  1637.8 358.7 reduce-scatter.16
  1999.4 357.2 reduce-scatter.8
  2359.5 357.3 reduce-scatter.10
  2719.6 357.3 reduce-scatter.12
  3079.7 968.0 reduce-scatter.18
  4050.5 967.3 reduce-scatter.20
  5020.6 967.3 reduce-scatter.22
where the time goes:
time: 6010 us; the launch traced here: 5990 us
  waiting for transfers between devices  5110 us (85%)
  matrix products  397 us (7%)
  other arithmetic  180 us (3%)
  blocking collectives  150 us (2%)
  local copies, waits for them, and re-layouts  140 us (2%)
    reduce_scatter x1, waiting for transfers between devices, on_device(): lax.psum_scatter(term_gate, ('dp', 'fsdp'), scatter_dimension=0, tiled=True)  971 us
    reduce_scatter x1, waiting for transfers between devices, on_device(): lax.psum_scatter(term_down, ('dp', 'fsdp'), scatter_dimension=0, tiled=True)  970 us
    reduce_scatter x1, waiting for transfers between devices, on_device(): lax.psum_scatter(term_up, ('dp', 'fsdp'), scatter_dimension=0, tiled=True)  970 us
    reduce_scatter x1, waiting for transfers between devices, on_device(): lax.psum_scatter(term_query, ('dp', 'fsdp'), scatter_dimension=0, tiled=T...  360 us
    reduce_scatter x1, waiting for transfers between devices, on_device(): lax.psum_scatter(term_forget, ('dp', 'fsdp'), scatter_dimension=0, tiled=...  360 us
    reduce_scatter x1, waiting for transfers between devices, on_device(): lax.psum_scatter(term_input, ('dp', 'fsdp'), scatter_dimension=0, tiled=T...  360 us
    reduce_scatter x1, waiting for transfers between devices, on_device(): lax.psum_scatter(term_out, ('dp', 'fsdp'), scatter_dimension=0, tiled=True)  287 us
    all_gather x1, waiting for transfers between devices, carried_in(): gathered = jax.tree.map(lambda a: lax.all_gather(a, axis), part)  183 us
  transfers between devices with their start and end apart: 18, of which 15 were waited for; matrix products, arithmetic and copies ran while one was open for 11% of the time, Pallas kernels for 0%

commit v1 on v0

v1 whole, which is shorter than its diff:
```python
import functools

import jax
import jax.numpy as jnp
from jax import lax
from jax.experimental import pallas as pl
from jax.experimental.pallas import tpu as pltpu
from jax.sharding import PartitionSpec as P

HEAD = 128
LANES = 128
HIGHEST = lax.Precision.HIGHEST
NN = (((1,), (0,)), ((), ()))
NT = (((1,), (1,)), ((), ()))
TN = (((0,), (0,)), ((), ()))


def ranks():
    return lax.axis_size("fsdp") // 2


def rank():
    return lax.axis_index("fsdp") // 2


def side():
    return lax.axis_index("fsdp") % 2


def pick(array, index, axis=0):
    return lax.dynamic_index_in_dim(array, index, axis, False)


def swapped(array):
    count = lax.axis_size("fsdp")
    return lax.ppermute(array, "fsdp", [(i, i ^ 1) for i in range(count)])


def turned(array, turn):
    count = lax.axis_size("fsdp")
    return lax.ppermute(array, "fsdp", [(i, (i + 2 * turn) % count) for i in range(count)])


def across(array, bit):
    count = lax.axis_size("dp")
    return lax.ppermute(array, "dp", [(i, i ^ bit) for i in range(count)])


def placed(pieces):
    whole = jnp.zeros((len(pieces),) + pieces[0][1].shape, pieces[0][1].dtype)
    for index, piece in pieces:
        whole = lax.dynamic_update_index_in_dim(whole, piece, index, 0)
    return whole


def to_side(*arrays):
    here = side()
    got = swapped(jnp.concatenate([pick(array, 1 - here) for array in arrays], axis=0))
    both = [placed([(here, pick(a, here)[0]), (1 - here, piece)]) for a, piece in zip(arrays, got)]
    return [rows.reshape((-1,) + rows.shape[2:]) for rows in both]


def from_side(rows):
    here = side()
    halves = rows.reshape((2, 1, rows.shape[0] // 2) + rows.shape[1:])
    got = swapped(pick(halves, 1 - here))
    return placed([(here, pick(halves, here)), (1 - here, got)])


def shifted(array, step, among=None):
    count = ranks()
    starts = [r for r in (range(count) if among is None else among) if 0 <= r + step < count]
    moves = [(2 * r + s, 2 * (r + step) + s) for r in starts for s in range(2)]
    return lax.ppermute(array, "fsdp", moves)


def ends_traded(array):
    last = lax.axis_size("fsdp") - 2
    moves = [(s, last + s) for s in range(2)] + [(last + s, s) for s in range(2)]
    return lax.ppermute(array, "fsdp", moves)


def gather_first(own):
    if ranks() != 4:
        return [turned(own, turn) for turn in range(1, ranks())]
    return [shifted(own, 1), shifted(own, -1), ends_traded(own)]


def gather_second(first):
    return [] if ranks() != 4 else [shifted(first[0], 1, (1, 2)), shifted(first[1], -1, (1, 2))]


def gathered(own, first, second):
    here = rank()
    if ranks() != 4:
        return jnp.concatenate([own] + first, axis=0)
    up, down, ends = first
    up2, down2 = second
    near = [jnp.where(here == 0, ends, up), jnp.where(here >= 2, up2, down2)]
    return jnp.concatenate([own] + near + [jnp.where(here == 3, ends, down)], axis=0)


def away_rows(operand):
    return operand[operand.shape[0] // ranks() :]


def own_rows(operand):
    return operand[: operand.shape[0] // ranks()]


def by_turn(away):
    return jnp.split(away.astype(jnp.bfloat16), ranks() - 1, axis=0)


def scatter_first(terms):
    if ranks() != 4:
        return [turned(term, -turn - 1) for turn, term in enumerate(terms)]
    ends = jnp.where(rank() == 0, terms[0], terms[2])
    return [shifted(terms[1], 1, (0, 1)), shifted(terms[1], -1, (2, 3)), ends_traded(ends)]


def scatter_second(terms, first):
    if ranks() != 4:
        return []
    up = terms[2].astype(jnp.float32) + first[0].astype(jnp.float32)
    down = terms[0].astype(jnp.float32) + first[1].astype(jnp.float32)
    return [shifted(up.astype(jnp.bfloat16), 1), shifted(down.astype(jnp.bfloat16), -1)]


def scattered(own, first, second):
    for piece in first if ranks() != 4 else first[2:] + second:
        own = own + piece.astype(jnp.float32)
    return own


def sync(*arrays):
    return lax.optimization_barrier(arrays)


def dp_bits():
    bits, bit = [], 1
    while bit < lax.axis_size("dp"):
        bits.append(bit)
        bit *= 2
    return bits


def routes(side_first):
    bits = [((bit, 0), functools.partial(across, bit=bit)) for bit in reversed(dp_bits())]
    return [((0, 1), swapped)] + bits if side_first else bits[:-1] + [((0, 1), swapped)] + bits[-1:]


def user_moves():
    dp, fsdp = lax.axis_size("dp"), lax.axis_size("fsdp")
    moves = []
    for block in range(dp * fsdp):
        user, part = divmod(block, 2 * dp)
        moves.append((block, (part // 2) * fsdp + 2 * user + part % 2))
    return moves


def to_users(rows):
    return lax.ppermute(rows, ("dp", "fsdp"), user_moves())


def to_owners(rows):
    return lax.ppermute(rows, ("dp", "fsdp"), [(b, a) for a, b in user_moves()])


def cut_kernel(order_ref, *refs):
    count = order_ref.shape[0]
    weights, pieces = refs[:-count], refs[-count:]
    for turn in range(count):
        start = 0
        for weight in weights:
            width = weight.shape[1] // (1 if weight.shape[1] == LANES else count)
            column = 0
            if weight.shape[1] != LANES:
                column = pl.multiple_of(order_ref[turn] * width, LANES)
            pieces[turn][:, start : start + width] = weight[:, pl.ds(column, width)]
            start += width


def cut_columns(order, *weights):
    count = ranks()
    rows = weights[0].shape[0]
    vmem = pl.BlockSpec(memory_space=pltpu.VMEM)
    width = sum(LANES if w.shape[1] == LANES else w.shape[1] // count for w in weights)
    return pl.pallas_call(
        cut_kernel,
        in_specs=[pl.BlockSpec(memory_space=pltpu.SMEM)] + [vmem] * len(weights),
        out_specs=[vmem] * count,
        out_shape=[jax.ShapeDtypeStruct((rows, width), weights[0].dtype)] * count,
        compiler_params=pltpu.CompilerParams(vmem_limit_bytes=24 * 1024 * 1024),
        name="cut_columns",
    )(order, *weights)


def join_kernel(order_ref, *refs):
    count = order_ref.shape[0]
    parts = (len(refs) - count - 1) // 2
    pieces, weights = refs[:count], refs[count : count + parts]
    grads, product = refs[count + parts : -1], refs[-1]
    total = jnp.zeros(product.shape, jnp.float32)
    for turn in range(count):
        start = 0
        for weight, grad in zip(weights, grads):
            width = weight.shape[1] // count
            columns = pl.ds(pl.multiple_of(order_ref[turn] * width, LANES), width)
            piece = pieces[turn][:, start : start + width].astype(jnp.float32)
            grad[:, columns] = piece
            term = piece * weight[:, columns].astype(jnp.float32)
            total = total + jnp.sum(term, axis=1, keepdims=True)
            start += width
    product[...] = total


def join_columns(order, pieces, weights):
    rows = weights[0].shape[0]
    vmem = pl.BlockSpec(memory_space=pltpu.VMEM)
    *grads, product = pl.pallas_call(
        join_kernel,
        in_specs=[pl.BlockSpec(memory_space=pltpu.SMEM)] + [vmem] * (len(pieces) + len(weights)),
        out_specs=[vmem] * (len(weights) + 1),
        out_shape=[jax.ShapeDtypeStruct(w.shape, jnp.float32) for w in weights]
        + [jax.ShapeDtypeStruct((rows, 1), jnp.float32)],
        compiler_params=pltpu.CompilerParams(vmem_limit_bytes=32 * 1024 * 1024),
        name="join_columns",
    )(order, *pieces, *weights)
    return grads, product[:, 0]


def assemble_kernel(place_ref, near_ref, far_ref, near_core_ref, far_core_ref, whole_ref, sems, *, marks):
    count = near_ref.shape[1]
    dp_index, here, first_rank = place_ref[0], place_ref[1], place_ref[2]
    copies = []
    for blocks, refs in ((0, (near_ref, far_ref)), (1, (near_core_ref, far_core_ref))):
        for outer in range(2):
            for inner in range(2):
                dp_mark, side_mark = marks[outer][inner]
                spot = jnp.bitwise_xor(dp_index, dp_mark + blocks)
                its_side = jnp.bitwise_xor(here, side_mark)
                for turn in range(count):
                    its_rank = lax.rem(first_rank - turn + count, count)
                    copies.append(
                        pltpu.make_async_copy(
                            refs[outer].at[inner, turn],
                            whole_ref.at[spot, its_rank, its_side],
                            sems.at[len(copies)],
                        )
                    )
                    copies[-1].start()
    for copy in copies:
        copy.wait()


def assembled(near, far, near_core, far_core, side_first):
    dp, (_, count, rows, columns) = lax.axis_size("dp"), near.shape
    big = dp // 2
    marks = (((0, 0), (0, 1)), ((big, 0), (big, 1))) if side_first else (((0, 0), (big, 0)), ((0, 1), (big, 1)))
    place = jnp.stack([lax.axis_index("dp"), side(), rank()]).astype(jnp.int32)
    anywhere = pl.BlockSpec(memory_space=pl.ANY)
    whole = pl.pallas_call(
        functools.partial(assemble_kernel, marks=marks),
        in_specs=[pl.BlockSpec(memory_space=pltpu.SMEM)] + [anywhere] * 4,
        out_specs=pl.BlockSpec(memory_space=pltpu.VMEM),
        out_shape=jax.ShapeDtypeStruct((dp, count, 2, rows, columns), near.dtype),
        scratch_shapes=[pltpu.SemaphoreType.DMA((8 * count,))],
        compiler_params=pltpu.CompilerParams(vmem_limit_bytes=24 * 1024 * 1024),
        cost_estimate=pl.CostEstimate(
            flops=0, bytes_accessed=32 * near.size, transcendentals=0
        ),
        name="assemble_rows",
    )(place, near, far, near_core, far_core)
    return whole.reshape(-1, columns)


def traded(pieces):
    return [pieces[0]] + [turned(piece, turn) for turn, piece in enumerate(pieces) if turn]


def turns(step):
    return (rank() + step * jnp.arange(ranks(), dtype=jnp.int32) + ranks()) % ranks()


def term_blocks(term):
    dp, count = lax.axis_size("dp"), ranks()
    bits = len(dp_bits())
    term = term.reshape((2,) * bits + (count, 2, term.shape[0] // (2 * dp * count), term.shape[-1]))
    return jnp.moveaxis(term, bits + 1, bits)


def shrunk(state, route):
    terms, marks = state
    mark, exchange = route
    axis = marks.index(mark)
    own = (lax.axis_index("dp") // mark[0]) % 2 if mark[0] else side()
    got = exchange(pick(terms, 1 - own, axis))
    total = pick(terms, own, axis).astype(jnp.float32) + got.astype(jnp.float32)
    return (total.astype(jnp.bfloat16), marks[:axis] + marks[axis + 1 :])


def block_marks():
    return [(bit, 0) for bit in reversed(dp_bits())] + [(0, 1)]


def peers():
    dp, fsdp = lax.axis_size("dp"), lax.axis_size("fsdp")
    return [[d * fsdp + 2 * r + s for d in range(dp) for s in range(2)] for r in range(fsdp // 2)]


def peers_gather(rows):
    return lax.all_gather(rows, ("dp", "fsdp"), tiled=True, axis_index_groups=peers())


def peers_scatter(terms):
    return lax.psum_scatter(
        terms, ("dp", "fsdp"), scatter_dimension=0, tiled=True, axis_index_groups=peers()
    )


def matmul(left_side, right_side):
    return jnp.dot(left_side, right_side, preferred_element_type=jnp.float32)


def outer_sum(left_side, right_side):
    return lax.dot_general(left_side, right_side, TN, preferred_element_type=jnp.float32)


def back_product(left_side, right_side):
    return lax.dot_general(left_side, right_side, NT, preferred_element_type=jnp.float32)


def dot(left, right, dims, precision=HIGHEST):
    return lax.dot_general(
        left, right, dims, precision=precision, preferred_element_type=jnp.float32
    )


def decayed(forget_proj, slack, lower):
    sig = jax.nn.sigmoid(forget_proj)
    keys = slack * (1.0 - sig)
    running = dot(lower, jnp.log1p(-keys), NN)
    return (sig, keys, running)


def triangle(size):
    rows = lax.broadcasted_iota(jnp.int32, (size, size), 0)
    columns = lax.broadcasted_iota(jnp.int32, (size, size), 1)
    return jnp.where(rows >= columns, 1.0, 0.0)


def normed_head(mixed, gate):
    sig = jax.nn.sigmoid(gate)
    silu = gate * sig
    gated = mixed * silu
    centred = gated - jnp.mean(gated, axis=-1, keepdims=True)
    inv = lax.rsqrt(jnp.mean(centred * centred, axis=-1, keepdims=True) + 1e-05)
    return (sig, silu, inv, centred * inv)


def forward_kernel(
    order_ref, query_ref, value_ref, slack_ref, gain_ref, unit_ref, mixed_ref, states_ref, state
):
    span = query_ref.shape[1]
    share = slack_ref.shape[1]

    @pl.when(pl.program_id(0) == 0)
    def _():
        state[...] = jnp.zeros_like(state)

    states_ref[0] = state[...]
    lower = triangle(span)
    _, keys, running = decayed(query_ref[0, :, share:], slack_ref[...], lower)
    grown = jnp.exp(running)
    queries = query_ref[0, :, :share] * grown
    keys = keys * jnp.exp(-running)
    for head in range(share // HEAD):
        here = slice(head * HEAD, (head + 1) * HEAD)
        gate_here = slice(share + head * HEAD, share + (head + 1) * HEAD)
        values = value_ref[0, :, here]
        before = state[head]
        scores = dot(queries[:, here], keys[:, here], NT) * lower
        mixed = dot(scores, values, NN) + dot(queries[:, here], before, NT)
        state[head] = (before + dot(values, keys[:, here], TN)) * grown[span - 1 :, here]
        mixed_ref[0, :, here] = mixed
        normed = normed_head(mixed, value_ref[0, :, gate_here])[3]
        unit_ref[0, :, here] = (normed * gain_ref[:, here]).astype(jnp.bfloat16)


def backward_kernel(
    order_ref,
    query_ref,
    value_ref,
    slack_ref,
    gain_ref,
    mixed_ref,
    states_ref,
    d_unit_ref,
    d_query_ref,
    d_value_ref,
    term_ref,
    back,
    carry,
):
    span = query_ref.shape[1]
    share = slack_ref.shape[1]

    @pl.when(pl.program_id(0) == 0)
    def _():
        back[...] = jnp.zeros_like(back)
        carry[...] = jnp.zeros_like(carry)
        term_ref[...] = jnp.zeros_like(term_ref)

    lower = triangle(span)
    slack = slack_ref[...]
    sig, raw_keys, running = decayed(query_ref[0, :, share:], slack, lower)
    grown, shrunk = jnp.exp(running), jnp.exp(-running)
    all_queries = query_ref[0, :, :share] * grown
    all_keys = raw_keys * shrunk
    d_running, d_raw_keys = [], []
    for head in range(share // HEAD):
        here = slice(head * HEAD, (head + 1) * HEAD)
        there = slice(share + head * HEAD, share + (head + 1) * HEAD)
        queries, keys = all_queries[:, here], all_keys[:, here]
        values, gate = value_ref[0, :, here], value_ref[0, :, there]
        mixed = mixed_ref[0, :, here]
        d_unit = d_unit_ref[0, :, here]
        sig_gate, silu, inv, normed = normed_head(mixed, gate)
        term_ref[1:2, here] += jnp.sum(d_unit * normed, axis=0, keepdims=True)
        d_n = d_unit * gain_ref[:, here]
        d_gated = inv * (
            d_n
            - jnp.mean(d_n, axis=-1, keepdims=True)
            - normed * jnp.mean(d_n * normed, axis=-1, keepdims=True)
        )
        d_mixed = d_gated * silu
        d_gate = d_gated * mixed * sig_gate * (1.0 + gate * (1.0 - sig_gate))
        d_value_ref[0, :, there] = d_gate.astype(jnp.bfloat16)
        before = states_ref[0, head]
        after_grad = back[head] * grown[span - 1 :, here]
        scores = dot(queries, keys, NT) * lower
        d_scores = dot(d_mixed, values, NT) * lower
        d_queries = dot(d_scores, keys, NN) + dot(d_mixed, before, NN)
        d_keys = dot(d_scores, queries, TN) + dot(values, after_grad, NN)
        d_values = dot(scores, d_mixed, TN) + dot(keys, after_grad, NT)
        before_grad = dot(d_mixed, queries, TN) + after_grad
        d_value_ref[0, :, here] = d_values.astype(jnp.bfloat16)
        d_query_ref[0, :, here] = (d_queries * grown[:, here]).astype(jnp.bfloat16)
        back[head] = before_grad
        d_running.append(queries * d_queries - keys * d_keys)
        d_raw_keys.append(d_keys * shrunk[:, here])
    d_log = dot(lower, jnp.concatenate(d_running, axis=-1), TN) + carry[...]
    for head in range(share // HEAD):
        here = slice(head * HEAD, (head + 1) * HEAD)
        carry[:, here] = jnp.sum(states_ref[0, head] * back[head], axis=0, keepdims=True)
    e = jnp.concatenate(d_raw_keys, axis=-1) - d_log / (1.0 - raw_keys)
    term_ref[0:1, :] += jnp.sum(e * (1.0 - sig), axis=0, keepdims=True)
    d_query_ref[0, :, share:] = (-e * slack * sig * (1.0 - sig)).astype(jnp.bfloat16)


def row_block(step, order_ref):
    return (order_ref[step], 0, 0)


def state_block(step, order_ref):
    return (order_ref[step], 0, 0, 0)


def fixed_block(step, order_ref):
    return (0, 0)


def run_forward(order, queries, values, slack, gain):
    blocks, span, columns = queries.shape
    share = columns // 2
    heads = share // HEAD
    return pl.pallas_call(
        forward_kernel,
        grid_spec=pltpu.PrefetchScalarGridSpec(
            num_scalar_prefetch=1,
            grid=(blocks,),
            in_specs=[
                pl.BlockSpec((1, span, columns), row_block),
                pl.BlockSpec((1, span, columns), row_block),
                pl.BlockSpec((1, share), fixed_block),
                pl.BlockSpec((1, share), fixed_block),
            ],
            out_specs=[
                pl.BlockSpec((1, span, share), row_block),
                pl.BlockSpec((1, span, share), row_block),
                pl.BlockSpec((1, heads, HEAD, HEAD), state_block),
            ],
            scratch_shapes=[pltpu.VMEM((heads, HEAD, HEAD), jnp.float32)],
        ),
        out_shape=[
            jax.ShapeDtypeStruct((blocks, span, share), jnp.bfloat16),
            jax.ShapeDtypeStruct((blocks, span, share), jnp.float32),
            jax.ShapeDtypeStruct((blocks, heads, HEAD, HEAD), jnp.float32),
        ],
        compiler_params=pltpu.CompilerParams(vmem_limit_bytes=24 * 1024 * 1024),
        cost_estimate=pl.CostEstimate(
            flops=40 * queries.size * span, bytes_accessed=20 * queries.size, transcendentals=2 * queries.size
        ),
        name="recurrence_forward",
    )(order, queries, values, slack, gain)


def run_backward(order, queries, values, slack, gain, mixed, states, d_unit):
    blocks, span, columns = queries.shape
    share = columns // 2
    heads = share // HEAD
    return pl.pallas_call(
        backward_kernel,
        grid_spec=pltpu.PrefetchScalarGridSpec(
            num_scalar_prefetch=1,
            grid=(blocks,),
            in_specs=[
                pl.BlockSpec((1, span, columns), row_block),
                pl.BlockSpec((1, span, columns), row_block),
                pl.BlockSpec((1, share), fixed_block),
                pl.BlockSpec((1, share), fixed_block),
                pl.BlockSpec((1, span, share), row_block),
                pl.BlockSpec((1, heads, HEAD, HEAD), state_block),
                pl.BlockSpec((1, span, share), row_block),
            ],
            out_specs=[
                pl.BlockSpec((1, span, columns), row_block),
                pl.BlockSpec((1, span, columns), row_block),
                pl.BlockSpec((2, share), fixed_block),
            ],
            scratch_shapes=[
                pltpu.VMEM((heads, HEAD, HEAD), jnp.float32),
                pltpu.VMEM((1, share), jnp.float32),
            ],
        ),
        out_shape=[
            jax.ShapeDtypeStruct((blocks, span, columns), jnp.bfloat16),
            jax.ShapeDtypeStruct((blocks, span, columns), jnp.bfloat16),
            jax.ShapeDtypeStruct((2, share), jnp.float32),
        ],
        compiler_params=pltpu.CompilerParams(vmem_limit_bytes=32 * 1024 * 1024),
        cost_estimate=pl.CostEstimate(
            flops=80 * queries.size * span, bytes_accessed=30 * queries.size, transcendentals=2 * queries.size
        ),
        name="recurrence_backward",
    )(order, queries, values, slack, gain, mixed, states, d_unit)


def inverse_rms(values):
    return lax.rsqrt(jnp.mean(values * values, axis=-1, keepdims=True) + 1e-06)


def unscaled_grad(d_scaled, scaled, inverse):
    return inverse * (d_scaled - scaled * jnp.mean(d_scaled * scaled, axis=-1, keepdims=True))


def on_device(
    inputs,
    cotangent,
    norm_gain,
    mixer_gain,
    ffn_gain,
    slack,
    w_query,
    w_forget,
    w_input,
    w_gate_out,
    w_out,
    w_gate,
    w_up,
    w_down,
):
    width = inputs.shape[-1]
    dp, count, here = lax.axis_size("dp"), ranks(), rank()
    float32, bfloat16 = jnp.float32, jnp.bfloat16
    sending, taking = turns(1), turns(-1)
    mixer_weights = (w_query, w_forget, w_input, w_gate_out)
    ffn_weights = (w_gate, w_up)
    core, big = 1, dp // 2

    gains = jnp.stack([norm_gain, ffn_gain, mixer_gain, slack], axis=1)
    gains = jnp.pad(gains, ((0, 0), (0, LANES - gains.shape[1])))
    cut = traded(cut_columns(sending, w_query, w_forget, gains, w_input, w_gate_out))
    users_out = to_users(w_out)
    own_in, own_d = to_side(inputs, cotangent)
    own_in, own_d, cut = sync(own_in, own_d, cut)

    first_in = gather_first(own_in)
    split = 2 * (width // count) + LANES
    query_cut = jnp.stack([piece[:, :split] for piece in cut])
    value_cut = jnp.stack([piece[:, split:] for piece in cut])
    query_near = jnp.stack([query_cut, across(query_cut, big)])
    value_near = jnp.stack([value_cut, swapped(value_cut)])
    first_in, query_near, value_near, users_out = sync(first_in, query_near, value_near, users_out)

    second_in = gather_second(first_in)
    query_far = swapped(query_near)
    value_far = across(value_near, big)
    mixer_out = peers_gather(users_out)
    second_in, query_far, value_far, late_gate, late_up, late_down = sync(
        second_in, query_far, value_far, w_gate, w_up, w_down
    )

    query_blocks = (query_near, query_far, across(query_near, core), across(query_far, core))
    value_blocks = (value_near, value_far, across(value_near, core), across(value_far, core))
    raw_in = gathered(own_in, first_in, second_in)
    raw_in, query_blocks, value_blocks = sync(raw_in, query_blocks, value_blocks)

    cut = traded(cut_columns(sending, late_gate, late_up))
    query_in = assembled(*query_blocks, False)
    value_in = assembled(*value_blocks, True)
    share = value_in.shape[-1]
    gains = jnp.transpose(query_in[:, share:])[:4].astype(float32)
    gain_first, gain_second = gains[0], gains[1]
    here_gains = lax.dynamic_slice(gains, (2, here * (width // count)), (2, width // count))
    mixer_gain_here, slack_here = here_gains[:1], here_gains[1:]
    query_in = query_in[:, :share]

    all_tokens = raw_in.astype(float32)
    rows_in = (all_tokens * inverse_rms(all_tokens) * gain_first).astype(bfloat16)
    queries = matmul(rows_in, query_in).reshape(count, -1, share)
    values = matmul(rows_in, value_in).reshape(count, -1, share)
    unit, mixed, states = run_forward(taking, queries, values, slack_here, mixer_gain_here)
    rows_unit = unit.reshape(-1, unit.shape[-1])
    branch_terms = by_turn(matmul(away_rows(rows_unit), mixer_out))
    branch_terms, cut, late_down = sync(branch_terms, cut, late_down)

    branch_first = scatter_first(branch_terms)
    branch_own = matmul(own_rows(rows_unit), mixer_out)
    units = cut[0].shape[-1] // 2
    gate_cut = jnp.stack([piece[:, :units] for piece in cut])
    up_cut = jnp.stack([piece[:, units:] for piece in cut])
    gate_near = jnp.stack([gate_cut, across(gate_cut, big)])
    up_near = jnp.stack([up_cut, swapped(up_cut)])
    branch_first, branch_own, gate_near, up_near = sync(branch_first, branch_own, gate_near, up_near)

    branch_second = scatter_second(branch_terms, branch_first)
    gate_far = swapped(gate_near)
    up_far = across(up_near, big)
    users_down = to_users(late_down)
    tokens = own_in.astype(float32)
    hidden = tokens + scattered(branch_own, branch_first, branch_second)
    second_inverse = inverse_rms(hidden)
    hidden_hat = hidden * second_inverse
    own_mid = (hidden_hat * gain_second).astype(bfloat16)
    own_mid, users_down = sync(own_mid, users_down)

    first_mid = gather_first(own_mid)
    down = peers_gather(users_down)
    first_mid, gate_far, up_far = sync(first_mid, gate_far, up_far)

    second_mid = gather_second(first_mid)
    gate_blocks = (gate_near, gate_far, across(gate_near, core), across(gate_far, core))
    up_blocks = (up_near, up_far, across(up_near, core), across(up_far, core))
    second_mid, gate_blocks, up_blocks, late_d = sync(second_mid, gate_blocks, up_blocks, own_d)

    first_d = gather_first(late_d)
    rows_mid = gathered(own_mid, first_mid, second_mid)
    gate_in = assembled(*gate_blocks, False)
    gate_proj = matmul(rows_mid, gate_in)
    first_d, gate_proj = sync(first_d, gate_proj)

    second_d = gather_second(first_d)
    up_in = assembled(*up_blocks, True)
    up_proj = matmul(rows_mid, up_in)
    second_d, up_proj = sync(second_d, up_proj)

    rows_d = gathered(own_d, first_d, second_d)
    sig = jax.nn.sigmoid(gate_proj)
    inner = (gate_proj * sig * up_proj).astype(bfloat16)
    d_inner = back_product(rows_d, down)
    d_gate = (d_inner * up_proj * sig * (1.0 + gate_proj * (1.0 - sig))).astype(bfloat16)
    d_up = (d_inner * gate_proj * sig).astype(bfloat16)

    def hidden_product(cut):
        return back_product(cut(d_gate), gate_in) + back_product(cut(d_up), up_in)

    mid_terms = by_turn(hidden_product(away_rows))
    mid_terms, d_gate, d_up = sync(mid_terms, d_gate, d_up)

    mid_first = scatter_first(mid_terms)
    mid_own = hidden_product(own_rows)
    gate_term = term_blocks(outer_sum(rows_mid, d_gate).astype(bfloat16))
    mid_first, mid_own, gate_term = sync(mid_first, mid_own, gate_term)

    mid_second = scatter_second(mid_terms, mid_first)
    up_term = term_blocks(outer_sum(rows_mid, d_up).astype(bfloat16))
    d_hidden = own_d.astype(float32) + unscaled_grad(
        scattered(mid_own, mid_first, mid_second) * gain_second, hidden_hat, second_inverse
    )
    own_branch = d_hidden.astype(bfloat16)
    own_branch, up_term = sync(own_branch, up_term)

    first_branch = gather_first(own_branch)
    gate_state = shrunk((gate_term, block_marks()), ((core, 0), functools.partial(across, bit=core)))
    up_state = shrunk((up_term, block_marks()), ((core, 0), functools.partial(across, bit=core)))
    out_terms = by_turn(matmul(away_rows(inner), down))
    down_sum = peers_scatter(outer_sum(inner, rows_d).astype(bfloat16))
    first_branch, gate_total, up_total, out_terms = sync(
        first_branch, gate_state[0], up_state[0], out_terms
    )

    by_big, by_side = ((big, 0), functools.partial(across, bit=big)), ((0, 1), swapped)
    second_branch = gather_second(first_branch)
    gate_state = shrunk((gate_total, gate_state[1]), by_side)
    up_state = shrunk((up_total, up_state[1]), by_big)
    out_own = matmul(own_rows(inner), down)
    second_branch, out_own, gate_total, up_total = sync(
        second_branch, out_own, gate_state[0], up_state[0]
    )

    out_first = scatter_first(out_terms)
    gate_state = shrunk((gate_total, gate_state[1]), by_big)
    up_state = shrunk((up_total, up_state[1]), by_side)
    rows_branch = gathered(own_branch, first_branch, second_branch)
    d_unit = back_product(rows_branch, mixer_out).reshape(count, -1, mixer_out.shape[0])
    out_sum = peers_scatter(outer_sum(rows_unit, rows_branch).astype(bfloat16))
    d_queries, d_values, terms = run_backward(
        taking[::-1], queries, values, slack_here, mixer_gain_here, mixed, states, d_unit
    )
    d_queries = d_queries.reshape(-1, share)
    d_values = d_values.reshape(-1, share)

    def token_product(cut):
        return back_product(cut(d_queries), query_in) + back_product(cut(d_values), value_in)

    in_terms = by_turn(token_product(away_rows))
    in_terms, d_queries, d_values, out_first, gate_total, up_total = sync(
        in_terms, d_queries, d_values, out_first, gate_state[0], up_state[0]
    )

    in_first = scatter_first(in_terms)
    query_term = term_blocks(outer_sum(rows_in, d_queries).astype(bfloat16))
    value_term = term_blocks(outer_sum(rows_in, d_values).astype(bfloat16))
    by_core = ((core, 0), functools.partial(across, bit=core))
    query_state = shrunk((query_term, block_marks()), by_core)
    value_state = shrunk((value_term, block_marks()), by_core)
    in_own = token_product(own_rows)
    terms = jnp.transpose(terms.reshape(2, 2 * dp, -1), (1, 0, 2))
    terms = peers_scatter(terms.reshape(2 * dp, -1))
    in_first, in_own, query_total, value_total = sync(
        in_first, in_own, query_state[0], value_state[0]
    )

    in_second = scatter_second(in_terms, in_first)
    query_state = shrunk((query_total, query_state[1]), by_side)
    value_state = shrunk((value_total, value_state[1]), by_big)
    in_second, query_total, value_total = sync(in_second, query_state[0], value_state[0])

    out_second = scatter_second(out_terms, out_first)
    query_state = shrunk((query_total, query_state[1]), by_big)
    value_state = shrunk((value_total, value_state[1]), by_side)
    output = hidden + scattered(out_own, out_first, out_second)
    first_inverse = inverse_rms(tokens)
    d_normed = scattered(in_own, in_first, in_second)
    input_grad = d_hidden + unscaled_grad(
        d_normed * gain_first, tokens * first_inverse, first_inverse
    )
    query_total, value_total, output, input_grad = sync(
        query_state[0], value_state[0], output, input_grad
    )

    def parts(*totals):
        picked = [[pick(total, sending[turn]) for total in totals] for turn in range(count)]
        return traded([jnp.concatenate(pieces, axis=-1) for pieces in picked])

    ffn_parts = parts(gate_total, up_total)
    output, input_grad = from_side(output), from_side(input_grad)
    ffn_parts, late_terms, down_sum, out_sum, query_total, value_total = sync(
        ffn_parts, terms, down_sum, out_sum, query_total, value_total
    )

    mixer_parts = parts(query_total, value_total)
    out_rows = out_sum.shape[0]
    sums = to_owners(jnp.concatenate([out_sum, down_sum], axis=0))
    grad_out, grad_down = sums[:out_rows], sums[out_rows:]
    terms = to_owners(late_terms).reshape(2, -1)
    grads_ffn, ffn_product = join_columns(taking, ffn_parts, ffn_weights)
    grads_mixer, mixer_product = join_columns(taking, mixer_parts, mixer_weights)

    return (
        output,
        input_grad,
        mixer_product / norm_gain.astype(float32),
        terms[1],
        ffn_product / ffn_gain.astype(float32),
        terms[0],
        *grads_mixer,
        grad_out.astype(float32),
        *grads_ffn,
        grad_down.astype(float32),
    )


def solution(mesh):
    in_specs = (
        P(None, "dp", "fsdp", None),
        P(None, "dp", "fsdp", None),
        P(("dp", "fsdp")),
        P(("dp", "fsdp")),
        P(("dp", "fsdp")),
        P(("dp", "fsdp")),
        P(("dp", "fsdp"), None),
        P(("dp", "fsdp"), None),
        P(("dp", "fsdp"), None),
        P(("dp", "fsdp"), None),
        P(("dp", "fsdp"), None),
        P(("dp", "fsdp"), None),
        P(("dp", "fsdp"), None),
        P(("dp", "fsdp"), None),
    )
    out_specs = (
        P(None, "dp", "fsdp", None),
        P(None, "dp", "fsdp", None),
        P(("dp", "fsdp")),
        P(("dp", "fsdp")),
        P(("dp", "fsdp")),
        P(("dp", "fsdp")),
        P(("dp", "fsdp"), None),
        P(("dp", "fsdp"), None),
        P(("dp", "fsdp"), None),
        P(("dp", "fsdp"), None),
        P(("dp", "fsdp"), None),
        P(("dp", "fsdp"), None),
        P(("dp", "fsdp"), None),
        P(("dp", "fsdp"), None),
    )
    return jax.shard_map(
        on_device, mesh=mesh, in_specs=in_specs, out_specs=out_specs, check_vma=False
    )
```

time: 6010 us -> 777 us (0.13)
  waiting for transfers between devices: 5110 us -> 284 us
  matrix products: 397 us -> 78.5 us
  starting transfers between devices: 1.12 us -> 183 us
  blocking collectives: 150 us -> 18.6 us
  other arithmetic: 180 us -> 63.1 us
  local copies, waits for them, and re-layouts: 140 us -> 59.7 us
    reduce_scatter x8 -> x2, waiting for transfers between devices: 4280 us -> 0.04 us  [peers_scatter(): lax.psum_scatter(terms, ('dp', 'fsdp'), scatter_dimension=0, tiled=True,...]
    all_gather x10 -> x2, waiting for transfers between devices: 826 us -> 0.02 us  [peers_gather(): lax.all_gather(rows, ('dp', 'fsdp'), tiled=True, axis_index_groups=peers())]
    dot_general x58 -> x16, matrix products: 334 us -> 50.2 us  [the longest x10 25.6 us: back_product(): lax.dot_general(left_side, right_side, NT, preferred_element_type=jnp.flo...]
    ppermute x0 -> x87, waiting for transfers between devices: none -> 284 us  [the longest x32 99.7 us: shifted(): return lax.ppermute(array, 'fsdp', moves)]
    ppermute x0 -> x87, starting transfers between devices: none -> 183 us  [the longest x32 89.6 us: shifted(): return lax.ppermute(array, 'fsdp', moves)]
    unnamed x2 -> x1, blocking collectives: 87.3 us -> 18.6 us
    all_gather x2 -> x0, blocking collectives: 62.7 us -> none  [the longest x1 31.6 us: carried_in(): gathered = jax.tree.map(lambda a: lax.all_gather(a, axis), part)]
  transfers between devices with their start and end apart: 18 -> 91, of which waited for: 15 -> 32; matrix products, arithmetic and copies ran while one was open for 11% -> 20% of each run, Pallas kernels for 0% -> 7%
where the time goes in v1:
time: 777 us; the launch traced here: 765 us
  waiting for transfers between devices  284 us (37%)
  starting transfers between devices  183 us (24%)
  matrix products  78.5 us (10%)
  other arithmetic  63.1 us (8%)
  local copies, waits for them, and re-layouts  59.7 us (8%)
  Pallas kernels  53.6 us (7%)
  between operations  24.5 us (3%)
  blocking collectives  18.6 us (2%)
    ppermute x32, waiting for transfers between devices, shifted(): return lax.ppermute(array, 'fsdp', moves)  99.7 us
    ppermute x32, starting transfers between devices, shifted(): return lax.ppermute(array, 'fsdp', moves)  89.6 us
    ppermute x2, waiting for transfers between devices, to_users(): return lax.ppermute(rows, ('dp', 'fsdp'), user_moves())  49 us
    ppermute x11, waiting for transfers between devices, swapped(): return lax.ppermute(array, 'fsdp', [(i, i ^ 1) for i in range(count)])  35.6 us
    ppermute x8, waiting for transfers between devices, ends_traded(): return lax.ppermute(array, 'fsdp', moves)  34.4 us
    ppermute x8, starting transfers between devices, ends_traded(): return lax.ppermute(array, 'fsdp', moves)  30.2 us
    ppermute x2, waiting for transfers between devices, to_owners(): return lax.ppermute(rows, ('dp', 'fsdp'), [(b, a) for a, b in user_moves()])  29.2 us
    dot_general x8, matrix products, matmul(): return jnp.dot(left_side, right_side, preferred_element_type=jnp.float32)  28.2 us
  transfers between devices with their start and end apart: 91, of which 32 were waited for; matrix products, arithmetic and copies ran while one was open for 20% of the time, Pallas kernels for 7%

profile of v1, /device:TPU:2, one launch (start us, length us, event | category | flops | bytes accessed | tf_op | source)
XLA Modules:
  0.0 764.8 jit_solution(7195745476381471118)
XLA Ops:
  27.0 10.5 %collective-permute-done.2 = bf16[64,2176]{1,0:T(8,128)(2,1)} collective-permute-done((bf16[64,2176]{1,0:T(8,128)(2,1)S(1)}, bf16[64,2176]{1,0:T(8,128)(2,1)}, u32[]{:S(2)}, u32[]{:S(2)}) %collective-permute-start.2) | collective-permute-done | bytes 278560 | tf_op jit(solution)/shard_map/ppermute | solution.py:41
  44.5 9.1 %collective-permute-start.4 = (bf16[128,2048]{1,0:T(8,128)(2,1)}, bf16[128,2048]{1,0:T(8,128)(2,1)}, u32[]{:S(2)}, u32[]{:S(2)}) collective-permute-start(bf16[128,2048]{1,0:T(8,128)(2,1)} %bitcast.3), channel_id=1, source_target_pairs={{0,2},{1,3},{2,4},{3,5},{4,6},{5,7},{8,10},{9,11},{10,12},{11,13},... | collective-permute-start | bytes 1572872 | tf_op jit(solution)/shard_map/ppermute | solution.py:74
  64.6 26.6 %collective-permute-done.9 = bf16[64,2048]{1,0:T(8,128)(2,1)S(1)} collective-permute-done((bf16[64,2048]{1,0:T(8,128)(2,1)S(1)}, bf16[64,2048]{1,0:T(8,128)(2,1)S(1)}, u32[]{:S(2)}, u32[]{:S(2)}) %collective-permute-start.9) | collective-permute-done | bytes 262176 | tf_op jit(solution)/shard_map/ppermute | solution.py:163
  96.4 11.8 %collective-permute-done.11 = bf16[128,2048]{1,0:T(8,128)(2,1)} collective-permute-done((bf16[128,2048]{1,0:T(8,128)(2,1)}, bf16[128,2048]{1,0:T(8,128)(2,1)}, u32[]{:S(2)}, u32[]{:S(2)}) %collective-permute-start.11) | collective-permute-done | bytes 524320 | tf_op jit(solution)/shard_map/ppermute | solution.py:74
  108.1 8.3 %collective-permute-done.13.far_ref = bf16[2,4,64,1024]{3,2,1,0:T(8,128)(2,1)} collective-permute-done((bf16[2,4,64,1024]{3,2,1,0:T(8,128)(2,1)S(1)}, bf16[2,4,64,1024]{3,2,1,0:T(8,128)(2,1)}, u32[]{:S(2)}, u32[]{:S(2)}) %collective-permute-start.13) | collective-permute-done | bytes 1048608 | tf_op jit(solution)/shard_map/ppermute | solution.py:46
  151.1 9.7 %recurrence_forward.1 = (bf16[4,128,512]{2,1,0:T(8,128)(2,1)S(1)}, f32[4,128,512]{2,1,0:T(8,128)S(1)}, f32[4,4,128,128]{3,2,1,0:T(8,128)S(1)}) custom-call(s32[4]{0:T(128)S(1)} %and_select_fusion.1.order_ref, f32[4,128,1024]{2,1,0:T(8,128)S(1)} %bitcast.276, f32[4,128,1024]{2,1,0:T(8,128)S(1)} %fusion.69.value_ref, ...), custom_call_target="tpu_custom_call" | custom-call | flops 2684354560 | bytes 10485760 | tf_op jit(solution)/shard_map/recurrence_forward/pallas_call | solution.py:478
  180.5 9.8 %collective-permute-done.24 = bf16[4,64,1408]{2,1,0:T(8,128)(2,1)S(1)} collective-permute-done((bf16[4,64,1408]{2,1,0:T(8,128)(2,1)S(1)}, bf16[4,64,1408]{2,1,0:T(8,128)(2,1)S(1)}, u32[]{:S(2)}, u32[]{:S(2)}) %collective-permute-start.24) | collective-permute-done | bytes 720928 | tf_op jit(solution)/shard_map/ppermute | solution.py:46
  216.5 22.4 %collective-permute-done.28 = bf16[176,2048]{1,0:T(8,128)(2,1)} collective-permute-done((bf16[176,2048]{1,0:T(8,128)(2,1)S(1)}, bf16[176,2048]{1,0:T(8,128)(2,1)}, u32[]{:S(2)}, u32[]{:S(2)}) %collective-permute-start.28) | collective-permute-done | bytes 720928 | tf_op jit(solution)/shard_map/ppermute | solution.py:163
  253.0 20.2 %collective-permute-done.30 = bf16[128,2048]{1,0:T(8,128)(2,1)} collective-permute-done((bf16[128,2048]{1,0:T(8,128)(2,1)}, bf16[128,2048]{1,0:T(8,128)(2,1)}, u32[]{:S(2)}, u32[]{:S(2)}) %collective-permute-start.30) | collective-permute-done | bytes 524320 | tf_op jit(solution)/shard_map/ppermute | solution.py:74
  279.2 30.6 %collective-permute-done.35 = bf16[128,2048]{1,0:T(8,128)(2,1)} collective-permute-done((bf16[128,2048]{1,0:T(8,128)(2,1)}, bf16[128,2048]{1,0:T(8,128)(2,1)}, u32[]{:S(2)}, u32[]{:S(2)}) %collective-permute-start.35) | collective-permute-done | bytes 524320 | tf_op jit(solution)/shard_map/ppermute | solution.py:74
  317.8 6.0 assemble_rows.6
  354.3 6.5 fusion.42
  399.9 5.7 collective-permute-start.48
  416.9 5.7 convolution_convert_fusion.6
  444.5 12.2 %collective-permute-done.52 = bf16[128,2048]{1,0:T(8,128)(2,1)S(1)} collective-permute-done((bf16[128,2048]{1,0:T(8,128)(2,1)}, bf16[128,2048]{1,0:T(8,128)(2,1)S(1)}, u32[]{:S(2)}, u32[]{:S(2)}) %collective-permute-start.52) | collective-permute-done | bytes 524320 | tf_op jit(solution)/shard_map/ppermute | solution.py:80
  468.4 23.1 %collective-permute-done.57 = bf16[2,4,64,1408]{3,2,1,0:T(8,128)(2,1)} collective-permute-done((bf16[2,4,64,1408]{3,2,1,0:T(8,128)(2,1)}, bf16[2,4,64,1408]{3,2,1,0:T(8,128)(2,1)}, u32[]{:S(2)}, u32[]{:S(2)}) %collective-permute-start.57) | collective-permute-done | bytes 1441824 | tf_op jit(solution)/shard_map/ppermute | solution.py:36
  509.7 7.0 convolution_convert_fusion
  527.9 16.5 %recurrence_backward.1 = (bf16[4,128,1024]{2,1,0:T(8,128)(2,1)S(1)}, bf16[4,128,1024]{2,1,0:T(8,128)(2,1)S(1)}, f32[2,512]{1,0:T(2,128)S(1)}) custom-call(s32[4]{0:T(128)S(1)} %rev.3.order_ref, f32[4,128,1024]{2,1,0:T(8,128)S(1)} %bitcast.277, f32[4,128,1024]{2,1,0:T(8,128)S(1)} %copy-done.30, f32[1,512]{1,0:T(1,128)S(1)} %get-tuple-element.377.slack_ref, ...), custom_call_target="tpu_custom_call" | custom-call | flops 5368709120 | bytes 15728640 | tf_op jit(solution)/shard_map/recurrence_backward/pallas_call | solution.py:513
  554.7 18.6 %all-reduce.1 = f32[8,128]{1,0:T(8,128)S(1)} all-reduce(f32[8,128]{1,0:T(8,128)S(1)} %reshape.169), channel_id=2, replica_groups={{0,1,8,9,16,17,24,25},{2,3,10,11,18,19,26,27},{4,5,12,13,20,21,28,29},{..., use_global_device_ids=true, to_apply=%region_5.6.clone | all-reduce | flops 1024 | bytes 8192
  617.3 16.2 %collective-permute-done.66 = bf16[128,2048]{1,0:T(8,128)(2,1)S(1)} collective-permute-done((bf16[128,2048]{1,0:T(8,128)(2,1)S(1)}, bf16[128,2048]{1,0:T(8,128)(2,1)S(1)}, u32[]{:S(2)}, u32[]{:S(2)}) %collective-permute-start.66) | collective-permute-done | bytes 524320 | tf_op jit(solution)/shard_map/ppermute | solution.py:80
  635.6 18.0 %collective-permute-start.69 = (bf16[128,2048]{1,0:T(8,128)(2,1)S(1)}, bf16[128,2048]{1,0:T(8,128)(2,1)S(1)}, u32[]{:S(2)}, u32[]{:S(2)}) collective-permute-start(bf16[128,2048]{1,0:T(8,128)(2,1)S(1)} %add_convert_fusion.5), channel_id=1, source_target_pairs={{0,2},{1,3},{2,4},{3,5},{4,6},{5,7},{8,10},{9,11},{10,12},{11,13},... | collective-permute-start | bytes 1572872 | tf_op jit(solution)/shard_map/ppermute | solution.py:74
  658.4 9.1 %collective-permute-start.81 = (bf16[64,2816]{1,0:T(8,128)(2,1)S(1)}, bf16[64,2816]{1,0:T(8,128)(2,1)S(1)}, u32[]{:S(2)}, u32[]{:S(2)}) collective-permute-start(bf16[64,2816]{1,0:T(8,128)(2,1)S(1)} %pad_maximum_fusion.17), channel_id=1, source_target_pairs={{0,6},{1,7},{2,0},{3,1},{4,2},{5,3},{6,4},{7,5},{8,14},{9,15},{10,... | collective-permute-start | bytes 1081352 | tf_op jit(solution)/shard_map/ppermute | solution.py:41
  713.3 21.9 %collective-permute-done.85 = f32[1,128]{1,0:T(1,128)S(1)} collective-permute-done((f32[1,128]{1,0:T(1,128)}, f32[1,128]{1,0:T(1,128)S(1)}, u32[]{:S(2)}, u32[]{:S(2)}) %collective-permute-start.85) | collective-permute-done | bytes 544 | tf_op jit(solution)/shard_map/ppermute | solution.py:167
  746.5 7.3 collective-permute-done.86
  (596 shorter events, 407.4 us)
Async XLA Ops:
  7.2 155.6 %all-gather.3.cloned.1.call-start = ((), (), s32[]{:S(2)}) async-start(), calls=%async_computation.2 | async-start | bytes 2359296 | tf_op jit(solution)/shard_map/all_gather | solution.py:313
  44.5 46.7 %collective-permute-start.4 = (bf16[128,2048]{1,0:T(8,128)(2,1)}, bf16[128,2048]{1,0:T(8,128)(2,1)}, u32[]{:S(2)}, u32[]{:S(2)}) collective-permute-start(bf16[128,2048]{1,0:T(8,128)(2,1)} %bitcast.3), channel_id=1, source_target_pairs={{0,2},{1,3},{2,4},{3,5},{4,6},{5,7},{8,10},{9,11},{10,12},{11,13},... | collective-permute-start | bytes 1572872 | tf_op jit(solution)/shard_map/ppermute | solution.py:74
  53.7 37.6 %collective-permute-start.5 = (bf16[128,2048]{1,0:T(8,128)(2,1)}, bf16[128,2048]{1,0:T(8,128)(2,1)}, u32[]{:S(2)}, u32[]{:S(2)}) collective-permute-start(bf16[128,2048]{1,0:T(8,128)(2,1)} %bitcast.3), channel_id=1, source_target_pairs={{2,0},{3,1},{4,2},{5,3},{6,4},{7,5},{10,8},{11,9},{12,10},{13,11},... | collective-permute-start | bytes 1572872 | tf_op jit(solution)/shard_map/ppermute | solution.py:74
  54.9 36.3 %collective-permute-start.6 = (bf16[128,2048]{1,0:T(8,128)(2,1)}, bf16[128,2048]{1,0:T(8,128)(2,1)}, u32[]{:S(2)}, u32[]{:S(2)}) collective-permute-start(bf16[128,2048]{1,0:T(8,128)(2,1)} %bitcast.3), channel_id=1, source_target_pairs={{0,6},{1,7},{6,0},{7,1},{8,14},{9,15},{14,8},{15,9},{16,22},{17,23... | collective-permute-start | bytes 1572872 | tf_op jit(solution)/shard_map/ppermute | solution.py:80
  95.7 258.5 %all-gather.5.cloned.1.call-start = ((), (), s32[]{:S(2)}) async-start(), calls=%async_computation.3 | async-start | bytes 6488064 | tf_op jit(solution)/shard_map/all_gather | solution.py:313
  120.6 45.0 %collective-permute-start.18 = (bf16[64,2816]{1,0:T(8,128)(2,1)}, bf16[64,2816]{1,0:T(8,128)(2,1)}, u32[]{:S(2)}, u32[]{:S(2)}) collective-permute-start(bf16[64,2816]{1,0:T(8,128)(2,1)} %get-tuple-element.196), channel_id=1, source_target_pairs={{0,2},{1,3},{2,4},{3,5},{4,6},{5,7},{6,0},{7,1},{8,10},{9,11},{10,... | collective-permute-start | bytes 1081352 | tf_op jit(solution)/shard_map/ppermute | solution.py:41
  126.1 39.5 %collective-permute-start.19 = (bf16[64,2816]{1,0:T(8,128)(2,1)}, bf16[64,2816]{1,0:T(8,128)(2,1)}, u32[]{:S(2)}, u32[]{:S(2)}) collective-permute-start(bf16[64,2816]{1,0:T(8,128)(2,1)} %get-tuple-element.197), channel_id=1, source_target_pairs={{0,4},{1,5},{2,6},{3,7},{4,0},{5,1},{6,2},{7,3},{8,12},{9,13},{10,... | collective-permute-start | bytes 1081352 | tf_op jit(solution)/shard_map/ppermute | solution.py:41
  126.4 39.2 %collective-permute-start.20 = (bf16[64,2816]{1,0:T(8,128)(2,1)}, bf16[64,2816]{1,0:T(8,128)(2,1)}, u32[]{:S(2)}, u32[]{:S(2)}) collective-permute-start(bf16[64,2816]{1,0:T(8,128)(2,1)} %get-tuple-element.198), channel_id=1, source_target_pairs={{0,6},{1,7},{2,0},{3,1},{4,2},{5,3},{6,4},{7,5},{8,14},{9,15},{10,... | collective-permute-start | bytes 1081352 | tf_op jit(solution)/shard_map/ppermute | solution.py:41
  200.8 38.2 %collective-permute-start.28 = (bf16[176,2048]{1,0:T(8,128)(2,1)S(1)}, bf16[176,2048]{1,0:T(8,128)(2,1)}, u32[]{:S(2)}, u32[]{:S(2)}) collective-permute-start(bf16[176,2048]{1,0:T(8,128)(2,1)S(1)} %copy-done.107), channel_id=1, source_target_pairs={{0,0},{1,1},{2,8},{3,9},{4,16},{5,17},{6,24},{7,25},{8,2},{9,3},{1... | collective-permute-start | bytes 2162696 | tf_op jit(solution)/shard_map/ppermute | solution.py:163
  239.0 453.0 %reduce-scatter.5.cloned.1.call-start = ((), (), s32[]{:S(2)}) async-start(), calls=%async_computation.5 | async-start | bytes 2359296 | tf_op jit(solution)/shard_map/reduce_scatter | solution.py:317
  273.4 36.5 %collective-permute-start.37 = (bf16[2,4,64,1408]{3,2,1,0:T(8,128)(2,1)}, bf16[2,4,64,1408]{3,2,1,0:T(8,128)(2,1)}, u32[]{:S(2)}, u32[]{:S(2)}) collective-permute-start(bf16[2,4,64,1408]{3,2,1,0:T(8,128)(2,1)} %collective-permute-done.32.far_ref), channel_id=1, source_target_pairs={{0,8},{8,0},{16,24},{24,16},{1,9},{9,1},{17,25},{25,17},{2,10},{10... | collective-permute-start | bytes 4325384 | tf_op jit(solution)/shard_map/ppermute | solution.py:46
  273.8 36.0 %collective-permute-start.39 = (bf16[2,4,64,1408]{3,2,1,0:T(8,128)(2,1)}, bf16[2,4,64,1408]{3,2,1,0:T(8,128)(2,1)}, u32[]{:S(2)}, u32[]{:S(2)}) collective-permute-start(bf16[2,4,64,1408]{3,2,1,0:T(8,128)(2,1)} %collective-permute-done.33.far_ref), channel_id=1, source_target_pairs={{0,8},{8,0},{16,24},{24,16},{1,9},{9,1},{17,25},{25,17},{2,10},{10... | collective-permute-start | bytes 4325384 | tf_op jit(solution)/shard_map/ppermute | solution.py:46
  500.6 191.4 %reduce-scatter.3.cloned.1.call-start = ((), (), s32[]{:S(2)}) async-start(), calls=%async_computation.4 | async-start | bytes 6488064 | tf_op jit(solution)/shard_map/reduce_scatter | solution.py:317
  516.7 61.1 %collective-permute-start.59 = (bf16[128,2048]{1,0:T(8,128)(2,1)}, bf16[128,2048]{1,0:T(8,128)(2,1)}, u32[]{:S(2)}, u32[]{:S(2)}) collective-permute-start(bf16[128,2048]{1,0:T(8,128)(2,1)} %get-tuple-element.260), channel_id=1, source_target_pairs={{0,2},{1,3},{2,4},{3,5},{8,10},{9,11},{10,12},{11,13},{16,18},{17,... | collective-permute-start | bytes 1572872 | tf_op jit(solution)/shard_map/ppermute | solution.py:74
  518.9 58.8 %collective-permute-start.60 = (bf16[128,2048]{1,0:T(8,128)(2,1)}, bf16[128,2048]{1,0:T(8,128)(2,1)}, u32[]{:S(2)}, u32[]{:S(2)}) collective-permute-start(bf16[128,2048]{1,0:T(8,128)(2,1)} %get-tuple-element.260), channel_id=1, source_target_pairs={{4,2},{5,3},{6,4},{7,5},{12,10},{13,11},{14,12},{15,13},{20,18},{2... | collective-permute-start | bytes 1572872 | tf_op jit(solution)/shard_map/ppermute | solution.py:74
  521.3 56.5 %collective-permute-start.61 = (bf16[128,2048]{1,0:T(8,128)(2,1)}, bf16[128,2048]{1,0:T(8,128)(2,1)}, u32[]{:S(2)}, u32[]{:S(2)}) collective-permute-start(bf16[128,2048]{1,0:T(8,128)(2,1)} %broadcast_select_fusion.9), channel_id=1, source_target_pairs={{0,6},{1,7},{6,0},{7,1},{8,14},{9,15},{14,8},{15,9},{16,22},{17,23... | collective-permute-start | bytes 1572872 | tf_op jit(solution)/shard_map/ppermute | solution.py:80
  577.8 39.5 %collective-permute-start.64 = (bf16[128,2048]{1,0:T(8,128)(2,1)}, bf16[128,2048]{1,0:T(8,128)(2,1)S(1)}, u32[]{:S(2)}, u32[]{:S(2)}) collective-permute-start(bf16[128,2048]{1,0:T(8,128)(2,1)} %get-tuple-element.266), channel_id=1, source_target_pairs={{0,2},{1,3},{2,4},{3,5},{8,10},{9,11},{10,12},{11,13},{16,18},{17,... | collective-permute-start | bytes 1572872 | tf_op jit(solution)/shard_map/ppermute | solution.py:74
  613.5 78.4 %collective-permute-start.79 = (bf16[64,2816]{1,0:T(8,128)(2,1)S(1)}, bf16[64,2816]{1,0:T(8,128)(2,1)S(1)}, u32[]{:S(2)}, u32[]{:S(2)}) collective-permute-start(bf16[64,2816]{1,0:T(8,128)(2,1)S(1)} %pad_maximum_fusion.15), channel_id=1, source_target_pairs={{0,2},{1,3},{2,4},{3,5},{4,6},{5,7},{6,0},{7,1},{8,10},{9,11},{10,... | collective-permute-start | bytes 1081352 | tf_op jit(solution)/shard_map/ppermute | solution.py:41
  614.6 77.3 %collective-permute-start.80 = (bf16[64,2816]{1,0:T(8,128)(2,1)S(1)}, bf16[64,2816]{1,0:T(8,128)(2,1)S(1)}, u32[]{:S(2)}, u32[]{:S(2)}) collective-permute-start(bf16[64,2816]{1,0:T(8,128)(2,1)S(1)} %pad_maximum_fusion.16), channel_id=1, source_target_pairs={{0,4},{1,5},{2,6},{3,7},{4,0},{5,1},{6,2},{7,3},{8,12},{9,13},{10,... | collective-permute-start | bytes 1081352 | tf_op jit(solution)/shard_map/ppermute | solution.py:41
  689.9 50.6 %collective-permute-start.77 = (f32[1,64,2048]{2,1,0:T(8,128)}, f32[1,64,2048]{2,1,0:T(8,128)}, u32[]{:S(2)}, u32[]{:S(2)}) collective-permute-start(f32[1,64,2048]{2,1,0:T(8,128)} %dynamic-slice_bitcast_fusion.9), channel_id=1, source_target_pairs={{0,1},{1,0},{2,3},{3,2},{4,5},{5,4},{6,7},{7,6},{8,9},{9,8},{10,11... | collective-permute-start | bytes 1572872 | tf_op jit(solution)/shard_map/ppermute | solution.py:36
  693.9 41.8 %collective-permute-start.82 = (bf16[64,2048]{1,0:T(8,128)(2,1)}, bf16[64,2048]{1,0:T(8,128)(2,1)S(1)}, u32[]{:S(2)}, u32[]{:S(2)}) collective-permute-start(bf16[64,2048]{1,0:T(8,128)(2,1)} %pad_maximum_fusion.23), channel_id=1, source_target_pairs={{0,2},{1,3},{2,4},{3,5},{4,6},{5,7},{6,0},{7,1},{8,10},{9,11},{10,... | collective-permute-start | bytes 786440 | tf_op jit(solution)/shard_map/ppermute | solution.py:41
  694.7 43.0 %collective-permute-start.83 = (bf16[64,2048]{1,0:T(8,128)(2,1)}, bf16[64,2048]{1,0:T(8,128)(2,1)S(1)}, u32[]{:S(2)}, u32[]{:S(2)}) collective-permute-start(bf16[64,2048]{1,0:T(8,128)(2,1)} %pad_maximum_fusion.24), channel_id=1, source_target_pairs={{0,4},{1,5},{2,6},{3,7},{4,0},{5,1},{6,2},{7,3},{8,12},{9,13},{10,... | collective-permute-start | bytes 786440 | tf_op jit(solution)/shard_map/ppermute | solution.py:41
  695.4 42.3 %collective-permute-start.84 = (bf16[64,2048]{1,0:T(8,128)(2,1)}, bf16[64,2048]{1,0:T(8,128)(2,1)S(1)}, u32[]{:S(2)}, u32[]{:S(2)}) collective-permute-start(bf16[64,2048]{1,0:T(8,128)(2,1)} %pad_maximum_fusion.25), channel_id=1, source_target_pairs={{0,6},{1,7},{2,0},{3,1},{4,2},{5,3},{6,4},{7,5},{8,14},{9,15},{10,... | collective-permute-start | bytes 786440 | tf_op jit(solution)/shard_map/ppermute | solution.py:41
  699.2 36.0 %collective-permute-start.85 = (f32[1,128]{1,0:T(1,128)}, f32[1,128]{1,0:T(1,128)S(1)}, u32[]{:S(2)}, u32[]{:S(2)}) collective-permute-start(f32[1,128]{1,0:T(1,128)} %constant_dynamic-slice_fusion.4), channel_id=1, source_target_pairs={{0,0},{1,1},{8,2},{9,3},{16,4},{17,5},{24,6},{25,7},{2,8},{3,9},{1... | collective-permute-start | bytes 1544 | tf_op jit(solution)/shard_map/ppermute | solution.py:167
  (191 other events, 2925.3 us)
Sparse Core Ops, SparseCore 0:
  95.9 31.1 all-gather.2
  239.1 51.8 all-gather.4
  500.7 39.5 reduce-scatter.4
  543.9 59.1 reduce-scatter.2

commit v2 on v1

--- a/solution.py
+++ b/solution.py
@@ -9,6 +9,7 @@
 
 HEAD = 128
 LANES = 128
+VMEM_BYTES = 56 * 1024 * 1024
 HIGHEST = lax.Precision.HIGHEST
 NN = (((1,), (0,)), ((), ()))
 NT = (((1,), (1,)), ((), ()))
@@ -60,11 +61,13 @@
     return [rows.reshape((-1,) + rows.shape[2:]) for rows in both]
 
 
-def from_side(rows):
+def from_side(*arrays):
     here = side()
-    halves = rows.reshape((2, 1, rows.shape[0] // 2) + rows.shape[1:])
-    got = swapped(pick(halves, 1 - here))
-    return placed([(here, pick(halves, here)), (1 - here, got)])
+    halves = [rows.reshape((2, 1, rows.shape[0] // 2) + rows.shape[1:]) for rows in arrays]
+    got = swapped(jnp.concatenate([pick(half, 1 - here) for half in halves], axis=0))
+    return [
+        placed([(here, pick(half, here)), (1 - here, piece[None])]) for half, piece in zip(halves, got)
+    ]
 
 
 def shifted(array, step, among=None):
@@ -80,14 +83,18 @@
     return lax.ppermute(array, "fsdp", moves)
 
 
-def gather_first(own):
-    if ranks() != 4:
+def gather_first(own, relay=True):
+    if ranks() != 4 or not relay:
         return [turned(own, turn) for turn in range(1, ranks())]
     return [shifted(own, 1), shifted(own, -1), ends_traded(own)]
 
 
 def gather_second(first):
     return [] if ranks() != 4 else [shifted(first[0], 1, (1, 2)), shifted(first[1], -1, (1, 2))]
+
+
+def gathered_directly(own, pieces):
+    return jnp.concatenate([own] + pieces, axis=0)
 
 
 def gathered(own, first, second):
@@ -167,112 +174,168 @@
     return lax.ppermute(rows, ("dp", "fsdp"), [(b, a) for a, b in user_moves()])
 
 
-def cut_kernel(order_ref, *refs):
+def for_rank(wanted, body, aligned):
+    if aligned:
+        body(wanted)
+        return
+    for number in range(ranks()):
+        pl.when(wanted == number)(functools.partial(body, number))
+
+
+def columns_of(number, chunk, weight, chunks, count):
+    width = weight.shape[1] // (chunks * count)
+    start = chunk * (weight.shape[1] // chunks) + number * width
+    return pl.ds(start if isinstance(number, int) else pl.multiple_of(start, LANES), width)
+
+
+def cut_kernel(order_ref, *refs, chunks):
     count = order_ref.shape[0]
     weights, pieces = refs[:-count], refs[-count:]
     for turn in range(count):
-        start = 0
-        for weight in weights:
-            width = weight.shape[1] // (1 if weight.shape[1] == LANES else count)
-            column = 0
-            if weight.shape[1] != LANES:
-                column = pl.multiple_of(order_ref[turn] * width, LANES)
-            pieces[turn][:, start : start + width] = weight[:, pl.ds(column, width)]
-            start += width
-
-
-def cut_columns(order, *weights):
+
+        def cut(number, turn=turn):
+            start = 0
+            for weight in weights:
+                if weight.shape[1] == LANES:
+                    pieces[turn][:, start : start + LANES] = weight[...]
+                    start += LANES
+                    continue
+                for chunk in range(chunks):
+                    columns = columns_of(number, chunk, weight, chunks, count)
+                    pieces[turn][:, start : start + columns.size] = weight[:, columns]
+                    start += columns.size
+
+        widths = [w.shape[1] // (chunks * count) for w in weights if w.shape[1] != LANES]
+        for_rank(order_ref[turn], cut, all(width % LANES == 0 for width in widths))
+
+
+def cut_columns(order, weights, chunks):
     count = ranks()
     rows = weights[0].shape[0]
     vmem = pl.BlockSpec(memory_space=pltpu.VMEM)
     width = sum(LANES if w.shape[1] == LANES else w.shape[1] // count for w in weights)
     return pl.pallas_call(
-        cut_kernel,
+        functools.partial(cut_kernel, chunks=chunks),
         in_specs=[pl.BlockSpec(memory_space=pltpu.SMEM)] + [vmem] * len(weights),
         out_specs=[vmem] * count,
         out_shape=[jax.ShapeDtypeStruct((rows, width), weights[0].dtype)] * count,
-        compiler_params=pltpu.CompilerParams(vmem_limit_bytes=24 * 1024 * 1024),
+        compiler_params=pltpu.CompilerParams(vmem_limit_bytes=VMEM_BYTES),
         name="cut_columns",
     )(order, *weights)
 
 
-def join_kernel(order_ref, *refs):
+def join_kernel(order_ref, *refs, chunks):
     count = order_ref.shape[0]
     parts = (len(refs) - count - 1) // 2
     pieces, weights = refs[:count], refs[count : count + parts]
     grads, product = refs[count + parts : -1], refs[-1]
-    total = jnp.zeros(product.shape, jnp.float32)
+    product[...] = jnp.zeros(product.shape, jnp.float32)
     for turn in range(count):
-        start = 0
-        for weight, grad in zip(weights, grads):
-            width = weight.shape[1] // count
-            columns = pl.ds(pl.multiple_of(order_ref[turn] * width, LANES), width)
-            piece = pieces[turn][:, start : start + width].astype(jnp.float32)
-            grad[:, columns] = piece
-            term = piece * weight[:, columns].astype(jnp.float32)
-            total = total + jnp.sum(term, axis=1, keepdims=True)
-            start += width
-    product[...] = total
-
-
-def join_columns(order, pieces, weights):
+
+        def join(number, turn=turn):
+            start = 0
+            total = jnp.zeros(product.shape, jnp.float32)
+            for weight, grad in zip(weights, grads):
+                for chunk in range(chunks):
+                    columns = columns_of(number, chunk, weight, chunks, count)
+                    piece = pieces[turn][:, start : start + columns.size].astype(jnp.float32)
+                    grad[:, columns] = piece
+                    term = piece * weight[:, columns].astype(jnp.float32)
+                    total = total + jnp.sum(term, axis=1, keepdims=True)
+                    start += columns.size
+            product[...] += total
+
+        widths = [w.shape[1] // (chunks * count) for w in weights]
+        for_rank(order_ref[turn], join, all(width % LANES == 0 for width in widths))
+
+
+def join_columns(order, pieces, weights, chunks):
     rows = weights[0].shape[0]
     vmem = pl.BlockSpec(memory_space=pltpu.VMEM)
     *grads, product = pl.pallas_call(
-        join_kernel,
+        functools.partial(join_kernel, chunks=chunks),
         in_specs=[pl.BlockSpec(memory_space=pltpu.SMEM)] + [vmem] * (len(pieces) + len(weights)),
         out_specs=[vmem] * (len(weights) + 1),
         out_shape=[jax.ShapeDtypeStruct(w.shape, jnp.float32) for w in weights]
         + [jax.ShapeDtypeStruct((rows, 1), jnp.float32)],
-        compiler_params=pltpu.CompilerParams(vmem_limit_bytes=32 * 1024 * 1024),
+        compiler_params=pltpu.CompilerParams(vmem_limit_bytes=VMEM_BYTES),
+        cost_estimate=pl.CostEstimate(
+            flops=0, bytes_accessed=40 * sum(w.size for w in weights), transcendentals=0
+        ),
         name="join_columns",
     )(order, *pieces, *weights)
     return grads, product[:, 0]
 
 
-def assemble_kernel(place_ref, near_ref, far_ref, near_core_ref, far_core_ref, whole_ref, sems, *, marks):
-    count = near_ref.shape[1]
+def assemble_kernel(place_ref, *refs, marks):
+    (*blocks, sems), wholes = refs[:4] + refs[-1:], refs[4:-1]
+    count = blocks[0].shape[1]
     dp_index, here, first_rank = place_ref[0], place_ref[1], place_ref[2]
     copies = []
-    for blocks, refs in ((0, (near_ref, far_ref)), (1, (near_core_ref, far_core_ref))):
+    for core in range(2):
         for outer in range(2):
+            block = blocks[2 * core + outer]
             for inner in range(2):
                 dp_mark, side_mark = marks[outer][inner]
-                spot = jnp.bitwise_xor(dp_index, dp_mark + blocks)
+                spot = jnp.bitwise_xor(dp_index, dp_mark + core)
                 its_side = jnp.bitwise_xor(here, side_mark)
                 for turn in range(count):
                     its_rank = lax.rem(first_rank - turn + count, count)
-                    copies.append(
-                        pltpu.make_async_copy(
-                            refs[outer].at[inner, turn],
-                            whole_ref.at[spot, its_rank, its_side],
-                            sems.at[len(copies)],
-                        )
-                    )
-                    copies[-1].start()
+                    start = 0
+                    for whole in wholes:
+                        columns = whole.shape[-1]
+                        source = block.at[inner, turn, :, pl.ds(start, columns)]
+                        target = whole.at[spot, its_rank, its_side]
+                        copies.append(pltpu.make_async_copy(source, target, sems.at[len(copies)]))
+                        copies[-1].start()
+                        start += columns
     for copy in copies:
         copy.wait()
 
 
-def assembled(near, far, near_core, far_core, side_first):
-    dp, (_, count, rows, columns) = lax.axis_size("dp"), near.shape
+def assembled(near, far, near_core, far_core, side_first, widths):
+    dp, (_, count, rows, _) = lax.axis_size("dp"), near.shape
     big = dp // 2
     marks = (((0, 0), (0, 1)), ((big, 0), (big, 1))) if side_first else (((0, 0), (big, 0)), ((0, 1), (big, 1)))
     place = jnp.stack([lax.axis_index("dp"), side(), rank()]).astype(jnp.int32)
     anywhere = pl.BlockSpec(memory_space=pl.ANY)
-    whole = pl.pallas_call(
+    wholes = pl.pallas_call(
         functools.partial(assemble_kernel, marks=marks),
         in_specs=[pl.BlockSpec(memory_space=pltpu.SMEM)] + [anywhere] * 4,
-        out_specs=pl.BlockSpec(memory_space=pltpu.VMEM),
-        out_shape=jax.ShapeDtypeStruct((dp, count, 2, rows, columns), near.dtype),
-        scratch_shapes=[pltpu.SemaphoreType.DMA((8 * count,))],
-        compiler_params=pltpu.CompilerParams(vmem_limit_bytes=24 * 1024 * 1024),
-        cost_estimate=pl.CostEstimate(
-            flops=0, bytes_accessed=32 * near.size, transcendentals=0
-        ),
+        out_specs=[pl.BlockSpec(memory_space=pltpu.VMEM)] * len(widths),
+        out_shape=[
+            jax.ShapeDtypeStruct((dp, count, 2, rows, columns), near.dtype) for columns in widths
+        ],
+        scratch_shapes=[pltpu.SemaphoreType.DMA((8 * count * len(widths),))],
+        compiler_params=pltpu.CompilerParams(vmem_limit_bytes=VMEM_BYTES),
+        cost_estimate=pl.CostEstimate(flops=0, bytes_accessed=64 * near.size, transcendentals=0),
         name="assemble_rows",
     )(place, near, far, near_core, far_core)
-    return whole.reshape(-1, columns)
+    return [whole.reshape(-1, whole.shape[-1]) for whole in wholes]
+
+
+def halves_kernel(*refs):
+    *pieces, first, second = refs
+    split = first.shape[2]
+    for turn, piece in enumerate(pieces):
+        first[turn] = piece[:, :split]
+        second[turn] = piece[:, split:]
+
+
+def halves(pieces, split):
+    count, (rows, width) = len(pieces), pieces[0].shape
+    vmem = pl.BlockSpec(memory_space=pltpu.VMEM)
+    return pl.pallas_call(
+        halves_kernel,
+        in_specs=[vmem] * count,
+        out_specs=[vmem] * 2,
+        out_shape=[
+            jax.ShapeDtypeStruct((count, rows, columns), pieces[0].dtype)
+            for columns in (split, width - split)
+        ],
+        compiler_params=pltpu.CompilerParams(vmem_limit_bytes=VMEM_BYTES),
+        name="stack_halves",
+    )(*pieces)
 
 
 def traded(pieces):
@@ -283,11 +346,37 @@
     return (rank() + step * jnp.arange(ranks(), dtype=jnp.int32) + ranks()) % ranks()
 
 
-def term_blocks(term):
+def split_kernel(core_ref, rows_ref, own_ref, other_ref, *, block):
+    for number in range(own_ref.shape[1] // block):
+        there = slice(number * block, (number + 1) * block)
+        for index, half_ref in ((core_ref[0], own_ref), (1 - core_ref[0], other_ref)):
+            column = pl.multiple_of((2 * number + index) * block, block)
+            half_ref[:, there] = rows_ref[:, pl.ds(column, block)]
+
+
+def core_halves(rows):
+    dp, (tokens, width) = lax.axis_size("dp"), rows.shape
+    own = (lax.axis_index("dp") % 2).astype(jnp.int32).reshape(1)
+    vmem = pl.BlockSpec(memory_space=pltpu.VMEM)
+    return pl.pallas_call(
+        functools.partial(split_kernel, block=width // dp),
+        in_specs=[pl.BlockSpec(memory_space=pltpu.SMEM), vmem],
+        out_specs=[vmem] * 2,
+        out_shape=[jax.ShapeDtypeStruct((tokens, width // 2), rows.dtype)] * 2,
+        compiler_params=pltpu.CompilerParams(vmem_limit_bytes=VMEM_BYTES),
+        name="core_halves",
+    )(own, rows)
+
+
+def core_given(rows, grads):
+    return outer_sum(rows[1], grads).astype(jnp.bfloat16)
+
+
+def core_sum(rows, grads, got):
     dp, count = lax.axis_size("dp"), ranks()
-    bits = len(dp_bits())
-    term = term.reshape((2,) * bits + (count, 2, term.shape[0] // (2 * dp * count), term.shape[-1]))
-    return jnp.moveaxis(term, bits + 1, bits)
+    total = (outer_sum(rows[0], grads) + got.astype(jnp.float32)).astype(jnp.bfloat16)
+    shape = (2,) * (len(dp_bits()) - 1) + (count, 2, total.shape[0] // (dp * count), total.shape[1])
+    return total.reshape(shape)
 
 
 def shrunk(state, route):
@@ -301,7 +390,16 @@
 
 
 def block_marks():
-    return [(bit, 0) for bit in reversed(dp_bits())] + [(0, 1)]
+    return [(bit, 0) for bit in reversed(dp_bits()[1:])] + [None, (0, 1)]
+
+
+def rank_groups():
+    count = lax.axis_size("fsdp")
+    return [list(range(here, count, 2)) for here in range(2)]
+
+
+def reordered(blocks):
+    return [pick(blocks, (rank() - number + ranks()) % ranks()) for number in range(ranks())]
 
 
 def peers():
@@ -498,9 +596,9 @@
             jax.ShapeDtypeStruct((blocks, span, share), jnp.float32),
             jax.ShapeDtypeStruct((blocks, heads, HEAD, HEAD), jnp.float32),
         ],
-        compiler_params=pltpu.CompilerParams(vmem_limit_bytes=24 * 1024 * 1024),
+        compiler_params=pltpu.CompilerParams(vmem_limit_bytes=VMEM_BYTES),
         cost_estimate=pl.CostEstimate(
-            flops=40 * queries.size * span, bytes_accessed=20 * queries.size, transcendentals=2 * queries.size
+            flops=150 * queries.size * span, bytes_accessed=20 * queries.size, transcendentals=0
         ),
         name="recurrence_forward",
     )(order, queries, values, slack, gain)
@@ -539,9 +637,9 @@
             jax.ShapeDtypeStruct((blocks, span, columns), jnp.bfloat16),
             jax.ShapeDtypeStruct((2, share), jnp.float32),
         ],
-        compiler_params=pltpu.CompilerParams(vmem_limit_bytes=32 * 1024 * 1024),
+        compiler_params=pltpu.CompilerParams(vmem_limit_bytes=VMEM_BYTES),
         cost_estimate=pl.CostEstimate(
-            flops=80 * queries.size * span, bytes_accessed=30 * queries.size, transcendentals=2 * queries.size
+            flops=250 * queries.size * span, bytes_accessed=30 * queries.size, transcendentals=0
         ),
         name="recurrence_backward",
     )(order, queries, values, slack, gain, mixed, states, d_unit)
@@ -578,95 +676,105 @@
     mixer_weights = (w_query, w_forget, w_input, w_gate_out)
     ffn_weights = (w_gate, w_up)
     core, big = 1, dp // 2
+    in_place = 2 * w_out.shape[0] == HEAD
+    chunks = dp if in_place else 1
+
+    def to_rank(rows):
+        return rows if in_place else to_users(rows)
+
+    def from_rank(rows):
+        return rows if in_place else to_owners(rows)
 
     gains = jnp.stack([norm_gain, ffn_gain, mixer_gain, slack], axis=1)
     gains = jnp.pad(gains, ((0, 0), (0, LANES - gains.shape[1])))
-    cut = traded(cut_columns(sending, w_query, w_forget, gains, w_input, w_gate_out))
-    users_out = to_users(w_out)
+    cut = traded(cut_columns(sending, (w_query, w_forget, gains, w_input, w_gate_out), chunks))
     own_in, own_d = to_side(inputs, cotangent)
+    mixer_out = peers_gather(to_rank(w_out))
     own_in, own_d, cut = sync(own_in, own_d, cut)
 
+    by_big, by_side = ((big, 0), functools.partial(across, bit=big)), ((0, 1), swapped)
     first_in = gather_first(own_in)
     split = 2 * (width // count) + LANES
-    query_cut = jnp.stack([piece[:, :split] for piece in cut])
-    value_cut = jnp.stack([piece[:, split:] for piece in cut])
+    query_cut, value_cut = halves(cut, split)
     query_near = jnp.stack([query_cut, across(query_cut, big)])
     value_near = jnp.stack([value_cut, swapped(value_cut)])
-    first_in, query_near, value_near, users_out = sync(first_in, query_near, value_near, users_out)
+    cut = cut_columns(sending, (w_gate, w_up), chunks)
+    first_in, query_near, value_near, own_d, cut, mixer_out = sync(
+        first_in, query_near, value_near, own_d, cut, mixer_out
+    )
 
     second_in = gather_second(first_in)
     query_far = swapped(query_near)
     value_far = across(value_near, big)
-    mixer_out = peers_gather(users_out)
-    second_in, query_far, value_far, late_gate, late_up, late_down = sync(
-        second_in, query_far, value_far, w_gate, w_up, w_down
+    waiting = list(cut[1:])
+    cut = [cut[0], turned(waiting[0], 1)]
+    second_in, query_far, value_far, cut, waiting, own_d = sync(
+        second_in, query_far, value_far, cut, waiting, own_d
     )
 
     query_blocks = (query_near, query_far, across(query_near, core), across(query_far, core))
     value_blocks = (value_near, value_far, across(value_near, core), across(value_far, core))
     raw_in = gathered(own_in, first_in, second_in)
-    raw_in, query_blocks, value_blocks = sync(raw_in, query_blocks, value_blocks)
-
-    cut = traded(cut_columns(sending, late_gate, late_up))
-    query_in = assembled(*query_blocks, False)
-    value_in = assembled(*value_blocks, True)
-    share = value_in.shape[-1]
-    gains = jnp.transpose(query_in[:, share:])[:4].astype(float32)
+    raw_in, query_blocks, value_blocks, cut, waiting, own_d, late_down = sync(
+        raw_in, query_blocks, value_blocks, cut, waiting, own_d, w_down
+    )
+
+    down = peers_gather(to_rank(late_down))
+    for turn in range(2, count):
+        cut = cut + [turned(waiting[turn - 1], turn)]
+    share = 2 * (width // count)
+    query_in, gains = assembled(*query_blocks, False, (share, LANES))
+    (value_in,) = assembled(*value_blocks, True, (share,))
+    gains = jnp.transpose(gains)[:4].astype(float32)
     gain_first, gain_second = gains[0], gains[1]
-    here_gains = lax.dynamic_slice(gains, (2, here * (width // count)), (2, width // count))
+    here_gains = pick(gains.reshape(4, chunks, count, -1), here, 2).reshape(4, -1)[2:]
     mixer_gain_here, slack_here = here_gains[:1], here_gains[1:]
-    query_in = query_in[:, :share]
-
     all_tokens = raw_in.astype(float32)
     rows_in = (all_tokens * inverse_rms(all_tokens) * gain_first).astype(bfloat16)
     queries = matmul(rows_in, query_in).reshape(count, -1, share)
     values = matmul(rows_in, value_in).reshape(count, -1, share)
+    queries, values, cut = sync(queries, values, cut)
+
+    units = cut[0].shape[-1] // 2
+    gate_cut, up_cut = halves(cut, units)
+    gate_near, up_near = across(gate_cut, big), swapped(up_cut)
     unit, mixed, states = run_forward(taking, queries, values, slack_here, mixer_gain_here)
+    unit, mixed, states, gate_near, up_near = sync(unit, mixed, states, gate_near, up_near)
+    gate_near, up_near = jnp.stack([gate_cut, gate_near]), jnp.stack([up_cut, up_near])
     rows_unit = unit.reshape(-1, unit.shape[-1])
     branch_terms = by_turn(matmul(away_rows(rows_unit), mixer_out))
-    branch_terms, cut, late_down = sync(branch_terms, cut, late_down)
+    branch_terms, gate_near, up_near, own_d = sync(branch_terms, gate_near, up_near, own_d)
 
     branch_first = scatter_first(branch_terms)
     branch_own = matmul(own_rows(rows_unit), mixer_out)
-    units = cut[0].shape[-1] // 2
-    gate_cut = jnp.stack([piece[:, :units] for piece in cut])
-    up_cut = jnp.stack([piece[:, units:] for piece in cut])
-    gate_near = jnp.stack([gate_cut, across(gate_cut, big)])
-    up_near = jnp.stack([up_cut, swapped(up_cut)])
-    branch_first, branch_own, gate_near, up_near = sync(branch_first, branch_own, gate_near, up_near)
-
-    branch_second = scatter_second(branch_terms, branch_first)
     gate_far = swapped(gate_near)
     up_far = across(up_near, big)
-    users_down = to_users(late_down)
+    rows_d = lax.all_gather(own_d, "fsdp", axis_index_groups=rank_groups())
+    branch_first, branch_own, gate_near, up_near, gate_far, up_far, branch_terms = sync(
+        branch_first, branch_own, gate_near, up_near, gate_far, up_far, branch_terms
+    )
+
+    branch_second = scatter_second(branch_terms, branch_first)
+    gate_blocks = (gate_near, gate_far, across(gate_near, core))
+    up_blocks = (up_near, up_far, across(up_near, core))
     tokens = own_in.astype(float32)
     hidden = tokens + scattered(branch_own, branch_first, branch_second)
     second_inverse = inverse_rms(hidden)
     hidden_hat = hidden * second_inverse
     own_mid = (hidden_hat * gain_second).astype(bfloat16)
-    own_mid, users_down = sync(own_mid, users_down)
-
-    first_mid = gather_first(own_mid)
-    down = peers_gather(users_down)
-    first_mid, gate_far, up_far = sync(first_mid, gate_far, up_far)
-
-    second_mid = gather_second(first_mid)
-    gate_blocks = (gate_near, gate_far, across(gate_near, core), across(gate_far, core))
-    up_blocks = (up_near, up_far, across(up_near, core), across(up_far, core))
-    second_mid, gate_blocks, up_blocks, late_d = sync(second_mid, gate_blocks, up_blocks, own_d)
-
-    first_d = gather_first(late_d)
-    rows_mid = gathered(own_mid, first_mid, second_mid)
-    gate_in = assembled(*gate_blocks, False)
+    own_mid, gate_blocks, up_blocks, down = sync(own_mid, gate_blocks, up_blocks, down)
+
+    all_mid = gather_first(own_mid, False)
+    gate_blocks = gate_blocks + (across(gate_blocks[1], core),)
+    up_blocks = up_blocks + (across(up_blocks[1], core),)
+    (gate_in,) = assembled(*gate_blocks, False, (units,))
+    (up_in,) = assembled(*up_blocks, True, (units,))
+    all_mid, rows_d, gate_in, up_in = sync(all_mid, rows_d, gate_in, up_in)
+
+    rows_mid = gathered_directly(own_mid, all_mid)
     gate_proj = matmul(rows_mid, gate_in)
-    first_d, gate_proj = sync(first_d, gate_proj)
-
-    second_d = gather_second(first_d)
-    up_in = assembled(*up_blocks, True)
     up_proj = matmul(rows_mid, up_in)
-    second_d, up_proj = sync(second_d, up_proj)
-
-    rows_d = gathered(own_d, first_d, second_d)
+    rows_d = jnp.concatenate(reordered(rows_d), axis=0)
     sig = jax.nn.sigmoid(gate_proj)
     inner = (gate_proj * sig * up_proj).astype(bfloat16)
     d_inner = back_product(rows_d, down)
@@ -677,48 +785,57 @@
         return back_product(cut(d_gate), gate_in) + back_product(cut(d_up), up_in)
 
     mid_terms = by_turn(hidden_product(away_rows))
-    mid_terms, d_gate, d_up = sync(mid_terms, d_gate, d_up)
+    mid_terms, d_gate, d_up, inner = sync(mid_terms, d_gate, d_up, inner)
 
     mid_first = scatter_first(mid_terms)
     mid_own = hidden_product(own_rows)
-    gate_term = term_blocks(outer_sum(rows_mid, d_gate).astype(bfloat16))
-    mid_first, mid_own, gate_term = sync(mid_first, mid_own, gate_term)
+    halves_mid = core_halves(rows_mid)
+    gate_given, up_given = core_given(halves_mid, d_gate), core_given(halves_mid, d_up)
+    mid_first, mid_own, mid_terms, halves_mid, inner, gate_given, up_given = sync(
+        mid_first, mid_own, mid_terms, halves_mid, inner, gate_given, up_given
+    )
 
     mid_second = scatter_second(mid_terms, mid_first)
-    up_term = term_blocks(outer_sum(rows_mid, d_up).astype(bfloat16))
+    gate_got, up_got = across(gate_given, core), across(up_given, core)
+    marks = block_marks()
     d_hidden = own_d.astype(float32) + unscaled_grad(
         scattered(mid_own, mid_first, mid_second) * gain_second, hidden_hat, second_inverse
     )
-    own_branch = d_hidden.astype(bfloat16)
-    own_branch, up_term = sync(own_branch, up_term)
-
-    first_branch = gather_first(own_branch)
-    gate_state = shrunk((gate_term, block_marks()), ((core, 0), functools.partial(across, bit=core)))
-    up_state = shrunk((up_term, block_marks()), ((core, 0), functools.partial(across, bit=core)))
-    out_terms = by_turn(matmul(away_rows(inner), down))
-    down_sum = peers_scatter(outer_sum(inner, rows_d).astype(bfloat16))
-    first_branch, gate_total, up_total, out_terms = sync(
-        first_branch, gate_state[0], up_state[0], out_terms
-    )
-
-    by_big, by_side = ((big, 0), functools.partial(across, bit=big)), ((0, 1), swapped)
-    second_branch = gather_second(first_branch)
-    gate_state = shrunk((gate_total, gate_state[1]), by_side)
-    up_state = shrunk((up_total, up_state[1]), by_big)
-    out_own = matmul(own_rows(inner), down)
-    second_branch, out_own, gate_total, up_total = sync(
-        second_branch, out_own, gate_state[0], up_state[0]
-    )
-
-    out_first = scatter_first(out_terms)
-    gate_state = shrunk((gate_total, gate_state[1]), by_big)
-    up_state = shrunk((up_total, up_state[1]), by_side)
-    rows_branch = gathered(own_branch, first_branch, second_branch)
+    own_branch, gate_got, up_got, inner, halves_mid = sync(
+        d_hidden.astype(bfloat16), gate_got, up_got, inner, halves_mid
+    )
+
+    all_branch = gather_first(own_branch, False)
+    gate_total = core_sum(halves_mid, d_gate, gate_got)
+    up_total = core_sum(halves_mid, d_up, up_got)
+    gate_total, gate_marks = shrunk((gate_total, marks), by_side)
+    up_total, up_marks = shrunk((up_total, marks), by_big)
+    out_part = matmul(inner, down).astype(bfloat16).reshape(count, -1, width)
+    out_part = jnp.stack(reordered(out_part))
+    down_term = outer_sum(inner, rows_d).astype(bfloat16)
+    halves_in = core_halves(rows_in)
+    all_branch, gate_total, up_total, out_part, halves_in, down_term = sync(
+        all_branch, gate_total, up_total, out_part, halves_in, down_term
+    )
+
+    out_part = lax.psum_scatter(
+        out_part, "fsdp", scatter_dimension=0, axis_index_groups=rank_groups()
+    )
+    gate_total, _ = shrunk((gate_total, gate_marks), by_big)
+    up_total, _ = shrunk((up_total, up_marks), by_side)
+
+    def parts(*totals):
+        picked = [[pick(total, sending[turn]) for total in totals] for turn in range(count)]
+        return [jnp.concatenate(pieces, axis=-1) for pieces in picked]
+
+    rows_branch = gathered_directly(own_branch, all_branch)
     d_unit = back_product(rows_branch, mixer_out).reshape(count, -1, mixer_out.shape[0])
-    out_sum = peers_scatter(outer_sum(rows_unit, rows_branch).astype(bfloat16))
     d_queries, d_values, terms = run_backward(
         taking[::-1], queries, values, slack_here, mixer_gain_here, mixed, states, d_unit
     )
+    d_queries, d_values, terms, gate_total, up_total = sync(
+        d_queries, d_values, terms, gate_total, up_total
+    )
     d_queries = d_queries.reshape(-1, share)
     d_values = d_values.reshape(-1, share)
 
@@ -726,58 +843,58 @@
         return back_product(cut(d_queries), query_in) + back_product(cut(d_values), value_in)
 
     in_terms = by_turn(token_product(away_rows))
-    in_terms, d_queries, d_values, out_first, gate_total, up_total = sync(
-        in_terms, d_queries, d_values, out_first, gate_state[0], up_state[0]
+    waiting = parts(gate_total, up_total)
+    in_terms, d_queries, d_values, terms, waiting, down_term = sync(
+        in_terms, d_queries, d_values, terms, waiting, down_term
     )
 
     in_first = scatter_first(in_terms)
-    query_term = term_blocks(outer_sum(rows_in, d_queries).astype(bfloat16))
-    value_term = term_blocks(outer_sum(rows_in, d_values).astype(bfloat16))
-    by_core = ((core, 0), functools.partial(across, bit=core))
-    query_state = shrunk((query_term, block_marks()), by_core)
-    value_state = shrunk((value_term, block_marks()), by_core)
+    query_total = core_sum(halves_in, d_queries, across(core_given(halves_in, d_queries), core))
+    value_total = core_sum(halves_in, d_values, across(core_given(halves_in, d_values), core))
     in_own = token_product(own_rows)
-    terms = jnp.transpose(terms.reshape(2, 2 * dp, -1), (1, 0, 2))
-    terms = peers_scatter(terms.reshape(2 * dp, -1))
-    in_first, in_own, query_total, value_total = sync(
-        in_first, in_own, query_state[0], value_state[0]
+    terms = terms + across(terms, core)
+    in_first, in_own, query_total, value_total, terms, in_terms, rows_branch, waiting, out_part = sync(
+        in_first, in_own, query_total, value_total, terms, in_terms, rows_branch, waiting, out_part
     )
 
     in_second = scatter_second(in_terms, in_first)
-    query_state = shrunk((query_total, query_state[1]), by_side)
-    value_state = shrunk((value_total, value_state[1]), by_big)
-    in_second, query_total, value_total = sync(in_second, query_state[0], value_state[0])
-
-    out_second = scatter_second(out_terms, out_first)
-    query_state = shrunk((query_total, query_state[1]), by_big)
-    value_state = shrunk((value_total, value_state[1]), by_side)
-    output = hidden + scattered(out_own, out_first, out_second)
+    query_next, query_marks = shrunk((query_total, marks), by_side)
+    value_next, value_marks = shrunk((value_total, marks), by_big)
+    out_term = outer_sum(rows_unit, rows_branch).astype(bfloat16)
+    peer_terms = [term.reshape(2 * dp, -1, width) for term in (out_term, down_term)]
+    peer_sum = peers_scatter(jnp.concatenate(peer_terms, axis=1).reshape(-1, width))
+    ffn_parts = [waiting[0], turned(waiting[1], 1)]
+    in_second, query_total, value_total, terms, ffn_parts, waiting = sync(
+        in_second, query_next, value_next, terms, ffn_parts, waiting
+    )
+
+    ffn_parts = ffn_parts + [turned(waiting[turn], turn) for turn in range(2, count)]
+
+    query_total, _ = shrunk((query_total, query_marks), by_big)
+    value_total, _ = shrunk((value_total, value_marks), by_side)
+    terms = terms + swapped(terms)
     first_inverse = inverse_rms(tokens)
     d_normed = scattered(in_own, in_first, in_second)
     input_grad = d_hidden + unscaled_grad(
         d_normed * gain_first, tokens * first_inverse, first_inverse
     )
-    query_total, value_total, output, input_grad = sync(
-        query_state[0], value_state[0], output, input_grad
-    )
-
-    def parts(*totals):
-        picked = [[pick(total, sending[turn]) for total in totals] for turn in range(count)]
-        return traded([jnp.concatenate(pieces, axis=-1) for pieces in picked])
-
-    ffn_parts = parts(gate_total, up_total)
-    output, input_grad = from_side(output), from_side(input_grad)
-    ffn_parts, late_terms, down_sum, out_sum, query_total, value_total = sync(
-        ffn_parts, terms, down_sum, out_sum, query_total, value_total
-    )
-
-    mixer_parts = parts(query_total, value_total)
-    out_rows = out_sum.shape[0]
-    sums = to_owners(jnp.concatenate([out_sum, down_sum], axis=0))
-    grad_out, grad_down = sums[:out_rows], sums[out_rows:]
-    terms = to_owners(late_terms).reshape(2, -1)
-    grads_ffn, ffn_product = join_columns(taking, ffn_parts, ffn_weights)
-    grads_mixer, mixer_product = join_columns(taking, mixer_parts, mixer_weights)
+    output = hidden + out_part.astype(float32)
+    query_total, value_total, terms, input_grad, output, ffn_parts = sync(
+        query_total, value_total, terms, input_grad, output, ffn_parts
+    )
+
+    waiting = parts(query_total, value_total)
+    mixer_parts = [waiting[0]] + [turned(waiting[turn], turn) for turn in range(1, count)]
+    ffn_parts, mixer_first = sync(ffn_parts, mixer_parts[1])
+    mixer_parts = mixer_parts[:1] + [mixer_first] + mixer_parts[2:]
+    grads_ffn, ffn_product = join_columns(taking, ffn_parts, ffn_weights, chunks)
+    out_rows = w_out.shape[0]
+    grad_out, grad_down = from_rank(peer_sum[:out_rows]), from_rank(peer_sum[out_rows:])
+    output, input_grad = from_side(output, input_grad)
+    terms = terms + across(terms, big)
+    terms = from_rank(pick(terms.reshape(2, 2 * dp, -1), 2 * lax.axis_index("dp") + side(), 1))
+    mixer_parts, ffn_product = sync(mixer_parts, ffn_product)
+    grads_mixer, mixer_product = join_columns(taking, mixer_parts, mixer_weights, chunks)
 
     return (
         output,

time: 777 us -> 637 us (0.82)
  waiting for transfers between devices: 284 us -> 212 us
  starting transfers between devices: 183 us -> 122 us
  Pallas kernels: 53.6 us -> 83.3 us
  blocking collectives: 18.6 us -> 0 us
  local copies, waits for them, and re-layouts: 59.7 us -> 42.4 us
  matrix products: 78.5 us -> 88.7 us
    ppermute x4 -> x0, waiting for transfers between devices: 78.2 us -> none  [the longest x2 49 us: to_users(): return lax.ppermute(rows, ('dp', 'fsdp'), user_moves())]
    ppermute x32 -> x16, waiting for transfers between devices: 99.7 us -> 46.7 us  [shifted(): return lax.ppermute(array, 'fsdp', moves)]
    ppermute x32 -> x16, starting transfers between devices: 89.6 us -> 51.5 us  [shifted(): return lax.ppermute(array, 'fsdp', moves)]
    ppermute x12 -> x18, waiting for transfers between devices: 13.2 us -> 39 us  [turned(): lax.ppermute(array, 'fsdp', [(i, (i + 2 * turn) % count) for i in range(c...]
    pallas_call x4 -> x8, Pallas kernels: 6.86 us -> 28.6 us  [the longest x2 11.9 us: join_columns(): pl.pallas_call(functools.partial(join_kernel, chunks=chunks), in_specs=[p...]
    unnamed x1 -> x0, blocking collectives: 18.6 us -> none
    ppermute x11, waiting for transfers between devices: 35.6 us -> 50.5 us  [swapped(): return lax.ppermute(array, 'fsdp', [(i, i ^ 1) for i in range(count)])]
    ppermute x4 -> x0, starting transfers between devices: 14.6 us -> none  [the longest x2 7.73 us: to_users(): return lax.ppermute(rows, ('dp', 'fsdp'), user_moves())]
  transfers between devices with their start and end apart: 91 -> 76, of which waited for: 32 -> 24; matrix products, arithmetic and copies ran while one was open for 20% -> 19% of each run, Pallas kernels for 7% -> 13%
where the time goes in v2:
time: 637 us; the launch traced here: 628 us
  waiting for transfers between devices  212 us (33%)
  starting transfers between devices  122 us (19%)
  matrix products  88.7 us (14%)
  Pallas kernels  83.3 us (13%)
  other arithmetic  56.4 us (9%)
  local copies, waits for them, and re-layouts  42.4 us (7%)
  between operations  23.1 us (4%)
    ppermute x16, starting transfers between devices, shifted(): return lax.ppermute(array, 'fsdp', moves)  51.5 us
    ppermute x11, waiting for transfers between devices, swapped(): return lax.ppermute(array, 'fsdp', [(i, i ^ 1) for i in range(count)])  50.5 us
    ppermute x16, waiting for transfers between devices, shifted(): return lax.ppermute(array, 'fsdp', moves)  46.7 us
    ppermute x4, waiting for transfers between devices, ends_traded(): return lax.ppermute(array, 'fsdp', moves)  40.8 us
    ppermute x18, waiting for transfers between devices, turned(): lax.ppermute(array, 'fsdp', [(i, (i + 2 * turn) % count) for i in range(c...  39 us
    dot_general x10, matrix products, outer_sum(): lax.dot_general(left_side, right_side, TN, preferred_element_type=jnp.flo...  36.4 us
    ppermute x22, waiting for transfers between devices, across(): return lax.ppermute(array, 'dp', [(i, i ^ bit) for i in range(count)])  34.1 us
    ppermute x18, starting transfers between devices, turned(): lax.ppermute(array, 'fsdp', [(i, (i + 2 * turn) % count) for i in range(c...  31.3 us
  transfers between devices with their start and end apart: 76, of which 24 were waited for; matrix products, arithmetic and copies ran while one was open for 19% of the time, Pallas kernels for 13%

profile of v2, /device:TPU:2, one launch (start us, length us, event | category | flops | bytes accessed | tf_op | source)
XLA Modules:
  0.0 628.0 jit_solution(17174098260077294916)
XLA Ops:
  27.2 10.6 %collective-permute-done.2.refs_2_ = bf16[64,2176]{1,0:T(8,128)(2,1)} collective-permute-done((bf16[64,2176]{1,0:T(8,128)(2,1)}, bf16[64,2176]{1,0:T(8,128)(2,1)}, u32[]{:S(2)}, u32[]{:S(2)}) %collective-permute-start.2) | collective-permute-done | bytes 278560 | tf_op jit(solution)/shard_map/ppermute | solution.py:42
  41.1 8.4 %collective-permute-start.4 = (bf16[128,2048]{1,0:T(8,128)(2,1)S(1)}, bf16[128,2048]{1,0:T(8,128)(2,1)S(1)}, u32[]{:S(2)}, u32[]{:S(2)}) collective-permute-start(bf16[128,2048]{1,0:T(8,128)(2,1)S(1)} %bitcast.233), channel_id=1, source_target_pairs={{0,2},{1,3},{2,4},{3,5},{4,6},{5,7},{8,10},{9,11},{10,12},{11,13},... | collective-permute-start | bytes 1572872 | tf_op jit(solution)/shard_map/ppermute | solution.py:77
  62.8 12.8 %collective-permute-done.5 = bf16[128,2048]{1,0:T(8,128)(2,1)S(1)} collective-permute-done((bf16[128,2048]{1,0:T(8,128)(2,1)S(1)}, bf16[128,2048]{1,0:T(8,128)(2,1)S(1)}, u32[]{:S(2)}, u32[]{:S(2)}) %collective-permute-start.5) | collective-permute-done | bytes 524320 | tf_op jit(solution)/shard_map/ppermute | solution.py:77
  83.3 7.0 %collective-permute-done.13.refs_1_ = bf16[64,2816]{1,0:T(8,128)(2,1)S(1)} collective-permute-done((bf16[64,2816]{1,0:T(8,128)(2,1)}, bf16[64,2816]{1,0:T(8,128)(2,1)S(1)}, u32[]{:S(2)}, u32[]{:S(2)}) %collective-permute-start.13) | collective-permute-done | bytes 360480 | tf_op jit(solution)/shard_map/ppermute | solution.py:42
  90.8 7.9 %collective-permute-done.10 = bf16[128,2048]{1,0:T(8,128)(2,1)S(1)} collective-permute-done((bf16[128,2048]{1,0:T(8,128)(2,1)S(1)}, bf16[128,2048]{1,0:T(8,128)(2,1)S(1)}, u32[]{:S(2)}, u32[]{:S(2)}) %collective-permute-start.10) | collective-permute-done | bytes 524320 | tf_op jit(solution)/shard_map/ppermute | solution.py:77
  106.2 5.9 assemble_rows.4
  139.9 12.0 %recurrence_forward.1 = (bf16[4,128,512]{2,1,0:T(8,128)(2,1)}, f32[4,128,512]{2,1,0:T(8,128)}, f32[4,4,128,128]{3,2,1,0:T(8,128)}) custom-call(s32[4]{0:T(128)} %and_select_fusion.1.order_ref, f32[4,128,1024]{2,1,0:T(8,128)} %fusion.47.query_ref, f32[4,128,1024]{2,1,0:T(8,128)} %fusion.48.value_ref, f32[1,512]{1,0:T(1,128)} %get-tuple-element.472.slack_ref, ...), custom_call_target="tpu_custom_call" | custom-call | flops 10066329600 | bytes 10485760 | tf_op jit(solution)/shard_map/recurrence_forward/pallas_call | solution.py:576
  151.9 9.0 %collective-permute-done.20 = bf16[4,64,1408]{2,1,0:T(8,128)(2,1)S(1)} collective-permute-done((bf16[4,64,1408]{2,1,0:T(8,128)(2,1)}, bf16[4,64,1408]{2,1,0:T(8,128)(2,1)S(1)}, u32[]{:S(2)}, u32[]{:S(2)}) %collective-permute-start.20) | collective-permute-done | bytes 720928 | tf_op jit(solution)/shard_map/ppermute | solution.py:47
  186.5 24.9 %collective-permute-done.24 = bf16[128,2048]{1,0:T(8,128)(2,1)S(1)} collective-permute-done((bf16[128,2048]{1,0:T(8,128)(2,1)}, bf16[128,2048]{1,0:T(8,128)(2,1)S(1)}, u32[]{:S(2)}, u32[]{:S(2)}) %collective-permute-start.24) | collective-permute-done | bytes 524320 | tf_op jit(solution)/shard_map/ppermute | solution.py:83
  219.2 22.7 %collective-permute-done.28 = bf16[128,2048]{1,0:T(8,128)(2,1)S(1)} collective-permute-done((bf16[128,2048]{1,0:T(8,128)(2,1)S(1)}, bf16[128,2048]{1,0:T(8,128)(2,1)S(1)}, u32[]{:S(2)}, u32[]{:S(2)}) %collective-permute-start.28) | collective-permute-done | bytes 524320 | tf_op jit(solution)/shard_map/ppermute | solution.py:77
  250.5 6.1 assemble_rows.6
  256.7 6.1 assemble_rows.7
  262.8 19.7 %collective-permute-done.32 = bf16[128,2048]{1,0:T(8,128)(2,1)} collective-permute-done((bf16[128,2048]{1,0:T(8,128)(2,1)}, bf16[128,2048]{1,0:T(8,128)(2,1)}, u32[]{:S(2)}, u32[]{:S(2)}) %collective-permute-start.32) | collective-permute-done | bytes 524320 | tf_op jit(solution)/shard_map/ppermute | solution.py:42
  286.0 8.6 %fusion.49 = f32[512,1408]{1,0:T(8,128)} fusion(bf16[512,2048]{1,0:T(8,128)(2,1)S(1)} %constant_dynamic-update-slice_fusion.rows_ref, bf16[2048,1408]{1,0:T(8,128)(2,1)} %bitcast.220), kind=kOutput, calls=%fused_computation.197 | convolution fusion | flops 2952790016 | bytes 10747904 | tf_op jit(solution)/shard_map/dot_general | solution.py:421
  299.2 6.9 %multiply_convert_fusion = (bf16[512,1408]{1,0:T(8,128)(2,1)}, bf16[512,1408]{1,0:T(8,128)(2,1)S(1)}, bf16[512,1408]{1,0:T(8,128)(2,1)S(1)}) fusion(f32[512,1408]{1,0:T(8,128)} %fusion.49, f32[512,1408]{1,0:T(8,128)S(1)} %fusion.26, bf16[512,2048]{1,0:T(8,128)(2,1)S(1)} %copy-done.21, bf16[2048,1408]{1,0:T(8,128)(2,1)S(1)} %bitcast.227), kind=kOutput, calls=%fused_computation.21 | convolution fusion | flops 2964324352 | bytes 17956864 | tf_op jit(solution)/shard_map/dot_general | solution.py:421
  312.5 14.3 %collective-permute-start.36 = (bf16[128,2048]{1,0:T(8,128)(2,1)}, bf16[128,2048]{1,0:T(8,128)(2,1)}, u32[]{:S(2)}, u32[]{:S(2)}) collective-permute-start(bf16[128,2048]{1,0:T(8,128)(2,1)} %get-tuple-element.316), channel_id=1, source_target_pairs={{0,2},{1,3},{2,4},{3,5},{8,10},{9,11},{10,12},{11,13},{16,18},{17,... | collective-permute-start | bytes 1572872 | tf_op jit(solution)/shard_map/ppermute | solution.py:77
  405.6 7.7 %convolution_convert_fusion = bf16[1408,2048]{1,0:T(8,128)(2,1)} fusion(bf16[512,1408]{1,0:T(8,128)(2,1)} %get-tuple-element.338, bf16[128,2048]{1,0:T(8,128)(2,1)} %copy-done.43, bf16[128,2048]{1,0:T(8,128)(2,1)} %copy-done.44, bf16[128,2048]{1,0:T(8,128)(2,1)} %copy-done.45, bf16[128,2048]{1,0:T(8,128)(2,1)} %copy-done.42), kind=kOutput, calls=%fused_computation.1 | convolution fusion | flops 2964062208 | bytes 9306112 | tf_op jit(solution)/shard_map/dot_general | solution.py:425
  413.4 16.3 %collective-permute-done.47 = bf16[4,2,64,1408]{3,2,0,1:T(8,128)(2,1)S(1)} collective-permute-done((bf16[4,2,64,1408]{3,2,0,1:T(8,128)(2,1)}, bf16[4,2,64,1408]{3,2,0,1:T(8,128)(2,1)S(1)}, u32[]{:S(2)}, u32[]{:S(2)}) %collective-permute-start.47) | collective-permute-done | bytes 1441824 | tf_op jit(solution)/shard_map/ppermute | solution.py:47
  443.3 19.3 %recurrence_backward.1 = (bf16[4,128,1024]{2,1,0:T(8,128)(2,1)}, bf16[4,128,1024]{2,1,0:T(8,128)(2,1)}, f32[2,512]{1,0:T(2,128)}) custom-call(s32[4]{0:T(128)} %rev.3.order_ref, f32[4,128,1024]{2,1,0:T(8,128)} %fusion.47.query_ref, f32[4,128,1024]{2,1,0:T(8,128)} %fusion.48.value_ref, f32[1,512]{1,0:T(1,128)} %get-tuple-element.472.slack_ref, ...), custom_call_target="tpu_custom_call" | custom-call | flops 16777216000 | bytes 15728640 | tf_op jit(solution)/shard_map/recurrence_backward/pallas_call | solution.py:611
  495.1 12.9 %collective-permute-done.52 = bf16[128,2048]{1,0:T(8,128)(2,1)} collective-permute-done((bf16[128,2048]{1,0:T(8,128)(2,1)S(1)}, bf16[128,2048]{1,0:T(8,128)(2,1)}, u32[]{:S(2)}, u32[]{:S(2)}) %collective-permute-start.52) | collective-permute-done | bytes 524320 | tf_op jit(solution)/shard_map/ppermute | solution.py:83
  512.4 8.0 %pad_maximum_fusion = bf16[8,240,2048]{2,1,0:T(8,128)(2,1)} fusion(bf16[8,176,2048]{2,1,0:T(8,128)(2,1)} %bitcast.242, bf16[8,64,2048]{2,1,0:T(8,128)(2,1)} %bitcast.255), kind=kLoop, calls=%fused_computation | loop fusion | flops 15728640 | bytes 15728640 | tf_op jit(solution)/shard_map/concatenate | solution.py:865
  532.6 21.7 %collective-permute-done.58 = bf16[2,4,64,1024]{3,2,1,0:T(8,128)(2,1)S(1)} collective-permute-done((bf16[2,4,64,1024]{3,2,1,0:T(8,128)(2,1)S(1)}, bf16[2,4,64,1024]{3,2,1,0:T(8,128)(2,1)S(1)}, u32[]{:S(2)}, u32[]{:S(2)}) %collective-permute-start.58) | collective-permute-done | bytes 1048608 | tf_op jit(solution)/shard_map/ppermute | solution.py:37
  565.4 16.4 %collective-permute-done.63 = f32[2,512]{1,0:T(2,128)S(1)} collective-permute-done((f32[2,512]{1,0:T(2,128)S(1)}, f32[2,512]{1,0:T(2,128)S(1)}, u32[]{:S(2)}, u32[]{:S(2)}) %collective-permute-start.63) | collective-permute-done | bytes 4128 | tf_op jit(solution)/shard_map/ppermute | solution.py:37
  596.9 8.6 %join_columns.2 = (f32[64,5632]{1,0:T(8,128)}, f32[64,5632]{1,0:T(8,128)}, f32[64,1]{1,0:T(8,128)}) custom-call(s32[4]{0:T(128)} %and_select_fusion.1.order_ref, bf16[64,2816]{1,0:T(8,128)(2,1)} %pad_maximum_fusion.10.refs_0_, bf16[64,2816]{1,0:T(8,128)(2,1)} %copy-done.46, bf16[64,2816]{1,0:T(8,128)(2,1)} %copy-done.47, bf16[64,2816]{1,0:T(8,128)(2,1)} %copy-done.48, ...), custom_call_target="tpu_custom_call" | custom-call | bytes 28835840 | tf_op jit(solution)/shard_map/join_columns/pallas_call | solution.py:255
  (467 shorter events, 311.1 us)
Async XLA Ops:
  7.2 68.4 %all-gather.5.cloned.1.call-start = ((), (), s32[]{:S(2)}) async-start(), calls=%async_computation.2 | async-start | bytes 2359296 | tf_op jit(solution)/shard_map/all_gather | solution.py:411
  8.0 235.4 %all-gather.7.cloned.1.call-start = ((), (), s32[]{:S(2)}) async-start(), calls=%async_computation.3 | async-start | bytes 6488064 | tf_op jit(solution)/shard_map/all_gather | solution.py:411
  105.1 157.7 %all-gather.9.cloned.1.call-start = ((), (), s32[]{:S(2)}) async-start(), calls=%async_computation.6 | async-start | bytes 2621440 | tf_op jit(solution)/shard_map/all_gather | solution.py:752
  168.4 43.0 %collective-permute-start.25 = (bf16[2,4,64,1408]{3,2,1,0:T(8,128)(2,1)}, bf16[2,4,64,1408]{3,2,1,0:T(8,128)(2,1)}, u32[]{:S(2)}, u32[]{:S(2)}) collective-permute-start(bf16[2,4,64,1408]{3,2,1,0:T(8,128)(2,1)} %pad_maximum_fusion.4.refs_0_), channel_id=1, source_target_pairs={{0,1},{1,0},{2,3},{3,2},{4,5},{5,4},{6,7},{7,6},{8,9},{9,8},{10,11... | collective-permute-start | bytes 4325384 | tf_op jit(solution)/shard_map/ppermute | solution.py:37
  169.0 42.4 %collective-permute-start.26 = (bf16[2,4,64,1408]{3,2,1,0:T(8,128)(2,1)S(1)}, bf16[2,4,64,1408]{3,2,1,0:T(8,128)(2,1)}, u32[]{:S(2)}, u32[]{:S(2)}) collective-permute-start(bf16[2,4,64,1408]{3,2,1,0:T(8,128)(2,1)S(1)} %pad_maximum_fusion.5.refs_0_), channel_id=1, source_target_pairs={{0,16},{8,24},{16,0},{24,8},{1,17},{9,25},{17,1},{25,9},{2,18},{10... | collective-permute-start | bytes 4325384 | tf_op jit(solution)/shard_map/ppermute | solution.py:47
  176.2 35.2 %collective-permute-start.24 = (bf16[128,2048]{1,0:T(8,128)(2,1)}, bf16[128,2048]{1,0:T(8,128)(2,1)S(1)}, u32[]{:S(2)}, u32[]{:S(2)}) collective-permute-start(bf16[128,2048]{1,0:T(8,128)(2,1)} %broadcast_select_fusion.4), channel_id=1, source_target_pairs={{0,6},{1,7},{6,0},{7,1},{8,14},{9,15},{14,8},{15,9},{16,22},{17,23... | collective-permute-start | bytes 1572872 | tf_op jit(solution)/shard_map/ppermute | solution.py:83
  181.1 326.9 %reduce-scatter.3.cloned.1.call-start = ((), (), s32[]{:S(2)}) async-start(), calls=%async_computation.4 | async-start | bytes 2621440 | tf_op jit(solution)/shard_map/reduce_scatter | solution.py:821
  212.6 29.3 %collective-permute-start.28 = (bf16[128,2048]{1,0:T(8,128)(2,1)S(1)}, bf16[128,2048]{1,0:T(8,128)(2,1)S(1)}, u32[]{:S(2)}, u32[]{:S(2)}) collective-permute-start(bf16[128,2048]{1,0:T(8,128)(2,1)S(1)} %add_convert_fusion.10), channel_id=1, source_target_pairs={{2,0},{3,1},{4,2},{5,3},{6,4},{7,5},{10,8},{11,9},{12,10},{13,11},... | collective-permute-start | bytes 1572872 | tf_op jit(solution)/shard_map/ppermute | solution.py:77
  214.0 27.8 %collective-permute-start.27 = (bf16[128,2048]{1,0:T(8,128)(2,1)S(1)}, bf16[128,2048]{1,0:T(8,128)(2,1)S(1)}, u32[]{:S(2)}, u32[]{:S(2)}) collective-permute-start(bf16[128,2048]{1,0:T(8,128)(2,1)S(1)} %add_convert_fusion.11), channel_id=1, source_target_pairs={{0,2},{1,3},{2,4},{3,5},{4,6},{5,7},{8,10},{9,11},{10,12},{11,13},... | collective-permute-start | bytes 1572872 | tf_op jit(solution)/shard_map/ppermute | solution.py:77
  245.0 37.6 %collective-permute-start.32 = (bf16[128,2048]{1,0:T(8,128)(2,1)}, bf16[128,2048]{1,0:T(8,128)(2,1)}, u32[]{:S(2)}, u32[]{:S(2)}) collective-permute-start(bf16[128,2048]{1,0:T(8,128)(2,1)} %multiply_convert_fusion.3), channel_id=1, source_target_pairs={{0,4},{1,5},{2,6},{3,7},{4,0},{5,1},{6,2},{7,3},{8,12},{9,13},{10,... | collective-permute-start | bytes 1572872 | tf_op jit(solution)/shard_map/ppermute | solution.py:42
  247.6 35.0 %collective-permute-start.33 = (bf16[128,2048]{1,0:T(8,128)(2,1)}, bf16[128,2048]{1,0:T(8,128)(2,1)}, u32[]{:S(2)}, u32[]{:S(2)}) collective-permute-start(bf16[128,2048]{1,0:T(8,128)(2,1)} %multiply_convert_fusion.3), channel_id=1, source_target_pairs={{0,6},{1,7},{2,0},{3,1},{4,2},{5,3},{6,4},{7,5},{8,14},{9,15},{10,... | collective-permute-start | bytes 1572872 | tf_op jit(solution)/shard_map/ppermute | solution.py:42
  312.5 35.5 %collective-permute-start.36 = (bf16[128,2048]{1,0:T(8,128)(2,1)}, bf16[128,2048]{1,0:T(8,128)(2,1)}, u32[]{:S(2)}, u32[]{:S(2)}) collective-permute-start(bf16[128,2048]{1,0:T(8,128)(2,1)} %get-tuple-element.316), channel_id=1, source_target_pairs={{0,2},{1,3},{2,4},{3,5},{8,10},{9,11},{10,12},{11,13},{16,18},{17,... | collective-permute-start | bytes 1572872 | tf_op jit(solution)/shard_map/ppermute | solution.py:77
  378.5 56.3 %collective-permute-start.43 = (bf16[128,2048]{1,0:T(8,128)(2,1)}, bf16[128,2048]{1,0:T(8,128)(2,1)S(1)}, u32[]{:S(2)}, u32[]{:S(2)}) collective-permute-start(bf16[128,2048]{1,0:T(8,128)(2,1)} %get-tuple-element.334), channel_id=1, source_target_pairs={{0,2},{1,3},{2,4},{3,5},{4,6},{5,7},{6,0},{7,1},{8,10},{9,11},{10,... | collective-permute-start | bytes 1572872 | tf_op jit(solution)/shard_map/ppermute | solution.py:42
  380.3 54.5 %collective-permute-start.44 = (bf16[128,2048]{1,0:T(8,128)(2,1)}, bf16[128,2048]{1,0:T(8,128)(2,1)S(1)}, u32[]{:S(2)}, u32[]{:S(2)}) collective-permute-start(bf16[128,2048]{1,0:T(8,128)(2,1)} %get-tuple-element.334), channel_id=1, source_target_pairs={{0,4},{1,5},{2,6},{3,7},{4,0},{5,1},{6,2},{7,3},{8,12},{9,13},{10,... | collective-permute-start | bytes 1572872 | tf_op jit(solution)/shard_map/ppermute | solution.py:42
  381.8 53.0 %collective-permute-start.45 = (bf16[128,2048]{1,0:T(8,128)(2,1)}, bf16[128,2048]{1,0:T(8,128)(2,1)}, u32[]{:S(2)}, u32[]{:S(2)}) collective-permute-start(bf16[128,2048]{1,0:T(8,128)(2,1)} %get-tuple-element.334), channel_id=1, source_target_pairs={{0,6},{1,7},{2,0},{3,1},{4,2},{5,3},{6,4},{7,5},{8,14},{9,15},{10,... | collective-permute-start | bytes 1572872 | tf_op jit(solution)/shard_map/ppermute | solution.py:42
  389.7 42.9 %collective-permute-start.46 = (bf16[2,4,64,1408]{3,2,1,0:T(8,128)(2,1)}, bf16[2,4,64,1408]{3,2,1,0:T(8,128)(2,1)}, u32[]{:S(2)}, u32[]{:S(2)}) collective-permute-start(bf16[2,4,64,1408]{3,2,1,0:T(8,128)(2,1)} %dynamic-slice_bitcast_fusion), channel_id=1, source_target_pairs={{0,1},{1,0},{2,3},{3,2},{4,5},{5,4},{6,7},{7,6},{8,9},{9,8},{10,11... | collective-permute-start | bytes 4325384 | tf_op jit(solution)/shard_map/ppermute | solution.py:37
  398.0 31.7 %collective-permute-start.47 = (bf16[4,2,64,1408]{3,2,0,1:T(8,128)(2,1)}, bf16[4,2,64,1408]{3,2,0,1:T(8,128)(2,1)S(1)}, u32[]{:S(2)}, u32[]{:S(2)}) collective-permute-start(bf16[4,2,64,1408]{3,2,0,1:T(8,128)(2,1)} %bitcast.218), channel_id=1, source_target_pairs={{0,16},{8,24},{16,0},{24,8},{1,17},{9,25},{17,1},{25,9},{2,18},{10... | collective-permute-start | bytes 4325384 | tf_op jit(solution)/shard_map/ppermute | solution.py:47
  443.0 173.6 %reduce-scatter.5.cloned.1.call-start = ((), (), s32[]{:S(2)}) async-start(), calls=%async_computation.5 | async-start | bytes 8847360 | tf_op jit(solution)/shard_map/reduce_scatter | solution.py:415
  521.7 37.5 %collective-permute-start.56 = (bf16[128,2048]{1,0:T(8,128)(2,1)S(1)}, bf16[128,2048]{1,0:T(8,128)(2,1)S(1)}, u32[]{:S(2)}, u32[]{:S(2)}) collective-permute-start(bf16[128,2048]{1,0:T(8,128)(2,1)S(1)} %add_convert_fusion.7), channel_id=1, source_target_pairs={{0,2},{1,3},{2,4},{3,5},{4,6},{5,7},{8,10},{9,11},{10,12},{11,13},... | collective-permute-start | bytes 1572872 | tf_op jit(solution)/shard_map/ppermute | solution.py:77
  524.4 29.9 %collective-permute-start.58 = (bf16[2,4,64,1024]{3,2,1,0:T(8,128)(2,1)S(1)}, bf16[2,4,64,1024]{3,2,1,0:T(8,128)(2,1)S(1)}, u32[]{:S(2)}, u32[]{:S(2)}) collective-permute-start(bf16[2,4,64,1024]{3,2,1,0:T(8,128)(2,1)S(1)} %dynamic-slice_bitcast_fusion.1), channel_id=1, source_target_pairs={{0,1},{1,0},{2,3},{3,2},{4,5},{5,4},{6,7},{7,6},{8,9},{9,8},{10,11... | collective-permute-start | bytes 3145736 | tf_op jit(solution)/shard_map/ppermute | solution.py:37
  526.0 32.7 %collective-permute-start.59 = (bf16[4,2,64,1024]{3,2,0,1:T(8,128)(2,1)S(1)}, bf16[4,2,64,1024]{3,2,0,1:T(8,128)(2,1)S(1)}, u32[]{:S(2)}, u32[]{:S(2)}) collective-permute-start(bf16[4,2,64,1024]{3,2,0,1:T(8,128)(2,1)S(1)} %copy_bitcast_fusion.2), channel_id=1, source_target_pairs={{0,16},{8,24},{16,0},{24,8},{1,17},{9,25},{17,1},{25,9},{2,18},{10... | collective-permute-start | bytes 3145736 | tf_op jit(solution)/shard_map/ppermute | solution.py:47
  528.5 30.8 %collective-permute-start.57 = (bf16[128,2048]{1,0:T(8,128)(2,1)S(1)}, bf16[128,2048]{1,0:T(8,128)(2,1)S(1)}, u32[]{:S(2)}, u32[]{:S(2)}) collective-permute-start(bf16[128,2048]{1,0:T(8,128)(2,1)S(1)} %add_convert_fusion.6), channel_id=1, source_target_pairs={{2,0},{3,1},{4,2},{5,3},{6,4},{7,5},{10,8},{11,9},{12,10},{13,11},... | collective-permute-start | bytes 1572872 | tf_op jit(solution)/shard_map/ppermute | solution.py:77
  529.8 29.4 %collective-permute-start.60 = (bf16[64,2816]{1,0:T(8,128)(2,1)S(1)}, bf16[64,2816]{1,0:T(8,128)(2,1)S(1)}, u32[]{:S(2)}, u32[]{:S(2)}) collective-permute-start(bf16[64,2816]{1,0:T(8,128)(2,1)S(1)} %copy-done.51), channel_id=1, source_target_pairs={{0,2},{1,3},{2,4},{3,5},{4,6},{5,7},{6,0},{7,1},{8,10},{9,11},{10,... | collective-permute-start | bytes 1081352 | tf_op jit(solution)/shard_map/ppermute | solution.py:42
  584.4 31.4 %collective-permute-start.66 = (f32[2,64,2048]{2,1,0:T(8,128)S(1)}, f32[2,64,2048]{2,1,0:T(8,128)S(1)}, u32[]{:S(2)}, u32[]{:S(2)}) collective-permute-start(f32[2,64,2048]{2,1,0:T(8,128)S(1)} %pad_maximum_fusion.8), channel_id=1, source_target_pairs={{0,1},{1,0},{2,3},{3,2},{4,5},{5,4},{6,7},{7,6},{8,9},{9,8},{10,11... | collective-permute-start | bytes 3145736 | tf_op jit(solution)/shard_map/ppermute | solution.py:37
  (139 other events, 1794.7 us)
Sparse Core Ops, SparseCore 0:
  10.0 31.8 all-gather.4
  105.2 48.6 all-gather.6
  181.3 64.8 all-gather.8
  443.2 42.1 reduce-scatter.2
  520.5 92.1 reduce-scatter.4

commit v3 on v2

--- a/solution.py
+++ b/solution.py
@@ -764,14 +764,15 @@
     own_mid = (hidden_hat * gain_second).astype(bfloat16)
     own_mid, gate_blocks, up_blocks, down = sync(own_mid, gate_blocks, up_blocks, down)
 
-    all_mid = gather_first(own_mid, False)
+    mid_step = gather_first(own_mid)
     gate_blocks = gate_blocks + (across(gate_blocks[1], core),)
     up_blocks = up_blocks + (across(up_blocks[1], core),)
     (gate_in,) = assembled(*gate_blocks, False, (units,))
     (up_in,) = assembled(*up_blocks, True, (units,))
-    all_mid, rows_d, gate_in, up_in = sync(all_mid, rows_d, gate_in, up_in)
-
-    rows_mid = gathered_directly(own_mid, all_mid)
+    mid_step, gate_in = sync(mid_step, gate_in)
+    mid_last = gather_second(mid_step)
+    mid_last, rows_d, up_in = sync(mid_last, rows_d, up_in)
+    rows_mid = gathered(own_mid, mid_step, mid_last)
     gate_proj = matmul(rows_mid, gate_in)
     up_proj = matmul(rows_mid, up_in)
     rows_d = jnp.concatenate(reordered(rows_d), axis=0)

time: 637 us -> 635 us (level)
  waiting for transfers between devices: 212 us -> 205 us
    ppermute x18 -> x15, waiting for transfers between devices: 39 us -> 19 us  [turned(): lax.ppermute(array, 'fsdp', [(i, (i + 2 * turn) % count) for i in range(c...]
    ppermute x16 -> x20, waiting for transfers between devices: 46.7 us -> 65.4 us  [shifted(): return lax.ppermute(array, 'fsdp', moves)]
    ppermute x4 -> x5, starting transfers between devices: 17.3 us -> 25.4 us  [ends_traded(): return lax.ppermute(array, 'fsdp', moves)]
    ppermute x4 -> x5, waiting for transfers between devices: 40.8 us -> 32.9 us  [ends_traded(): return lax.ppermute(array, 'fsdp', moves)]
    ppermute x18 -> x15, starting transfers between devices: 31.3 us -> 25.5 us  [turned(): lax.ppermute(array, 'fsdp', [(i, (i + 2 * turn) % count) for i in range(c...]
    unnamed x180 -> x195, local copies, waits for them, and re-layouts: 20.5 us -> 21.4 us
    ppermute x16 -> x20, starting transfers between devices: 51.5 us -> 51.1 us  [shifted(): return lax.ppermute(array, 'fsdp', moves)]
  transfers between devices with their start and end apart: 76 -> 78, of which waited for: 24 -> 29; matrix products, arithmetic and copies ran while one was open for 19% -> 20% of each run, Pallas kernels for 13% -> 13%
where the time goes in v3:
time: 635 us; the launch traced here: 626 us
  waiting for transfers between devices  205 us (32%)
  starting transfers between devices  125 us (20%)
  matrix products  86.6 us (14%)
  Pallas kernels  83.3 us (13%)
  other arithmetic  61 us (10%)
  local copies, waits for them, and re-layouts  41.2 us (6%)
  between operations  23.3 us (4%)
    ppermute x20, waiting for transfers between devices, shifted(): return lax.ppermute(array, 'fsdp', moves)  65.4 us
    ppermute x20, starting transfers between devices, shifted(): return lax.ppermute(array, 'fsdp', moves)  51.1 us
    ppermute x11, waiting for transfers between devices, swapped(): return lax.ppermute(array, 'fsdp', [(i, i ^ 1) for i in range(count)])  51 us
    dot_general x10, matrix products, outer_sum(): lax.dot_general(left_side, right_side, TN, preferred_element_type=jnp.flo...  36.5 us
    ppermute x22, waiting for transfers between devices, across(): return lax.ppermute(array, 'dp', [(i, i ^ bit) for i in range(count)])  35.5 us
    ppermute x5, waiting for transfers between devices, ends_traded(): return lax.ppermute(array, 'fsdp', moves)  32.9 us
    dot_general x7, matrix products, matmul(): return jnp.dot(left_side, right_side, preferred_element_type=jnp.float32)  27.4 us
    ppermute x15, starting transfers between devices, turned(): lax.ppermute(array, 'fsdp', [(i, (i + 2 * turn) % count) for i in range(c...  25.5 us
  transfers between devices with their start and end apart: 78, of which 29 were waited for; matrix products, arithmetic and copies ran while one was open for 20% of the time, Pallas kernels for 13%

profile of v3, /device:TPU:2, one launch (start us, length us, event | category | flops | bytes accessed | tf_op | source)
XLA Modules:
  0.0 625.5 jit_solution(11035494837851395756)
XLA Ops:
  27.2 10.6 %collective-permute-done.2.refs_2_ = bf16[64,2176]{1,0:T(8,128)(2,1)} collective-permute-done((bf16[64,2176]{1,0:T(8,128)(2,1)}, bf16[64,2176]{1,0:T(8,128)(2,1)}, u32[]{:S(2)}, u32[]{:S(2)}) %collective-permute-start.2) | collective-permute-done | bytes 278560 | tf_op jit(solution)/shard_map/ppermute | solution.py:42
  41.2 8.4 %collective-permute-start.4 = (bf16[128,2048]{1,0:T(8,128)(2,1)S(1)}, bf16[128,2048]{1,0:T(8,128)(2,1)S(1)}, u32[]{:S(2)}, u32[]{:S(2)}) collective-permute-start(bf16[128,2048]{1,0:T(8,128)(2,1)S(1)} %bitcast.231), channel_id=1, source_target_pairs={{0,2},{1,3},{2,4},{3,5},{4,6},{5,7},{8,10},{9,11},{10,12},{11,13},... | collective-permute-start | bytes 1572872 | tf_op jit(solution)/shard_map/ppermute | solution.py:77
  62.9 12.8 %collective-permute-done.5 = bf16[128,2048]{1,0:T(8,128)(2,1)S(1)} collective-permute-done((bf16[128,2048]{1,0:T(8,128)(2,1)S(1)}, bf16[128,2048]{1,0:T(8,128)(2,1)S(1)}, u32[]{:S(2)}, u32[]{:S(2)}) %collective-permute-start.5) | collective-permute-done | bytes 524320 | tf_op jit(solution)/shard_map/ppermute | solution.py:77
  83.4 7.0 %collective-permute-done.13.refs_1_ = bf16[64,2816]{1,0:T(8,128)(2,1)S(1)} collective-permute-done((bf16[64,2816]{1,0:T(8,128)(2,1)}, bf16[64,2816]{1,0:T(8,128)(2,1)S(1)}, u32[]{:S(2)}, u32[]{:S(2)}) %collective-permute-start.13) | collective-permute-done | bytes 360480 | tf_op jit(solution)/shard_map/ppermute | solution.py:42
  90.8 7.9 %collective-permute-done.10 = bf16[128,2048]{1,0:T(8,128)(2,1)S(1)} collective-permute-done((bf16[128,2048]{1,0:T(8,128)(2,1)S(1)}, bf16[128,2048]{1,0:T(8,128)(2,1)S(1)}, u32[]{:S(2)}, u32[]{:S(2)}) %collective-permute-start.10) | collective-permute-done | bytes 524320 | tf_op jit(solution)/shard_map/ppermute | solution.py:77
  140.0 12.0 %recurrence_forward.1 = (bf16[4,128,512]{2,1,0:T(8,128)(2,1)}, f32[4,128,512]{2,1,0:T(8,128)}, f32[4,4,128,128]{3,2,1,0:T(8,128)}) custom-call(s32[4]{0:T(128)} %and_select_fusion.1.order_ref, f32[4,128,1024]{2,1,0:T(8,128)} %fusion.49.query_ref, f32[4,128,1024]{2,1,0:T(8,128)} %fusion.50.value_ref, f32[1,512]{1,0:T(1,128)} %get-tuple-element.478.slack_ref, ...), custom_call_target="tpu_custom_call" | custom-call | flops 10066329600 | bytes 10485760 | tf_op jit(solution)/shard_map/recurrence_forward/pallas_call | solution.py:576
  152.0 8.9 %collective-permute-done.20 = bf16[4,64,1408]{2,1,0:T(8,128)(2,1)S(1)} collective-permute-done((bf16[4,64,1408]{2,1,0:T(8,128)(2,1)}, bf16[4,64,1408]{2,1,0:T(8,128)(2,1)S(1)}, u32[]{:S(2)}, u32[]{:S(2)}) %collective-permute-start.20) | collective-permute-done | bytes 720928 | tf_op jit(solution)/shard_map/ppermute | solution.py:47
  185.6 13.6 %collective-permute-done.24 = bf16[128,2048]{1,0:T(8,128)(2,1)S(1)} collective-permute-done((bf16[128,2048]{1,0:T(8,128)(2,1)S(1)}, bf16[128,2048]{1,0:T(8,128)(2,1)S(1)}, u32[]{:S(2)}, u32[]{:S(2)}) %collective-permute-start.24) | collective-permute-done | bytes 524320 | tf_op jit(solution)/shard_map/ppermute | solution.py:83
  210.6 6.2 collective-permute-done.28
  229.7 8.6 %collective-permute-start.33 = (bf16[128,2048]{1,0:T(8,128)(2,1)S(1)}, bf16[128,2048]{1,0:T(8,128)(2,1)S(1)}, u32[]{:S(2)}, u32[]{:S(2)}) collective-permute-start(bf16[128,2048]{1,0:T(8,128)(2,1)S(1)} %multiply_convert_fusion.3), channel_id=1, source_target_pairs={{0,6},{1,7},{6,0},{7,1},{8,14},{9,15},{14,8},{15,9},{16,22},{17,23... | collective-permute-start | bytes 1572872 | tf_op jit(solution)/shard_map/ppermute | solution.py:83
  239.5 6.1 assemble_rows.6
  251.2 20.3 %collective-permute-done.32 = bf16[128,2048]{1,0:T(8,128)(2,1)} collective-permute-done((bf16[128,2048]{1,0:T(8,128)(2,1)S(1)}, bf16[128,2048]{1,0:T(8,128)(2,1)}, u32[]{:S(2)}, u32[]{:S(2)}) %collective-permute-start.32) | collective-permute-done | bytes 524320 | tf_op jit(solution)/shard_map/ppermute | solution.py:77
  271.5 6.8 %collective-permute-done.33 = bf16[128,2048]{1,0:T(8,128)(2,1)S(1)} collective-permute-done((bf16[128,2048]{1,0:T(8,128)(2,1)S(1)}, bf16[128,2048]{1,0:T(8,128)(2,1)S(1)}, u32[]{:S(2)}, u32[]{:S(2)}) %collective-permute-start.33) | collective-permute-done | bytes 524320 | tf_op jit(solution)/shard_map/ppermute | solution.py:83
  283.2 6.1 assemble_rows.7
  297.5 6.2 fusion.41
  308.7 6.9 %multiply_convert_fusion = (bf16[512,1408]{1,0:T(8,128)(2,1)}, bf16[512,1408]{1,0:T(8,128)(2,1)S(1)}, bf16[512,1408]{1,0:T(8,128)(2,1)S(1)}) fusion(f32[512,1408]{1,0:T(8,128)S(1)} %fusion.41, f32[512,1408]{1,0:T(8,128)S(1)} %fusion.26, bf16[2048,1408]{1,0:T(8,128)(2,1)S(1)} %bitcast.225, bf16[128,2048]{1,0:T(8,128)(2,1)S(1)} %get-tuple-element.470, ...), kind=kOutput, calls=%fused_computation.21 | convolution fusion | flops 2972712960 | bytes 17956864 | tf_op jit(solution)/shard_map/dot_general | solution.py:421
  402.5 7.7 %convolution_convert_fusion = bf16[1408,2048]{1,0:T(8,128)(2,1)} fusion(bf16[512,1408]{1,0:T(8,128)(2,1)} %get-tuple-element.342, bf16[128,2048]{1,0:T(8,128)(2,1)} %copy-done.50, bf16[128,2048]{1,0:T(8,128)(2,1)} %copy-done.51, bf16[128,2048]{1,0:T(8,128)(2,1)} %copy-done.52, bf16[128,2048]{1,0:T(8,128)(2,1)} %copy-done.49), kind=kOutput, calls=%fused_computation.1 | convolution fusion | flops 2964062208 | bytes 9306112 | tf_op jit(solution)/shard_map/dot_general | solution.py:425
  410.2 16.7 %collective-permute-done.49 = bf16[4,2,64,1408]{3,2,0,1:T(8,128)(2,1)S(1)} collective-permute-done((bf16[4,2,64,1408]{3,2,0,1:T(8,128)(2,1)}, bf16[4,2,64,1408]{3,2,0,1:T(8,128)(2,1)S(1)}, u32[]{:S(2)}, u32[]{:S(2)}) %collective-permute-start.49) | collective-permute-done | bytes 1441824 | tf_op jit(solution)/shard_map/ppermute | solution.py:47
  440.0 19.2 %recurrence_backward.1 = (bf16[4,128,1024]{2,1,0:T(8,128)(2,1)}, bf16[4,128,1024]{2,1,0:T(8,128)(2,1)}, f32[2,512]{1,0:T(2,128)}) custom-call(s32[4]{0:T(128)} %rev.3.order_ref, f32[4,128,1024]{2,1,0:T(8,128)} %fusion.49.query_ref, f32[4,128,1024]{2,1,0:T(8,128)} %fusion.50.value_ref, f32[1,512]{1,0:T(1,128)} %get-tuple-element.478.slack_ref, ...), custom_call_target="tpu_custom_call" | custom-call | flops 16777216000 | bytes 15728640 | tf_op jit(solution)/shard_map/recurrence_backward/pallas_call | solution.py:611
  492.2 12.5 %collective-permute-done.54 = bf16[128,2048]{1,0:T(8,128)(2,1)} collective-permute-done((bf16[128,2048]{1,0:T(8,128)(2,1)S(1)}, bf16[128,2048]{1,0:T(8,128)(2,1)}, u32[]{:S(2)}, u32[]{:S(2)}) %collective-permute-start.54) | collective-permute-done | bytes 524320 | tf_op jit(solution)/shard_map/ppermute | solution.py:83
  509.1 8.0 %pad_maximum_fusion = bf16[8,240,2048]{2,1,0:T(8,128)(2,1)} fusion(bf16[8,176,2048]{2,1,0:T(8,128)(2,1)} %bitcast.240, bf16[8,64,2048]{2,1,0:T(8,128)(2,1)} %bitcast.253), kind=kLoop, calls=%fused_computation | loop fusion | flops 15728640 | bytes 15728640 | tf_op jit(solution)/shard_map/concatenate | solution.py:866
  531.0 21.6 %collective-permute-done.60 = bf16[2,4,64,1024]{3,2,1,0:T(8,128)(2,1)S(1)} collective-permute-done((bf16[2,4,64,1024]{3,2,1,0:T(8,128)(2,1)S(1)}, bf16[2,4,64,1024]{3,2,1,0:T(8,128)(2,1)S(1)}, u32[]{:S(2)}, u32[]{:S(2)}) %collective-permute-start.60) | collective-permute-done | bytes 1048608 | tf_op jit(solution)/shard_map/ppermute | solution.py:37
  563.9 15.2 %collective-permute-done.65 = f32[2,512]{1,0:T(2,128)S(1)} collective-permute-done((f32[2,512]{1,0:T(2,128)S(1)}, f32[2,512]{1,0:T(2,128)S(1)}, u32[]{:S(2)}, u32[]{:S(2)}) %collective-permute-start.65) | collective-permute-done | bytes 4128 | tf_op jit(solution)/shard_map/ppermute | solution.py:37
  594.5 8.5 %join_columns.2 = (f32[64,5632]{1,0:T(8,128)}, f32[64,5632]{1,0:T(8,128)}, f32[64,1]{1,0:T(8,128)}) custom-call(s32[4]{0:T(128)} %and_select_fusion.1.order_ref, bf16[64,2816]{1,0:T(8,128)(2,1)} %pad_maximum_fusion.11.refs_0_, bf16[64,2816]{1,0:T(8,128)(2,1)} %copy-done.53, bf16[64,2816]{1,0:T(8,128)(2,1)} %copy-done.54, bf16[64,2816]{1,0:T(8,128)(2,1)} %copy-done.55, ...), custom_call_target="tpu_custom_call" | custom-call | bytes 28835840 | tf_op jit(solution)/shard_map/join_columns/pallas_call | solution.py:255
  (488 shorter events, 344.4 us)
Async XLA Ops:
  7.2 68.4 %all-gather.5.cloned.1.call-start = ((), (), s32[]{:S(2)}) async-start(), calls=%async_computation.2 | async-start | bytes 2359296 | tf_op jit(solution)/shard_map/all_gather | solution.py:411
  8.0 214.7 %all-gather.7.cloned.1.call-start = ((), (), s32[]{:S(2)}) async-start(), calls=%async_computation.3 | async-start | bytes 6488064 | tf_op jit(solution)/shard_map/all_gather | solution.py:411
  105.1 185.4 %all-gather.9.cloned.1.call-start = ((), (), s32[]{:S(2)}) async-start(), calls=%async_computation.6 | async-start | bytes 2621440 | tf_op jit(solution)/shard_map/all_gather | solution.py:752
  167.6 33.4 %collective-permute-start.25 = (bf16[2,4,64,1408]{3,2,1,0:T(8,128)(2,1)}, bf16[2,4,64,1408]{3,2,1,0:T(8,128)(2,1)S(1)}, u32[]{:S(2)}, u32[]{:S(2)}) collective-permute-start(bf16[2,4,64,1408]{3,2,1,0:T(8,128)(2,1)} %pad_maximum_fusion.5.refs_0_), channel_id=1, source_target_pairs={{0,1},{1,0},{2,3},{3,2},{4,5},{5,4},{6,7},{7,6},{8,9},{9,8},{10,11... | collective-permute-start | bytes 4325384 | tf_op jit(solution)/shard_map/ppermute | solution.py:37
  168.3 32.9 %collective-permute-start.26 = (bf16[2,4,64,1408]{3,2,1,0:T(8,128)(2,1)S(1)}, bf16[2,4,64,1408]{3,2,1,0:T(8,128)(2,1)S(1)}, u32[]{:S(2)}, u32[]{:S(2)}) collective-permute-start(bf16[2,4,64,1408]{3,2,1,0:T(8,128)(2,1)S(1)} %pad_maximum_fusion.6.refs_0_), channel_id=1, source_target_pairs={{0,16},{8,24},{16,0},{24,8},{1,17},{9,25},{17,1},{25,9},{2,18},{10... | collective-permute-start | bytes 4325384 | tf_op jit(solution)/shard_map/ppermute | solution.py:47
  210.5 294.2 %reduce-scatter.3.cloned.1.call-start = ((), (), s32[]{:S(2)}) async-start(), calls=%async_computation.4 | async-start | bytes 2621440 | tf_op jit(solution)/shard_map/reduce_scatter | solution.py:822
  222.8 59.3 %collective-permute-start.37 = (bf16[2,4,64,1408]{3,2,1,0:T(8,128)(2,1)}, bf16[2,4,64,1408]{3,2,1,0:T(8,128)(2,1)S(1)}, u32[]{:S(2)}, u32[]{:S(2)}) collective-permute-start(bf16[2,4,64,1408]{3,2,1,0:T(8,128)(2,1)} %copy-done.30), channel_id=1, source_target_pairs={{0,8},{8,0},{16,24},{24,16},{1,9},{9,1},{17,25},{25,17},{2,10},{10... | collective-permute-start | bytes 4325384 | tf_op jit(solution)/shard_map/ppermute | solution.py:47
  223.3 27.9 %collective-permute-start.31 = (bf16[128,2048]{1,0:T(8,128)(2,1)S(1)}, bf16[128,2048]{1,0:T(8,128)(2,1)}, u32[]{:S(2)}, u32[]{:S(2)}) collective-permute-start(bf16[128,2048]{1,0:T(8,128)(2,1)S(1)} %multiply_convert_fusion.3), channel_id=1, source_target_pairs={{0,2},{1,3},{2,4},{3,5},{4,6},{5,7},{8,10},{9,11},{10,12},{11,13},... | collective-permute-start | bytes 1572872 | tf_op jit(solution)/shard_map/ppermute | solution.py:77
  228.5 43.0 %collective-permute-start.32 = (bf16[128,2048]{1,0:T(8,128)(2,1)S(1)}, bf16[128,2048]{1,0:T(8,128)(2,1)}, u32[]{:S(2)}, u32[]{:S(2)}) collective-permute-start(bf16[128,2048]{1,0:T(8,128)(2,1)S(1)} %multiply_convert_fusion.3), channel_id=1, source_target_pairs={{2,0},{3,1},{4,2},{5,3},{6,4},{7,5},{10,8},{11,9},{12,10},{13,11},... | collective-permute-start | bytes 1572872 | tf_op jit(solution)/shard_map/ppermute | solution.py:77
  229.7 48.5 %collective-permute-start.33 = (bf16[128,2048]{1,0:T(8,128)(2,1)S(1)}, bf16[128,2048]{1,0:T(8,128)(2,1)S(1)}, u32[]{:S(2)}, u32[]{:S(2)}) collective-permute-start(bf16[128,2048]{1,0:T(8,128)(2,1)S(1)} %multiply_convert_fusion.3), channel_id=1, source_target_pairs={{0,6},{1,7},{6,0},{7,1},{8,14},{9,15},{14,8},{15,9},{16,22},{17,23... | collective-permute-start | bytes 1572872 | tf_op jit(solution)/shard_map/ppermute | solution.py:83
  348.3 27.6 %collective-permute-start.43 = (bf16[1024,1408]{1,0:T(8,128)(2,1)}, bf16[1024,1408]{1,0:T(8,128)(2,1)}, u32[]{:S(2)}, u32[]{:S(2)}) collective-permute-start(bf16[1024,1408]{1,0:T(8,128)(2,1)} %convolution_convert_fusion.2), channel_id=1, source_target_pairs={{0,8},{8,0},{16,24},{24,16},{1,9},{9,1},{17,25},{25,17},{2,10},{10... | collective-permute-start | bytes 8650760 | tf_op jit(solution)/shard_map/ppermute | solution.py:47
  348.3 27.5 %collective-permute-start.44 = (bf16[1024,1408]{1,0:T(8,128)(2,1)}, bf16[1024,1408]{1,0:T(8,128)(2,1)}, u32[]{:S(2)}, u32[]{:S(2)}) collective-permute-start(bf16[1024,1408]{1,0:T(8,128)(2,1)} %convolution_convert_fusion.1), channel_id=1, source_target_pairs={{0,8},{8,0},{16,24},{24,16},{1,9},{9,1},{17,25},{25,17},{2,10},{10... | collective-permute-start | bytes 8650760 | tf_op jit(solution)/shard_map/ppermute | solution.py:47
  375.9 56.1 %collective-permute-start.45 = (bf16[128,2048]{1,0:T(8,128)(2,1)}, bf16[128,2048]{1,0:T(8,128)(2,1)S(1)}, u32[]{:S(2)}, u32[]{:S(2)}) collective-permute-start(bf16[128,2048]{1,0:T(8,128)(2,1)} %get-tuple-element.338), channel_id=1, source_target_pairs={{0,2},{1,3},{2,4},{3,5},{4,6},{5,7},{6,0},{7,1},{8,10},{9,11},{10,... | collective-permute-start | bytes 1572872 | tf_op jit(solution)/shard_map/ppermute | solution.py:42
  377.6 54.5 %collective-permute-start.46 = (bf16[128,2048]{1,0:T(8,128)(2,1)}, bf16[128,2048]{1,0:T(8,128)(2,1)S(1)}, u32[]{:S(2)}, u32[]{:S(2)}) collective-permute-start(bf16[128,2048]{1,0:T(8,128)(2,1)} %get-tuple-element.338), channel_id=1, source_target_pairs={{0,4},{1,5},{2,6},{3,7},{4,0},{5,1},{6,2},{7,3},{8,12},{9,13},{10,... | collective-permute-start | bytes 1572872 | tf_op jit(solution)/shard_map/ppermute | solution.py:42
  379.1 53.0 %collective-permute-start.47 = (bf16[128,2048]{1,0:T(8,128)(2,1)}, bf16[128,2048]{1,0:T(8,128)(2,1)}, u32[]{:S(2)}, u32[]{:S(2)}) collective-permute-start(bf16[128,2048]{1,0:T(8,128)(2,1)} %get-tuple-element.338), channel_id=1, source_target_pairs={{0,6},{1,7},{2,0},{3,1},{4,2},{5,3},{6,4},{7,5},{8,14},{9,15},{10,... | collective-permute-start | bytes 1572872 | tf_op jit(solution)/shard_map/ppermute | solution.py:42
  387.0 42.9 %collective-permute-start.48 = (bf16[2,4,64,1408]{3,2,1,0:T(8,128)(2,1)}, bf16[2,4,64,1408]{3,2,1,0:T(8,128)(2,1)}, u32[]{:S(2)}, u32[]{:S(2)}) collective-permute-start(bf16[2,4,64,1408]{3,2,1,0:T(8,128)(2,1)} %dynamic-slice_bitcast_fusion), channel_id=1, source_target_pairs={{0,1},{1,0},{2,3},{3,2},{4,5},{5,4},{6,7},{7,6},{8,9},{9,8},{10,11... | collective-permute-start | bytes 4325384 | tf_op jit(solution)/shard_map/ppermute | solution.py:37
  395.2 31.7 %collective-permute-start.49 = (bf16[4,2,64,1408]{3,2,0,1:T(8,128)(2,1)}, bf16[4,2,64,1408]{3,2,0,1:T(8,128)(2,1)S(1)}, u32[]{:S(2)}, u32[]{:S(2)}) collective-permute-start(bf16[4,2,64,1408]{3,2,0,1:T(8,128)(2,1)} %bitcast.216), channel_id=1, source_target_pairs={{0,16},{8,24},{16,0},{24,8},{1,17},{9,25},{17,1},{25,9},{2,18},{10... | collective-permute-start | bytes 4325384 | tf_op jit(solution)/shard_map/ppermute | solution.py:47
  439.7 174.5 %reduce-scatter.5.cloned.1.call-start = ((), (), s32[]{:S(2)}) async-start(), calls=%async_computation.5 | async-start | bytes 8847360 | tf_op jit(solution)/shard_map/reduce_scatter | solution.py:415
  519.0 38.9 %collective-permute-start.58 = (bf16[128,2048]{1,0:T(8,128)(2,1)S(1)}, bf16[128,2048]{1,0:T(8,128)(2,1)S(1)}, u32[]{:S(2)}, u32[]{:S(2)}) collective-permute-start(bf16[128,2048]{1,0:T(8,128)(2,1)S(1)} %add_convert_fusion.7), channel_id=1, source_target_pairs={{0,2},{1,3},{2,4},{3,5},{4,6},{5,7},{8,10},{9,11},{10,12},{11,13},... | collective-permute-start | bytes 1572872 | tf_op jit(solution)/shard_map/ppermute | solution.py:77
  521.7 30.8 %collective-permute-start.60 = (bf16[2,4,64,1024]{3,2,1,0:T(8,128)(2,1)S(1)}, bf16[2,4,64,1024]{3,2,1,0:T(8,128)(2,1)S(1)}, u32[]{:S(2)}, u32[]{:S(2)}) collective-permute-start(bf16[2,4,64,1024]{3,2,1,0:T(8,128)(2,1)S(1)} %dynamic-slice_bitcast_fusion.1), channel_id=1, source_target_pairs={{0,1},{1,0},{2,3},{3,2},{4,5},{5,4},{6,7},{7,6},{8,9},{9,8},{10,11... | collective-permute-start | bytes 3145736 | tf_op jit(solution)/shard_map/ppermute | solution.py:37
  523.8 33.5 %collective-permute-start.61 = (bf16[4,2,64,1024]{3,2,0,1:T(8,128)(2,1)S(1)}, bf16[4,2,64,1024]{3,2,0,1:T(8,128)(2,1)S(1)}, u32[]{:S(2)}, u32[]{:S(2)}) collective-permute-start(bf16[4,2,64,1024]{3,2,0,1:T(8,128)(2,1)S(1)} %copy_bitcast_fusion.2), channel_id=1, source_target_pairs={{0,16},{8,24},{16,0},{24,8},{1,17},{9,25},{17,1},{25,9},{2,18},{10... | collective-permute-start | bytes 3145736 | tf_op jit(solution)/shard_map/ppermute | solution.py:47
  526.8 31.0 %collective-permute-start.59 = (bf16[128,2048]{1,0:T(8,128)(2,1)S(1)}, bf16[128,2048]{1,0:T(8,128)(2,1)S(1)}, u32[]{:S(2)}, u32[]{:S(2)}) collective-permute-start(bf16[128,2048]{1,0:T(8,128)(2,1)S(1)} %add_convert_fusion.6), channel_id=1, source_target_pairs={{2,0},{3,1},{4,2},{5,3},{6,4},{7,5},{10,8},{11,9},{12,10},{13,11},... | collective-permute-start | bytes 1572872 | tf_op jit(solution)/shard_map/ppermute | solution.py:77
  528.1 29.7 %collective-permute-start.62 = (bf16[64,2816]{1,0:T(8,128)(2,1)S(1)}, bf16[64,2816]{1,0:T(8,128)(2,1)S(1)}, u32[]{:S(2)}, u32[]{:S(2)}) collective-permute-start(bf16[64,2816]{1,0:T(8,128)(2,1)S(1)} %copy-done.58), channel_id=1, source_target_pairs={{0,2},{1,3},{2,4},{3,5},{4,6},{5,7},{6,0},{7,1},{8,10},{9,11},{10,... | collective-permute-start | bytes 1081352 | tf_op jit(solution)/shard_map/ppermute | solution.py:42
  582.0 31.4 %collective-permute-start.68 = (f32[2,64,2048]{2,1,0:T(8,128)S(1)}, f32[2,64,2048]{2,1,0:T(8,128)S(1)}, u32[]{:S(2)}, u32[]{:S(2)}) collective-permute-start(f32[2,64,2048]{2,1,0:T(8,128)S(1)} %pad_maximum_fusion.9), channel_id=1, source_target_pairs={{0,1},{1,0},{2,3},{3,2},{4,5},{5,4},{6,7},{7,6},{8,9},{9,8},{10,11... | collective-permute-start | bytes 3145736 | tf_op jit(solution)/shard_map/ppermute | solution.py:37
  (150 other events, 1794.2 us)
Sparse Core Ops, SparseCore 0:
  10.0 31.8 all-gather.4
  105.2 48.5 all-gather.6
  210.6 64.5 all-gather.8
  439.9 42.1 reduce-scatter.2
  517.3 92.7 reduce-scatter.4

commit v4 on v3

--- a/solution.py
+++ b/solution.py
@@ -9,7 +9,7 @@
 
 HEAD = 128
 LANES = 128
-VMEM_BYTES = 56 * 1024 * 1024
+VMEM_BYTES = 24 * 1024 * 1024
 HIGHEST = lax.Precision.HIGHEST
 NN = (((1,), (0,)), ((), ()))
 NT = (((1,), (1,)), ((), ()))

time: 635 us -> 634 us (level)
  local copies, waits for them, and re-layouts: 41.2 us -> 69.2 us
  Pallas kernels: 83.3 us -> 58.9 us
  other arithmetic: 61 us -> 53.7 us
    unnamed x195 -> x269, local copies, waits for them, and re-layouts: 21.4 us -> 47.6 us
    ppermute x5, waiting for transfers between devices: 32.9 us -> 41.5 us  [ends_traded(): return lax.ppermute(array, 'fsdp', moves)]
  transfers between devices with their start and end apart: 78 -> 78, of which waited for: 29 -> 30; matrix products, arithmetic and copies ran while one was open for 20% -> 19% of each run, Pallas kernels for 13% -> 9%
where the time goes in v4:
time: 634 us; the launch traced here: 626 us
  waiting for transfers between devices  208 us (33%)
  starting transfers between devices  128 us (20%)
  matrix products  84.3 us (13%)
  local copies, waits for them, and re-layouts  69.2 us (11%)
  Pallas kernels  58.9 us (9%)
  other arithmetic  53.7 us (8%)
  between operations  24.3 us (4%)
    ppermute x20, waiting for transfers between devices, shifted(): return lax.ppermute(array, 'fsdp', moves)  63 us
    ppermute x11, waiting for transfers between devices, swapped(): return lax.ppermute(array, 'fsdp', [(i, i ^ 1) for i in range(count)])  52.6 us
    ppermute x20, starting transfers between devices, shifted(): return lax.ppermute(array, 'fsdp', moves)  50.6 us
    unnamed x269, local copies, waits for them, and re-layouts  47.6 us
    ppermute x5, waiting for transfers between devices, ends_traded(): return lax.ppermute(array, 'fsdp', moves)  41.5 us
    dot_general x10, matrix products, outer_sum(): lax.dot_general(left_side, right_side, TN, preferred_element_type=jnp.flo...  34.9 us
    ppermute x22, waiting for transfers between devices, across(): return lax.ppermute(array, 'dp', [(i, i ^ bit) for i in range(count)])  34.7 us
    ppermute x5, starting transfers between devices, ends_traded(): return lax.ppermute(array, 'fsdp', moves)  29.3 us
  transfers between devices with their start and end apart: 78, of which 30 were waited for; matrix products, arithmetic and copies ran while one was open for 19% of the time, Pallas kernels for 9%

profile of v4, /device:TPU:2, one launch (start us, length us, event | category | flops | bytes accessed | tf_op | source)
XLA Modules:
  0.0 626.2 jit_solution(10102922679681991129)
XLA Ops:
  21.2 6.5 %collective-permute-done = bf16[2,64,2048]{2,1,0:T(8,128)(2,1)} collective-permute-done((bf16[2,64,2048]{2,1,0:T(8,128)(2,1)}, bf16[2,64,2048]{2,1,0:T(8,128)(2,1)}, u32[]{:S(2)}, u32[]{:S(2)}) %collective-permute-start) | collective-permute-done | bytes 524320 | tf_op jit(solution)/shard_map/ppermute | solution.py:37
  28.8 6.8 %collective-permute-done.2.refs_2_ = bf16[64,2176]{1,0:T(8,128)(2,1)S(1)} collective-permute-done((bf16[64,2176]{1,0:T(8,128)(2,1)S(1)}, bf16[64,2176]{1,0:T(8,128)(2,1)S(1)}, u32[]{:S(2)}, u32[]{:S(2)}) %collective-permute-start.2) | collective-permute-done | bytes 278560 | tf_op jit(solution)/shard_map/ppermute | solution.py:42
  36.7 8.4 %collective-permute-start.4 = (bf16[128,2048]{1,0:T(8,128)(2,1)}, bf16[128,2048]{1,0:T(8,128)(2,1)S(1)}, u32[]{:S(2)}, u32[]{:S(2)}) collective-permute-start(bf16[128,2048]{1,0:T(8,128)(2,1)} %bitcast.249), channel_id=1, source_target_pairs={{0,2},{1,3},{2,4},{3,5},{4,6},{5,7},{8,10},{9,11},{10,12},{11,13},... | collective-permute-start | bytes 1572872 | tf_op jit(solution)/shard_map/ppermute | solution.py:77
  57.7 13.8 %collective-permute-done.5 = bf16[128,2048]{1,0:T(8,128)(2,1)S(1)} collective-permute-done((bf16[128,2048]{1,0:T(8,128)(2,1)}, bf16[128,2048]{1,0:T(8,128)(2,1)S(1)}, u32[]{:S(2)}, u32[]{:S(2)}) %collective-permute-start.5) | collective-permute-done | bytes 524320 | tf_op jit(solution)/shard_map/ppermute | solution.py:77
  80.8 7.1 %collective-permute-done.13.refs_1_ = bf16[64,2816]{1,0:T(8,128)(2,1)} collective-permute-done((bf16[64,2816]{1,0:T(8,128)(2,1)}, bf16[64,2816]{1,0:T(8,128)(2,1)}, u32[]{:S(2)}, u32[]{:S(2)}) %collective-permute-start.13) | collective-permute-done | bytes 360480 | tf_op jit(solution)/shard_map/ppermute | solution.py:42
  88.4 7.5 %collective-permute-done.10 = bf16[128,2048]{1,0:T(8,128)(2,1)} collective-permute-done((bf16[128,2048]{1,0:T(8,128)(2,1)}, bf16[128,2048]{1,0:T(8,128)(2,1)}, u32[]{:S(2)}, u32[]{:S(2)}) %collective-permute-start.10) | collective-permute-done | bytes 524320 | tf_op jit(solution)/shard_map/ppermute | solution.py:77
  142.7 9.7 %recurrence_forward.1 = (bf16[4,128,512]{2,1,0:T(8,128)(2,1)S(1)}, f32[4,128,512]{2,1,0:T(8,128)S(1)}, f32[4,4,128,128]{3,2,1,0:T(8,128)S(1)}) custom-call(s32[4]{0:T(128)S(1)} %and_select_fusion.1.order_ref, f32[4,128,1024]{2,1,0:T(8,128)S(1)} %copy-done.49, f32[4,128,1024]{2,1,0:T(8,128)S(1)} %copy-done.51, f32[1,512]{1,0:T(1,128)S(1)} %get-tuple-element.478.slack_ref, ...), custom_call_target="tpu_custom_call" | custom-call | flops 10066329600 | bytes 10485760 | tf_op jit(solution)/shard_map/recurrence_forward/pallas_call | solution.py:576
  152.5 8.1 %collective-permute-done.20 = bf16[4,64,1408]{2,1,0:T(8,128)(2,1)S(1)} collective-permute-done((bf16[4,64,1408]{2,1,0:T(8,128)(2,1)S(1)}, bf16[4,64,1408]{2,1,0:T(8,128)(2,1)S(1)}, u32[]{:S(2)}, u32[]{:S(2)}) %collective-permute-start.20) | collective-permute-done | bytes 720928 | tf_op jit(solution)/shard_map/ppermute | solution.py:47
  183.6 13.7 %collective-permute-done.24 = bf16[128,2048]{1,0:T(8,128)(2,1)S(1)} collective-permute-done((bf16[128,2048]{1,0:T(8,128)(2,1)S(1)}, bf16[128,2048]{1,0:T(8,128)(2,1)S(1)}, u32[]{:S(2)}, u32[]{:S(2)}) %collective-permute-start.24) | collective-permute-done | bytes 524320 | tf_op jit(solution)/shard_map/ppermute | solution.py:83
  228.8 10.2 %collective-permute-start.33 = (bf16[128,2048]{1,0:T(8,128)(2,1)}, bf16[128,2048]{1,0:T(8,128)(2,1)}, u32[]{:S(2)}, u32[]{:S(2)}) collective-permute-start(bf16[128,2048]{1,0:T(8,128)(2,1)} %multiply_convert_fusion.3), channel_id=1, source_target_pairs={{0,6},{1,7},{6,0},{7,1},{8,14},{9,15},{14,8},{15,9},{16,22},{17,23... | collective-permute-start | bytes 1572872 | tf_op jit(solution)/shard_map/ppermute | solution.py:83
  250.5 17.6 %collective-permute-done.32 = bf16[128,2048]{1,0:T(8,128)(2,1)} collective-permute-done((bf16[128,2048]{1,0:T(8,128)(2,1)}, bf16[128,2048]{1,0:T(8,128)(2,1)}, u32[]{:S(2)}, u32[]{:S(2)}) %collective-permute-start.32) | collective-permute-done | bytes 524320 | tf_op jit(solution)/shard_map/ppermute | solution.py:77
  268.2 9.0 %collective-permute-done.33 = bf16[128,2048]{1,0:T(8,128)(2,1)} collective-permute-done((bf16[128,2048]{1,0:T(8,128)(2,1)}, bf16[128,2048]{1,0:T(8,128)(2,1)}, u32[]{:S(2)}, u32[]{:S(2)}) %collective-permute-start.33) | collective-permute-done | bytes 524320 | tf_op jit(solution)/shard_map/ppermute | solution.py:83
  281.5 6.4 %assemble_rows.7 = bf16[4,4,2,64,1408]{4,3,2,1,0:T(8,128)(2,1)S(1)} custom-call(s32[3]{0:T(128)S(1)} %pad_add_fusion.place_ref, bf16[2,4,64,1408]{3,2,1,0:T(8,128)(2,1)S(1)} %pad_maximum_fusion.6.refs_0_, bf16[2,4,64,1408]{3,2,1,0:T(8,128)(2,1)S(1)} %copy-done.12, bf16[2,4,64,1408]{3,2,1,0:T(8,128)(2,1)} %collective-permute-done.30.refs_2_, ...), custom_call_target="tpu_custom_call" | custom-call | bytes 46137344 | tf_op jit(solution)/shard_map/assemble_rows/pallas_call | solution.py:302
  295.6 6.4 %fusion.41 = f32[512,1408]{1,0:T(8,128)S(1)} fusion(bf16[2048,1408]{1,0:T(8,128)(2,1)} %bitcast.217, bf16[128,2048]{1,0:T(8,128)(2,1)S(1)} %get-tuple-element.470, bf16[128,2048]{1,0:T(8,128)(2,1)S(1)} %broadcast_select_fusion.2, bf16[128,2048]{1,0:T(8,128)(2,1)S(1)} %get-tuple-element.469, bf16[128,2048]{1,0:T(8,128)(2,1)} %multiply_convert_fusion.3), kind=kOutput, calls=%fused_computation.189 | convolution fusion | flops 2961178624 | bytes 10747904 | tf_op jit(solution)/shard_map/dot_general | solution.py:421
  307.1 6.9 %multiply_convert_fusion = (bf16[512,1408]{1,0:T(8,128)(2,1)}, bf16[512,1408]{1,0:T(8,128)(2,1)S(1)}, bf16[512,1408]{1,0:T(8,128)(2,1)S(1)}) fusion(f32[512,1408]{1,0:T(8,128)S(1)} %fusion.41, f32[512,1408]{1,0:T(8,128)S(1)} %fusion.26, bf16[2048,1408]{1,0:T(8,128)(2,1)S(1)} %bitcast.224, bf16[128,2048]{1,0:T(8,128)(2,1)S(1)} %get-tuple-element.470, ...), kind=kOutput, calls=%fused_computation.21 | convolution fusion | flops 2972712960 | bytes 17956864 | tf_op jit(solution)/shard_map/dot_general | solution.py:421
  341.0 8.1 %collective-permute-done.40 = bf16[128,2048]{1,0:T(8,128)(2,1)S(1)} collective-permute-done((bf16[128,2048]{1,0:T(8,128)(2,1)S(1)}, bf16[128,2048]{1,0:T(8,128)(2,1)S(1)}, u32[]{:S(2)}, u32[]{:S(2)}) %collective-permute-start.40) | collective-permute-done | bytes 524320 | tf_op jit(solution)/shard_map/ppermute | solution.py:83
  400.0 7.6 %convolution_convert_fusion = bf16[1408,2048]{1,0:T(8,128)(2,1)} fusion(bf16[512,1408]{1,0:T(8,128)(2,1)} %get-tuple-element.342, bf16[128,2048]{1,0:T(8,128)(2,1)} %copy-done.100, bf16[128,2048]{1,0:T(8,128)(2,1)} %copy-done.101, bf16[128,2048]{1,0:T(8,128)(2,1)} %copy-done.102, bf16[128,2048]{1,0:T(8,128)(2,1)} %copy-done.99), kind=kOutput, calls=%fused_computation.1 | convolution fusion | flops 2964062208 | bytes 9306112 | tf_op jit(solution)/shard_map/dot_general | solution.py:425
  407.6 17.2 %collective-permute-done.49 = bf16[4,2,64,1408]{3,2,0,1:T(8,128)(2,1)} collective-permute-done((bf16[4,2,64,1408]{3,2,0,1:T(8,128)(2,1)}, bf16[4,2,64,1408]{3,2,0,1:T(8,128)(2,1)}, u32[]{:S(2)}, u32[]{:S(2)}) %collective-permute-start.49) | collective-permute-done | bytes 1441824 | tf_op jit(solution)/shard_map/ppermute | solution.py:47
  444.4 16.5 %recurrence_backward.1 = (bf16[4,128,1024]{2,1,0:T(8,128)(2,1)S(1)}, bf16[4,128,1024]{2,1,0:T(8,128)(2,1)S(1)}, f32[2,512]{1,0:T(2,128)S(1)}) custom-call(s32[4]{0:T(128)S(1)} %rev.3.order_ref, f32[4,128,1024]{2,1,0:T(8,128)S(1)} %copy-done.50, f32[4,128,1024]{2,1,0:T(8,128)S(1)} %copy-done.52, f32[1,512]{1,0:T(1,128)S(1)} %copy-done.41, ...), custom_call_target="tpu_custom_call" | custom-call | flops 16777216000 | bytes 15728640 | tf_op jit(solution)/shard_map/recurrence_backward/pallas_call | solution.py:611
  492.2 10.7 %collective-permute-done.54 = bf16[128,2048]{1,0:T(8,128)(2,1)S(1)} collective-permute-done((bf16[128,2048]{1,0:T(8,128)(2,1)S(1)}, bf16[128,2048]{1,0:T(8,128)(2,1)S(1)}, u32[]{:S(2)}, u32[]{:S(2)}) %collective-permute-start.54) | collective-permute-done | bytes 524320 | tf_op jit(solution)/shard_map/ppermute | solution.py:83
  507.3 7.9 %pad_maximum_fusion = bf16[8,240,2048]{2,1,0:T(8,128)(2,1)} fusion(bf16[8,176,2048]{2,1,0:T(8,128)(2,1)} %bitcast.256, bf16[8,64,2048]{2,1,0:T(8,128)(2,1)} %bitcast.266), kind=kLoop, calls=%fused_computation | loop fusion | flops 15728640 | bytes 15728640 | tf_op jit(solution)/shard_map/concatenate | solution.py:866
  528.8 21.7 %collective-permute-done.60 = bf16[2,4,64,1024]{3,2,1,0:T(8,128)(2,1)S(1)} collective-permute-done((bf16[2,4,64,1024]{3,2,1,0:T(8,128)(2,1)S(1)}, bf16[2,4,64,1024]{3,2,1,0:T(8,128)(2,1)S(1)}, u32[]{:S(2)}, u32[]{:S(2)}) %collective-permute-start.60) | collective-permute-done | bytes 1048608 | tf_op jit(solution)/shard_map/ppermute | solution.py:37
  560.7 15.8 %collective-permute-done.65 = f32[2,512]{1,0:T(2,128)S(1)} collective-permute-done((f32[2,512]{1,0:T(2,128)S(1)}, f32[2,512]{1,0:T(2,128)S(1)}, u32[]{:S(2)}, u32[]{:S(2)}) %collective-permute-start.65) | collective-permute-done | bytes 4128 | tf_op jit(solution)/shard_map/ppermute | solution.py:37
  595.7 7.2 %join_columns.2 = (f32[64,5632]{1,0:T(8,128)}, f32[64,5632]{1,0:T(8,128)}, f32[64,1]{1,0:T(8,128)S(1)}) custom-call(s32[4]{0:T(128)S(1)} %and_select_fusion.1.order_ref, bf16[64,2816]{1,0:T(8,128)(2,1)S(1)} %pad_maximum_fusion.11.refs_0_, bf16[64,2816]{1,0:T(8,128)(2,1)S(1)} %collective-permute-done.62.refs_1_, bf16[64,2816]{1,0:T(8,128)(2,1)S(1)} %copy-done.35, ...), custom_call_target="tpu_custom_call" | custom-call | bytes 28835840 | tf_op jit(solution)/shard_map/join_columns/pallas_call | solution.py:255
  (562 shorter events, 351.0 us)
Async XLA Ops:
  7.3 64.3 %all-gather.5.cloned.1.call-start = ((), (), s32[]{:S(2)}) async-start(), calls=%async_computation.2 | async-start | bytes 2359296 | tf_op jit(solution)/shard_map/all_gather | solution.py:411
  8.0 213.9 %all-gather.7.cloned.1.call-start = ((), (), s32[]{:S(2)}) async-start(), calls=%async_computation.3 | async-start | bytes 6488064 | tf_op jit(solution)/shard_map/all_gather | solution.py:411
  45.1 26.4 %collective-permute-start.5 = (bf16[128,2048]{1,0:T(8,128)(2,1)}, bf16[128,2048]{1,0:T(8,128)(2,1)S(1)}, u32[]{:S(2)}, u32[]{:S(2)}) collective-permute-start(bf16[128,2048]{1,0:T(8,128)(2,1)} %bitcast.250), channel_id=1, source_target_pairs={{2,0},{3,1},{4,2},{5,3},{6,4},{7,5},{10,8},{11,9},{12,10},{13,11},... | collective-permute-start | bytes 1572872 | tf_op jit(solution)/shard_map/ppermute | solution.py:77
  104.6 187.1 %all-gather.9.cloned.1.call-start = ((), (), s32[]{:S(2)}) async-start(), calls=%async_computation.6 | async-start | bytes 2621440 | tf_op jit(solution)/shard_map/all_gather | solution.py:752
  165.7 33.2 %collective-permute-start.25 = (bf16[2,4,64,1408]{3,2,1,0:T(8,128)(2,1)}, bf16[2,4,64,1408]{3,2,1,0:T(8,128)(2,1)S(1)}, u32[]{:S(2)}, u32[]{:S(2)}) collective-permute-start(bf16[2,4,64,1408]{3,2,1,0:T(8,128)(2,1)} %pad_maximum_fusion.5.refs_0_), channel_id=1, source_target_pairs={{0,1},{1,0},{2,3},{3,2},{4,5},{5,4},{6,7},{7,6},{8,9},{9,8},{10,11... | collective-permute-start | bytes 4325384 | tf_op jit(solution)/shard_map/ppermute | solution.py:37
  166.3 32.9 %collective-permute-start.26 = (bf16[2,4,64,1408]{3,2,1,0:T(8,128)(2,1)S(1)}, bf16[2,4,64,1408]{3,2,1,0:T(8,128)(2,1)S(1)}, u32[]{:S(2)}, u32[]{:S(2)}) collective-permute-start(bf16[2,4,64,1408]{3,2,1,0:T(8,128)(2,1)S(1)} %pad_maximum_fusion.6.refs_0_), channel_id=1, source_target_pairs={{0,16},{8,24},{16,0},{24,8},{1,17},{9,25},{17,1},{25,9},{2,18},{10... | collective-permute-start | bytes 4325384 | tf_op jit(solution)/shard_map/ppermute | solution.py:47
  208.5 294.4 %reduce-scatter.3.cloned.1.call-start = ((), (), s32[]{:S(2)}) async-start(), calls=%async_computation.4 | async-start | bytes 2621440 | tf_op jit(solution)/shard_map/reduce_scatter | solution.py:822
  222.0 58.2 %collective-permute-start.37 = (bf16[2,4,64,1408]{3,2,1,0:T(8,128)(2,1)}, bf16[2,4,64,1408]{3,2,1,0:T(8,128)(2,1)}, u32[]{:S(2)}, u32[]{:S(2)}) collective-permute-start(bf16[2,4,64,1408]{3,2,1,0:T(8,128)(2,1)} %copy-done.11), channel_id=1, source_target_pairs={{0,8},{8,0},{16,24},{24,16},{1,9},{9,1},{17,25},{25,17},{2,10},{10... | collective-permute-start | bytes 4325384 | tf_op jit(solution)/shard_map/ppermute | solution.py:47
  222.5 28.1 %collective-permute-start.31 = (bf16[128,2048]{1,0:T(8,128)(2,1)}, bf16[128,2048]{1,0:T(8,128)(2,1)}, u32[]{:S(2)}, u32[]{:S(2)}) collective-permute-start(bf16[128,2048]{1,0:T(8,128)(2,1)} %multiply_convert_fusion.3), channel_id=1, source_target_pairs={{0,2},{1,3},{2,4},{3,5},{4,6},{5,7},{8,10},{9,11},{10,12},{11,13},... | collective-permute-start | bytes 1572872 | tf_op jit(solution)/shard_map/ppermute | solution.py:77
  227.5 40.6 %collective-permute-start.32 = (bf16[128,2048]{1,0:T(8,128)(2,1)}, bf16[128,2048]{1,0:T(8,128)(2,1)}, u32[]{:S(2)}, u32[]{:S(2)}) collective-permute-start(bf16[128,2048]{1,0:T(8,128)(2,1)} %multiply_convert_fusion.3), channel_id=1, source_target_pairs={{2,0},{3,1},{4,2},{5,3},{6,4},{7,5},{10,8},{11,9},{12,10},{13,11},... | collective-permute-start | bytes 1572872 | tf_op jit(solution)/shard_map/ppermute | solution.py:77
  228.8 48.3 %collective-permute-start.33 = (bf16[128,2048]{1,0:T(8,128)(2,1)}, bf16[128,2048]{1,0:T(8,128)(2,1)}, u32[]{:S(2)}, u32[]{:S(2)}) collective-permute-start(bf16[128,2048]{1,0:T(8,128)(2,1)} %multiply_convert_fusion.3), channel_id=1, source_target_pairs={{0,6},{1,7},{6,0},{7,1},{8,14},{9,15},{14,8},{15,9},{16,22},{17,23... | collective-permute-start | bytes 1572872 | tf_op jit(solution)/shard_map/ppermute | solution.py:83
  374.1 54.8 %collective-permute-start.45 = (bf16[128,2048]{1,0:T(8,128)(2,1)S(1)}, bf16[128,2048]{1,0:T(8,128)(2,1)}, u32[]{:S(2)}, u32[]{:S(2)}) collective-permute-start(bf16[128,2048]{1,0:T(8,128)(2,1)S(1)} %get-tuple-element.338), channel_id=1, source_target_pairs={{0,2},{1,3},{2,4},{3,5},{4,6},{5,7},{6,0},{7,1},{8,10},{9,11},{10,... | collective-permute-start | bytes 1572872 | tf_op jit(solution)/shard_map/ppermute | solution.py:42
  376.7 52.3 %collective-permute-start.46 = (bf16[128,2048]{1,0:T(8,128)(2,1)S(1)}, bf16[128,2048]{1,0:T(8,128)(2,1)}, u32[]{:S(2)}, u32[]{:S(2)}) collective-permute-start(bf16[128,2048]{1,0:T(8,128)(2,1)S(1)} %get-tuple-element.338), channel_id=1, source_target_pairs={{0,4},{1,5},{2,6},{3,7},{4,0},{5,1},{6,2},{7,3},{8,12},{9,13},{10,... | collective-permute-start | bytes 1572872 | tf_op jit(solution)/shard_map/ppermute | solution.py:42
  377.9 51.1 %collective-permute-start.47 = (bf16[128,2048]{1,0:T(8,128)(2,1)S(1)}, bf16[128,2048]{1,0:T(8,128)(2,1)}, u32[]{:S(2)}, u32[]{:S(2)}) collective-permute-start(bf16[128,2048]{1,0:T(8,128)(2,1)S(1)} %get-tuple-element.338), channel_id=1, source_target_pairs={{0,6},{1,7},{2,0},{3,1},{4,2},{5,3},{6,4},{7,5},{8,14},{9,15},{10,... | collective-permute-start | bytes 1572872 | tf_op jit(solution)/shard_map/ppermute | solution.py:42
  385.8 40.9 %collective-permute-start.48 = (bf16[2,4,64,1408]{3,2,1,0:T(8,128)(2,1)}, bf16[2,4,64,1408]{3,2,1,0:T(8,128)(2,1)}, u32[]{:S(2)}, u32[]{:S(2)}) collective-permute-start(bf16[2,4,64,1408]{3,2,1,0:T(8,128)(2,1)} %dynamic-slice_bitcast_fusion), channel_id=1, source_target_pairs={{0,1},{1,0},{2,3},{3,2},{4,5},{5,4},{6,7},{7,6},{8,9},{9,8},{10,11... | collective-permute-start | bytes 4325384 | tf_op jit(solution)/shard_map/ppermute | solution.py:37
  393.0 31.9 %collective-permute-start.49 = (bf16[4,2,64,1408]{3,2,0,1:T(8,128)(2,1)}, bf16[4,2,64,1408]{3,2,0,1:T(8,128)(2,1)}, u32[]{:S(2)}, u32[]{:S(2)}) collective-permute-start(bf16[4,2,64,1408]{3,2,0,1:T(8,128)(2,1)} %bitcast.216), channel_id=1, source_target_pairs={{0,16},{8,24},{16,0},{24,8},{1,17},{9,25},{17,1},{25,9},{2,18},{10... | collective-permute-start | bytes 4325384 | tf_op jit(solution)/shard_map/ppermute | solution.py:47
  435.1 25.9 %collective-permute-start.50 = (bf16[4,64,1408]{2,1,0:T(8,128)(2,1)}, bf16[4,64,1408]{2,1,0:T(8,128)(2,1)}, u32[]{:S(2)}, u32[]{:S(2)}) collective-permute-start(bf16[4,64,1408]{2,1,0:T(8,128)(2,1)} %dynamic-slice_bitcast_fusion.3), channel_id=1, source_target_pairs={{0,16},{8,24},{16,0},{24,8},{1,17},{9,25},{17,1},{25,9},{2,18},{10... | collective-permute-start | bytes 2162696 | tf_op jit(solution)/shard_map/ppermute | solution.py:47
  438.3 176.7 %reduce-scatter.5.cloned.1.call-start = ((), (), s32[]{:S(2)}) async-start(), calls=%async_computation.5 | async-start | bytes 8847360 | tf_op jit(solution)/shard_map/reduce_scatter | solution.py:415
  516.6 40.6 %collective-permute-start.58 = (bf16[128,2048]{1,0:T(8,128)(2,1)S(1)}, bf16[128,2048]{1,0:T(8,128)(2,1)S(1)}, u32[]{:S(2)}, u32[]{:S(2)}) collective-permute-start(bf16[128,2048]{1,0:T(8,128)(2,1)S(1)} %add_convert_fusion.7), channel_id=1, source_target_pairs={{0,2},{1,3},{2,4},{3,5},{4,6},{5,7},{8,10},{9,11},{10,12},{11,13},... | collective-permute-start | bytes 1572872 | tf_op jit(solution)/shard_map/ppermute | solution.py:77
  520.6 29.9 %collective-permute-start.60 = (bf16[2,4,64,1024]{3,2,1,0:T(8,128)(2,1)S(1)}, bf16[2,4,64,1024]{3,2,1,0:T(8,128)(2,1)S(1)}, u32[]{:S(2)}, u32[]{:S(2)}) collective-permute-start(bf16[2,4,64,1024]{3,2,1,0:T(8,128)(2,1)S(1)} %dynamic-slice_bitcast_fusion.1), channel_id=1, source_target_pairs={{0,1},{1,0},{2,3},{3,2},{4,5},{5,4},{6,7},{7,6},{8,9},{9,8},{10,11... | collective-permute-start | bytes 3145736 | tf_op jit(solution)/shard_map/ppermute | solution.py:37
  522.3 34.3 %collective-permute-start.61 = (bf16[4,2,64,1024]{3,2,0,1:T(8,128)(2,1)S(1)}, bf16[4,2,64,1024]{3,2,0,1:T(8,128)(2,1)S(1)}, u32[]{:S(2)}, u32[]{:S(2)}) collective-permute-start(bf16[4,2,64,1024]{3,2,0,1:T(8,128)(2,1)S(1)} %copy_bitcast_fusion.2), channel_id=1, source_target_pairs={{0,16},{8,24},{16,0},{24,8},{1,17},{9,25},{17,1},{25,9},{2,18},{10... | collective-permute-start | bytes 3145736 | tf_op jit(solution)/shard_map/ppermute | solution.py:47
  524.6 32.5 %collective-permute-start.59 = (bf16[128,2048]{1,0:T(8,128)(2,1)S(1)}, bf16[128,2048]{1,0:T(8,128)(2,1)S(1)}, u32[]{:S(2)}, u32[]{:S(2)}) collective-permute-start(bf16[128,2048]{1,0:T(8,128)(2,1)S(1)} %add_convert_fusion.6), channel_id=1, source_target_pairs={{2,0},{3,1},{4,2},{5,3},{6,4},{7,5},{10,8},{11,9},{12,10},{13,11},... | collective-permute-start | bytes 1572872 | tf_op jit(solution)/shard_map/ppermute | solution.py:77
  525.9 31.2 %collective-permute-start.62 = (bf16[64,2816]{1,0:T(8,128)(2,1)S(1)}, bf16[64,2816]{1,0:T(8,128)(2,1)S(1)}, u32[]{:S(2)}, u32[]{:S(2)}) collective-permute-start(bf16[64,2816]{1,0:T(8,128)(2,1)S(1)} %copy-done.105), channel_id=1, source_target_pairs={{0,2},{1,3},{2,4},{3,5},{4,6},{5,7},{6,0},{7,1},{8,10},{9,11},{10,... | collective-permute-start | bytes 1081352 | tf_op jit(solution)/shard_map/ppermute | solution.py:42
  580.6 32.1 %collective-permute-start.68 = (f32[2,64,2048]{2,1,0:T(8,128)}, f32[2,64,2048]{2,1,0:T(8,128)}, u32[]{:S(2)}, u32[]{:S(2)}) collective-permute-start(f32[2,64,2048]{2,1,0:T(8,128)} %pad_maximum_fusion.9), channel_id=1, source_target_pairs={{0,1},{1,0},{2,3},{3,2},{4,5},{5,4},{6,7},{7,6},{8,9},{9,8},{10,11... | collective-permute-start | bytes 3145736 | tf_op jit(solution)/shard_map/ppermute | solution.py:37
  (187 other events, 1822.9 us)
Sparse Core Ops, SparseCore 0:
  10.0 34.1 all-gather.4
  104.7 49.0 all-gather.6
  208.7 64.6 all-gather.8
  438.5 41.7 reduce-scatter.2
  515.4 93.2 reduce-scatter.4
